TPU v7x, 256 devices: a whole 4x4x8 slice. The times are simulated.
256 devices in a mesh: dp: 2 (over z_hi), ctx: 8 (over z_lo, core), vocab: 16 (over x, y).
Axes of the slice: x: 4, y: 4, z: 8 (z_hi: 2, z_lo: 4; z = z_hi * 4 + z_lo), core: 2. Of those that a mesh axis runs over, the one named last changes fastest.
Arguments:
- hidden: bfloat16 [1024, 4096], P(('dp', 'ctx')), may hold values from -32 to 32
- head_weight: bfloat16 [4096, 76032], P(None, ('ctx', 'vocab')), may hold values from -2 to 2
- targets: int32 [1024], P('dp'), may hold values from 0 to 76031
- segment_ids: int32 [1024], P('dp'), may hold values from 0 to 63, as said below
- lengths: int32 [64], replicated, may hold values from 8 to 24, as said below
- loss_mask: int32 [1024], P('dp'), may hold values 0 or 1
- advantages: float32 [64], replicated, may hold values from -4 to 4
- ref_logprobs: float32 [1024], P('dp'), may hold values from -40 to -2
Outputs:
- grad_hidden: bfloat16 [1024, 4096], P(('dp', 'ctx', 'vocab'))
- grad_head: bfloat16 [4096, 76032], P(None, ('ctx', 'vocab'))
Inputs may be any that keep to these rules, and one draw needn't show every extreme that they name: `segment_ids`: each sequence's tokens are contiguous; the tokens b * 64 to (b + 1) * 64 - 1 carry ids b * 4 to (b + 1) * 4 - 1, never falling, each id used. lengths[s] is the number of tokens whose segment id is s.
All inputs are finite; a program needn't handle non-finite values. No bound on the sum of `loss_mask` on one device may be relied on, other than what follows from the above.
Results may differ from a plain program's by a relative error of at most 0.012.
Values may be sent and summed in bfloat16 or wider, within the bound.
No kernel may reach another device: no remote copies, remote signals or barrier semaphores. Data moves between devices by JAX's collectives and lax.ppermute only.
A program may use at most 128 MiB of HBM per device.

v0:
```python
import jax
import jax.numpy as jnp
from jax import lax
from jax.sharding import PartitionSpec as P

LOSS_SCALE = 1024


kl_weight = 0.1
entropy_weight = 0.05


def per_device(
    hidden, head_weight, targets, segment_ids, lengths, loss_mask, advantages, ref_logprobs
):
    vocab_width = head_weight.shape[1]
    first_column = (
        lax.axis_index("ctx") * lax.axis_size("vocab") + lax.axis_index("vocab")
    ) * vocab_width
    gathered = lax.all_gather(hidden, "ctx", axis=0, tiled=True)
    logits = jnp.dot(gathered, head_weight, preferred_element_type=jnp.float32)
    columns = first_column + lax.iota(jnp.int32, vocab_width)
    target_hits = targets[:, None] == columns[None, :]
    target_part = jnp.sum(jnp.where(target_hits, logits, 0.0), axis=1)
    row_max = lax.pmax(jnp.max(logits, axis=1), ("ctx", "vocab"))
    shifted = jnp.exp(logits - row_max[:, None])
    exp_total, exp_logit, target_logit = lax.psum(
        (jnp.sum(shifted, axis=1), jnp.sum(shifted * logits, axis=1), target_part), ("ctx", "vocab")
    )
    log_total = row_max + jnp.log(exp_total)
    target_logp = target_logit - log_total
    mean_logit = exp_logit / exp_total
    probs = jnp.exp(logits - log_total[:, None])
    seq_onehot = segment_ids[:, None] == lax.iota(jnp.int32, advantages.shape[0])[None, :]
    token_adv = jnp.sum(jnp.where(seq_onehot, advantages[None, :], 0.0), axis=1)
    token_len = jnp.sum(jnp.where(seq_onehot, lengths[None, :].astype(jnp.float32), 0.0), axis=1)
    token_weight = LOSS_SCALE * loss_mask.astype(jnp.float32) / token_len
    logp_grad = -token_adv + kl_weight * (target_logp - ref_logprobs)
    inner = logp_grad[:, None] * (target_hits.astype(jnp.float32) - probs)
    inner = inner + entropy_weight * probs * (logits - mean_logit[:, None])
    grad_logits = (token_weight[:, None] * inner).astype(jnp.bfloat16)
    head_local = lax.dot_general(
        gathered, grad_logits, (((0,), (0,)), ((), ())), preferred_element_type=jnp.float32
    ).astype(jnp.bfloat16)
    grad_head = lax.psum(head_local, "dp").astype(jnp.float32).astype(jnp.bfloat16)
    grad_hidden = lax.psum_scatter(
        lax.dot_general(
            grad_logits, head_weight, (((1,), (1,)), ((), ())), preferred_element_type=jnp.float32
        ),
        ("ctx", "vocab"),
        scatter_dimension=0,
        tiled=True,
    )
    return (grad_hidden.astype(jnp.bfloat16), grad_head)


def solution(mesh):
    return jax.shard_map(
        per_device,
        mesh=mesh,
        in_specs=(
            P(("dp", "ctx"), None),
            P(None, ("ctx", "vocab")),
            P("dp"),
            P("dp"),
            P(),
            P("dp"),
            P(),
            P("dp"),
        ),
        out_specs=(P(("dp", "ctx", "vocab"), None), P(None, ("ctx", "vocab"))),
        check_vma=False,
    )
```

profile of v0, /device:TPU:2, one launch (start us, length us, event | category | flops | bytes accessed | tf_op | source)
XLA Modules:
  0.0 1618.7 jit_solution(10992157121747155881)
XLA Ops:
  7.2 0.0 all-gather.2.cloned.1.call-start
  7.2 0.7 all-gather.2.cloned.1.call-update
  7.9 0.0 all-reduce.5.cloned.1.call-start
  8.0 0.7 convert_element_type.25
  8.6 1.3 dynamic-slice
  10.5 0.8 select_reduce_fusion.1
  11.3 0.7 multiply_divide_fusion
  12.0 0.0 copy-start
  12.0 55.5 %all-gather.2.cloned.1.call-done = bf16[512,4096]{1,0:T(8,128)(2,1)} async-done(((bf16[64,4096]{1,0:T(8,128)(2,1)}), bf16[512,4096]{1,0:T(8,128)(2,1)}) %all-gather.2.cloned.1.call-update) | async-done | bytes 4194320 | tf_op jit(solution)/shard_map/all_gather | solution.py:20
  67.5 6.2 fusion.11
  73.7 0.0 copy-start.1
  73.7 327.9 %pmax.7 = f32[512]{0:T(512)S(1)} all-reduce(f32[512]{0:T(512)S(1)} %get-tuple-element.13), channel_id=1, replica_groups=mesh['dp'=2,'ctx'=8,'vocab'=16] {'ctx','vocab'}, use_global_device_ids=true, to_apply=%region_5.6 | all-reduce | flops 512 | bytes 4096 | tf_op jit(solution)/shard_map/pmax | solution.py:25
  401.6 0.0 copy-done
  401.6 0.4 fusion.7
  402.0 337.2 %all-reduce.1 = (f32[512]{0:T(512)S(1)}, f32[512]{0:T(512)S(1)}, f32[512]{0:T(512)S(1)}) all-reduce(f32[512]{0:T(512)S(1)} %get-tuple-element.3, f32[512]{0:T(512)S(1)} %get-tuple-element.2, f32[512]{0:T(512)S(1)} %get-tuple-element.4), channel_id=1, replica_groups=mesh['dp'=2,'ctx'=8,'vocab'=16] {'ctx','vocab'}, use_global_device_ids=true, to_apply=%region_9.10 | all-reduce | flops 1536 | bytes 12288 | tf_op jit(solution)/shard_map/psum | solution.py:27
  739.2 0.0 copy-done.1
  739.2 0.0 copy-start.2
  739.2 8.7 fusion.9
  747.9 0.0 copy-done.2
  747.9 5.1 fusion
  753.0 0.0 all-reduce.5.cloned.1.call-update
  753.0 852.1 %all-reduce.6 = bf16[512,4096]{1,0:T(8,128)(2,1)} all-reduce(f32[512,4096]{1,0:T(8,128)} %fusion.9), channel_id=2, replica_groups=mesh['dp'=2,'ctx'=8,'vocab'=16] {'ctx','vocab'}, use_global_device_ids=true, to_apply=%region_10.11.clone | all-reduce | flops 2097152 | bytes 12582912
  1605.1 1.5 dynamic-slice_convert_fusion
  1606.6 5.2 copy.13
  (3 shorter events, 0.0 us)
Async XLA Ops:
  7.2 60.3 %all-gather.2.cloned.1.call-start = ((), (), s32[]{:S(2)}) async-start(), calls=%async_computation | async-start | bytes 4718592 | tf_op jit(solution)/shard_map/all_gather | solution.py:20
  7.9 1598.7 %all-reduce.5.cloned.1.call-start = ((), (), s32[]{:S(2)}) async-start(), calls=%async_computation.1 | async-start | bytes 9830400 | tf_op jit(solution)/shard_map/psum | solution.py:45
  12.0 389.6 %copy-start = (s32[512]{0:T(512)S(1)}, s32[512]{0:T(512)}, u32[]{:S(2)}) copy-start(s32[512]{0:T(512)} %param.10) | copy-start | bytes 6148
  73.7 665.5 %copy-start.1 = (f32[512]{0:T(512)S(1)}, f32[512]{0:T(512)}, u32[]{:S(2)}) copy-start(f32[512]{0:T(512)} %param.15) | copy-start | bytes 6148
  739.2 8.7 copy-start.2
Sparse Core Ops, SparseCore 0:
  9.8 57.6 all-gather.1
  753.1 262.5 all-reduce.4
where the time goes:
time: 1630 us; the launch traced here: 1620 us
  blocking collectives  1520 us (93%)
  waiting for transfers between devices  56.2 us (3%)
  matrix products  19.9 us (1%)
    unnamed x1, blocking collectives  852 us
    psum x1, blocking collectives, per_device(): lax.psum((jnp.sum(shifted, axis=1), jnp.sum(shifted * logits, axis=1), ta...  337 us
    pmax x1, blocking collectives, per_device(): row_max = lax.pmax(jnp.max(logits, axis=1), ('ctx', 'vocab'))  328 us
    all_gather x1, waiting for transfers between devices, per_device(): gathered = lax.all_gather(hidden, 'ctx', axis=0, tiled=True)  55.5 us
  transfers between devices with their start and end apart: 2, of which 1 were waited for; matrix products, arithmetic and copies ran while one was open for 0% of the time, Pallas kernels for 0%

commit v1 on v0

v1 whole, which is shorter than its diff:
```python
import jax
import jax.numpy as jnp
from jax import lax
from jax.sharding import Mesh, PartitionSpec as P

LOSS_SCALE = 1024
KL_WEIGHT = 0.1
ENTROPY_WEIGHT = 0.05


def combine(parts):
    top = parts[0][0]
    for part in parts[1:]:
        top = jnp.maximum(top, part[0])
    scales = [jnp.exp(part[0] - top) for part in parts]
    total = sum(part[1] * scale for part, scale in zip(parts, scales))
    logit = sum(part[2] * scale for part, scale in zip(parts, scales))
    target = sum(part[3] for part in parts)
    return jnp.stack([top, total, logit, target])


def exchange(stats, axis):
    size = lax.axis_size(axis)
    others = [
        lax.ppermute(stats, axis, [(i, (i + step) % size) for i in range(size)])
        for step in range(1, size)
    ]
    return combine([stats] + others)


def scatter_sum(parts, axis):
    got = lax.all_to_all(parts, axis, 0, 0, tiled=True)
    return jnp.sum(got.astype(jnp.float32), axis=0)


def per_device(
    hidden, head_weight, targets, segment_ids, lengths, loss_mask, advantages, ref_logprobs
):
    bf16, f32 = jnp.bfloat16, jnp.float32
    width = head_weight.shape[1]
    depth = head_weight.shape[0]
    group = targets.shape[0]
    nz, ncore = lax.axis_size("z"), lax.axis_size("core")
    nv = lax.axis_size("x") * lax.axis_size("y")
    first_column = lax.axis_index(("z", "core", "x", "y")) * width

    seq_onehot = segment_ids[:, None] == lax.iota(jnp.int32, advantages.shape[0])[None, :]
    token_adv = jnp.sum(jnp.where(seq_onehot, advantages[None, :], 0.0), axis=1)
    token_len = jnp.sum(jnp.where(seq_onehot, lengths[None, :].astype(f32), 0.0), axis=1)
    token_weight = LOSS_SCALE * loss_mask.astype(f32) / token_len
    own = jnp.stack([token_adv, token_weight, ref_logprobs, targets.astype(f32)])
    other = lax.ppermute(own, "dp", [(0, 1), (1, 0)])
    first = lax.axis_index("dp") == 0
    both = jnp.concatenate(
        [jnp.where(first, own, other), jnp.where(first, other, own)], axis=1
    )
    adv_all, weight_all, ref_all = both[0], both[1], both[2]
    targets_all = both[3].astype(jnp.int32)

    gathered = lax.all_gather(hidden, ("dp", "z", "core"), axis=0, tiled=True)
    logits = jnp.dot(gathered, head_weight, preferred_element_type=f32)
    columns = first_column + lax.iota(jnp.int32, width)
    hits = targets_all[:, None] == columns[None, :]
    local_max = jnp.max(logits, axis=1)
    shifted = jnp.exp(logits - local_max[:, None])
    stats = jnp.stack(
        [
            local_max,
            jnp.sum(shifted, axis=1),
            jnp.sum(shifted * logits, axis=1),
            jnp.sum(jnp.where(hits, logits, 0.0), axis=1),
        ]
    )
    for axis in ("core", "y", "x", "z"):
        stats = exchange(stats, axis)
    row_max, exp_total, exp_logit, target_logit = stats[0], stats[1], stats[2], stats[3]
    log_total = row_max + jnp.log(exp_total)
    target_logp = target_logit - log_total
    mean_logit = exp_logit / exp_total
    probs = jnp.exp(logits - log_total[:, None])
    logp_grad = -adv_all + KL_WEIGHT * (target_logp - ref_all)
    inner = logp_grad[:, None] * (hits.astype(f32) - probs)
    inner = inner + ENTROPY_WEIGHT * probs * (logits - mean_logit[:, None])
    grad_logits = (weight_all[:, None] * inner).astype(bf16)

    mine = lax.dynamic_slice_in_dim(grad_logits, lax.axis_index("dp") * group, group, 0)
    rows = group // (nz * ncore * nv)
    mine = mine.reshape(nz, ncore, nv, rows, width).transpose(1, 2, 0, 3, 4).reshape(group, width)
    partial = lax.dot_general(
        mine, head_weight, (((1,), (1,)), ((), ())), preferred_element_type=f32
    ).astype(bf16)
    partial = scatter_sum(partial.reshape(ncore, -1, depth), "core").astype(bf16)
    partial = scatter_sum(partial.reshape(nv, -1, depth), ("x", "y")).astype(bf16)
    grad_hidden = scatter_sum(partial.reshape(nz, rows, depth), "z").astype(bf16)

    grad_head = lax.dot_general(
        gathered, grad_logits, (((0,), (0,)), ((), ())), preferred_element_type=f32
    ).astype(bf16)
    return grad_hidden, grad_head


def solution(mesh):
    devices = mesh.devices.reshape(2, 4, 2, 4, 4)
    fine = Mesh(devices, ("dp", "z", "core", "x", "y"))
    ctx, vocab = ("z", "core"), ("x", "y")
    return jax.shard_map(
        per_device,
        mesh=fine,
        in_specs=(
            P(("dp",) + ctx, None),
            P(None, ctx + vocab),
            P("dp"),
            P("dp"),
            P(),
            P("dp"),
            P(),
            P("dp"),
        ),
        out_specs=(P(("dp",) + ctx + vocab, None), P(None, ctx + vocab)),
        check_vma=False,
    )
```

time: 1630 us -> 184 us (0.11)
  blocking collectives: 1520 us -> 40.5 us
  starting transfers between devices: 0.08 us -> 23.9 us
    unnamed x1 -> x0, blocking collectives: 852 us -> none
    psum x1 -> x0, blocking collectives: 337 us -> none  [per_device(): lax.psum((jnp.sum(shifted, axis=1), jnp.sum(shifted * logits, axis=1), ta...]
    pmax x1 -> x0, blocking collectives: 328 us -> none  [per_device(): row_max = lax.pmax(jnp.max(logits, axis=1), ('ctx', 'vocab'))]
    all_to_all x0 -> x2, blocking collectives: none -> 40.5 us  [scatter_sum(): got = lax.all_to_all(parts, axis, 0, 0, tiled=True)]
    ppermute x0 -> x11, starting transfers between devices: none -> 20.6 us  [the longest x10 13.3 us: exchange(): lax.ppermute(stats, axis, [(i, (i + step) % size) for i in range(size)])]
  transfers between devices with their start and end apart: 2 -> 13, of which waited for: 1 -> 10; matrix products, arithmetic and copies ran while one was open for 0% -> 8% of each run, Pallas kernels for 0% -> 0%
where the time goes in v1:
time: 184 us; the launch traced here: 181 us
  waiting for transfers between devices  61.8 us (34%)
  blocking collectives  40.5 us (22%)
  matrix products  25.6 us (14%)
  starting transfers between devices  23.9 us (13%)
  between operations  14.2 us (8%)
  other arithmetic  12.5 us (7%)
  local copies, waits for them, and re-layouts  2.83 us (2%)
    all_gather x1, waiting for transfers between devices, per_device(): gathered = lax.all_gather(hidden, ('dp', 'z', 'core'), axis=0, tiled=True)  47.7 us
    all_to_all x2, blocking collectives, scatter_sum(): got = lax.all_to_all(parts, axis, 0, 0, tiled=True)  40.5 us
    ppermute x10, starting transfers between devices, exchange(): lax.ppermute(stats, axis, [(i, (i + step) % size) for i in range(size)])  13.3 us
    ppermute x10, waiting for transfers between devices, exchange(): lax.ppermute(stats, axis, [(i, (i + step) % size) for i in range(size)])  11.8 us
    dot_general x1, matrix products, per_device(): lax.dot_general(gathered, grad_logits, (((0,), (0,)), ((), ())), preferre...  10.3 us
    dot_general x1, matrix products, per_device(): logits = jnp.dot(gathered, head_weight, preferred_element_type=f32)  9.19 us
    ppermute x1, starting transfers between devices, per_device(): other = lax.ppermute(own, 'dp', [(0, 1), (1, 0)])  7.28 us
    dot_general x1, matrix products, per_device(): lax.dot_general(mine, head_weight, (((1,), (1,)), ((), ())), preferred_el...  6.07 us
  transfers between devices with their start and end apart: 13, of which 10 were waited for; matrix products, arithmetic and copies ran while one was open for 8% of the time, Pallas kernels for 0%

profile of v1, /device:TPU:2, one launch (start us, length us, event | category | flops | bytes accessed | tf_op | source)
XLA Modules:
  0.0 181.3 jit_solution(15356965969303987617)
XLA Ops:
  11.4 7.3 %collective-permute-start = (f32[4,512]{1,0:T(4,128)S(1)}, f32[4,512]{1,0:T(4,128)S(1)}, u32[]{:S(2)}, u32[]{:S(2)}) collective-permute-start(f32[4,512]{1,0:T(4,128)S(1)} %pad_maximum_fusion.4), channel_id=1, source_target_pairs={{0,128},{128,0},{1,129},{129,1},{2,130},{130,2},{3,131},{131,3},{4... | collective-permute-start | bytes 24584 | tf_op jit(solution)/shard_map/ppermute | solution.py:52
  18.7 1.6 collective-permute-done
  21.1 47.7 %all-gather.2.cloned.1.call-done = bf16[1024,4096]{1,0:T(8,128)(2,1)} async-done(((bf16[64,4096]{1,0:T(8,128)(2,1)}), bf16[1024,4096]{1,0:T(8,128)(2,1)}) %all-gather.2.cloned.1.call-update) | async-done | bytes 8388624 | tf_op jit(solution)/shard_map/all_gather | solution.py:60
  68.7 9.2 %fusion.17 = (f32[1024]{0:T(1024)S(1)}, f32[1024,594]{0,1:T(8,128)S(1)}) fusion(bf16[1024,4096]{1,0:T(8,128)(2,1)} %all-gather.2.cloned.1.call-done, bf16[4096,594]{0,1:T(8,128)(2,1)} %param.9), kind=kOutput, calls=%fused_computation.86 | convolution fusion | flops 4983440384 | bytes 15691776 | tf_op jit(solution)/shard_map/dot_general | solution.py:61
  79.0 0.9 collective-permute-done.1
  80.1 2.8 %collective-permute-start.4 = (f32[4,1024]{1,0:T(4,128)S(1)}, f32[4,1024]{1,0:T(4,128)S(1)}, u32[]{:S(2)}, u32[]{:S(2)}) collective-permute-start(f32[4,1024]{1,0:T(4,128)S(1)} %pad_maximum_fusion.1), channel_id=1, source_target_pairs={{0,3},{1,0},{2,1},{3,2},{4,7},{5,4},{6,5},{7,6},{8,11},{9,8},{10,9... | collective-permute-start | bytes 49160 | tf_op jit(solution)/shard_map/ppermute | solution.py:25
  83.7 0.9 collective-permute-start.2
  84.6 3.6 %collective-permute-done.3 = f32[4,1024]{1,0:T(4,128)S(1)} collective-permute-done((f32[4,1024]{1,0:T(4,128)S(1)}, f32[4,1024]{1,0:T(4,128)S(1)}, u32[]{:S(2)}, u32[]{:S(2)}) %collective-permute-start.3) | collective-permute-done | bytes 16416 | tf_op jit(solution)/shard_map/ppermute | solution.py:25
  89.4 2.4 %collective-permute-start.6 = (f32[4,1024]{1,0:T(4,128)S(1)}, f32[4,1024]{1,0:T(4,128)S(1)}, u32[]{:S(2)}, u32[]{:S(2)}) collective-permute-start(f32[4,1024]{1,0:T(4,128)S(1)} %pad_maximum_fusion.2), channel_id=1, source_target_pairs={{0,8},{4,12},{8,0},{12,4},{1,9},{5,13},{9,1},{13,5},{2,10},{6,14},... | collective-permute-start | bytes 49160 | tf_op jit(solution)/shard_map/ppermute | solution.py:25
  91.8 1.8 collective-permute-start.5
  93.6 1.1 collective-permute-done.6
  94.7 0.9 collective-permute-done.5
  95.7 3.0 %collective-permute-start.10 = (f32[4,1024]{1,0:T(4,128)S(1)}, f32[4,1024]{1,0:T(4,128)S(1)}, u32[]{:S(2)}, u32[]{:S(2)}) collective-permute-start(f32[4,1024]{1,0:T(4,128)S(1)} %pad_maximum_fusion.3), channel_id=1, source_target_pairs={{0,96},{32,0},{64,32},{96,64},{1,97},{33,1},{65,33},{97,65},{2,98}... | collective-permute-start | bytes 49160 | tf_op jit(solution)/shard_map/ppermute | solution.py:25
  100.1 3.2 %collective-permute-done.9 = f32[4,1024]{1,0:T(4,128)S(1)} collective-permute-done((f32[4,1024]{1,0:T(4,128)S(1)}, f32[4,1024]{1,0:T(4,128)S(1)}, u32[]{:S(2)}, u32[]{:S(2)}) %collective-permute-start.9) | collective-permute-done | bytes 16416 | tf_op jit(solution)/shard_map/ppermute | solution.py:25
  103.3 0.9 collective-permute-done.8
  104.3 1.0 fusion.6
  105.4 1.0 copy-done
  107.5 6.1 %convolution_convert_fusion.1 = bf16[512,4096]{1,0:T(8,128)(2,1)S(1)} fusion(bf16[512,594]{1,0:T(8,128)(2,1)S(1)} %reshape.533, bf16[4096,594]{0,1:T(8,128)(2,1)} %param.9), kind=kOutput, calls=%fused_computation.1 | convolution fusion | flops 2493513728 | bytes 9668608 | tf_op jit(solution)/shard_map/dot_general | solution.py:89
  113.6 8.2 %all_to_all.15 = bf16[2,256,4096]{2,1,0:T(8,128)(2,1)} all-to-all(bf16[2,256,4096]{2,1,0:T(8,128)(2,1)S(1)} %bitcast.64), channel_id=1, replica_groups=mesh['dp'=2,'z'=4,'core'=2,'x'=4,'y'=4] {'core'}, dimensions={0} | all-to-all | bytes 8388608 | tf_op jit(solution)/shard_map/all_to_all | solution.py:32
  121.8 3.3 %reduce_sum.86 = bf16[256,4096]{1,0:T(8,128)(2,1)S(1)} reduce(bf16[2,256,4096]{2,1,0:T(8,128)(2,1)} %all_to_all.15, bf16[]{:T(256)} %constant.48.clone.1), dimensions={0}, to_apply=%region_6.7 | reduce | flops 1048576 | bytes 6291458 | tf_op jit(solution)/shard_map/reduce_sum | solution.py:33
  125.1 32.3 %all_to_all.16 = bf16[16,16,4096]{2,1,0:T(8,128)(2,1)} all-to-all(bf16[16,16,4096]{2,1,0:T(8,128)(2,1)S(1)} %bitcast.63), channel_id=1, replica_groups=mesh['dp'=2,'z'=4,'core'=2,'x'=4,'y'=4] {'x','y'}, dimensions={0} | all-to-all | bytes 4194304 | tf_op jit(solution)/shard_map/all_to_all | solution.py:32
  157.4 2.0 %reduce_sum.87 = bf16[16,4096]{1,0:T(8,128)(2,1)S(1)} reduce(bf16[16,16,4096]{2,1,0:T(8,128)(2,1)} %all_to_all.16, bf16[]{:T(256)} %constant.48.clone.1), dimensions={0}, to_apply=%region_7.8 | reduce | flops 983040 | bytes 2228226 | tf_op jit(solution)/shard_map/reduce_sum | solution.py:33
  160.1 3.3 %all-to-all-start.2 = ((bf16[4,4,4096]{2,1,0:T(4,128)(2,1)}), bf16[4,4,4096]{2,1,0:T(4,128)(2,1)S(1)}, u32[]{:S(2)}, u32[]{:S(2)}) async-start(bf16[4,4,4096]{2,1,0:T(4,128)(2,1)} %reshape.536), calls=%async_computation.2 | async-start | bytes 262144 | tf_op jit(solution)/shard_map/all_to_all | solution.py:32
  163.5 10.3 %fusion = bf16[4096,594]{0,1:T(8,128)(2,1)} fusion(bf16[1024,594]{0,1:T(8,128)(2,1)S(1)} %copy-done.1, bf16[1024,4096]{1,0:T(8,128)(2,1)} %all-gather.2.cloned.1.call-done), kind=kOutput, calls=%fused_computation.2 | convolution fusion | flops 4985266176 | bytes 14471168 | tf_op jit(solution)/shard_map/dot_general | solution.py:96
  (46 shorter events, 12.4 us)
Async XLA Ops:
  7.2 61.6 %all-gather.2.cloned.1.call-start = ((), (), s32[]{:S(2)}) async-start(), calls=%async_computation.3 | async-start | bytes 8912896 | tf_op jit(solution)/shard_map/all_gather | solution.py:60
  11.4 8.9 %collective-permute-start = (f32[4,512]{1,0:T(4,128)S(1)}, f32[4,512]{1,0:T(4,128)S(1)}, u32[]{:S(2)}, u32[]{:S(2)}) collective-permute-start(f32[4,512]{1,0:T(4,128)S(1)} %pad_maximum_fusion.4), channel_id=1, source_target_pairs={{0,128},{128,0},{1,129},{129,1},{2,130},{130,2},{3,131},{131,3},{4... | collective-permute-start | bytes 24584 | tf_op jit(solution)/shard_map/ppermute | solution.py:52
  78.7 1.3 collective-permute-start.1
  80.1 4.5 %collective-permute-start.4 = (f32[4,1024]{1,0:T(4,128)S(1)}, f32[4,1024]{1,0:T(4,128)S(1)}, u32[]{:S(2)}, u32[]{:S(2)}) collective-permute-start(f32[4,1024]{1,0:T(4,128)S(1)} %pad_maximum_fusion.1), channel_id=1, source_target_pairs={{0,3},{1,0},{2,1},{3,2},{4,7},{5,4},{6,5},{7,6},{8,11},{9,8},{10,9... | collective-permute-start | bytes 49160 | tf_op jit(solution)/shard_map/ppermute | solution.py:25
  82.9 5.2 %collective-permute-start.3 = (f32[4,1024]{1,0:T(4,128)S(1)}, f32[4,1024]{1,0:T(4,128)S(1)}, u32[]{:S(2)}, u32[]{:S(2)}) collective-permute-start(f32[4,1024]{1,0:T(4,128)S(1)} %pad_maximum_fusion.1), channel_id=1, source_target_pairs={{0,2},{1,3},{2,0},{3,1},{4,6},{5,7},{6,4},{7,5},{8,10},{9,11},{10,... | collective-permute-start | bytes 49160 | tf_op jit(solution)/shard_map/ppermute | solution.py:25
  83.7 4.9 %collective-permute-start.2 = (f32[4,1024]{1,0:T(4,128)S(1)}, f32[4,1024]{1,0:T(4,128)S(1)}, u32[]{:S(2)}, u32[]{:S(2)}) collective-permute-start(f32[4,1024]{1,0:T(4,128)S(1)} %pad_maximum_fusion.1), channel_id=1, source_target_pairs={{0,1},{1,2},{2,3},{3,0},{4,5},{5,6},{6,7},{7,4},{8,9},{9,10},{10,1... | collective-permute-start | bytes 49160 | tf_op jit(solution)/shard_map/ppermute | solution.py:25
  88.8 4.8 %collective-permute-start.7 = (f32[4,1024]{1,0:T(4,128)S(1)}, f32[4,1024]{1,0:T(4,128)S(1)}, u32[]{:S(2)}, u32[]{:S(2)}) collective-permute-start(f32[4,1024]{1,0:T(4,128)S(1)} %pad_maximum_fusion.2), channel_id=1, source_target_pairs={{0,12},{4,0},{8,4},{12,8},{1,13},{5,1},{9,5},{13,9},{2,14},{6,2},{... | collective-permute-start | bytes 49160 | tf_op jit(solution)/shard_map/ppermute | solution.py:25
  89.4 5.2 %collective-permute-start.6 = (f32[4,1024]{1,0:T(4,128)S(1)}, f32[4,1024]{1,0:T(4,128)S(1)}, u32[]{:S(2)}, u32[]{:S(2)}) collective-permute-start(f32[4,1024]{1,0:T(4,128)S(1)} %pad_maximum_fusion.2), channel_id=1, source_target_pairs={{0,8},{4,12},{8,0},{12,4},{1,9},{5,13},{9,1},{13,5},{2,10},{6,14},... | collective-permute-start | bytes 49160 | tf_op jit(solution)/shard_map/ppermute | solution.py:25
  91.8 3.7 %collective-permute-start.5 = (f32[4,1024]{1,0:T(4,128)S(1)}, f32[4,1024]{1,0:T(4,128)S(1)}, u32[]{:S(2)}, u32[]{:S(2)}) collective-permute-start(f32[4,1024]{1,0:T(4,128)S(1)} %pad_maximum_fusion.2), channel_id=1, source_target_pairs={{0,4},{4,8},{8,12},{12,0},{1,5},{5,9},{9,13},{13,1},{2,6},{6,10},{... | collective-permute-start | bytes 49160 | tf_op jit(solution)/shard_map/ppermute | solution.py:25
  95.7 4.4 %collective-permute-start.10 = (f32[4,1024]{1,0:T(4,128)S(1)}, f32[4,1024]{1,0:T(4,128)S(1)}, u32[]{:S(2)}, u32[]{:S(2)}) collective-permute-start(f32[4,1024]{1,0:T(4,128)S(1)} %pad_maximum_fusion.3), channel_id=1, source_target_pairs={{0,96},{32,0},{64,32},{96,64},{1,97},{33,1},{65,33},{97,65},{2,98}... | collective-permute-start | bytes 49160 | tf_op jit(solution)/shard_map/ppermute | solution.py:25
  98.7 4.6 %collective-permute-start.9 = (f32[4,1024]{1,0:T(4,128)S(1)}, f32[4,1024]{1,0:T(4,128)S(1)}, u32[]{:S(2)}, u32[]{:S(2)}) collective-permute-start(f32[4,1024]{1,0:T(4,128)S(1)} %pad_maximum_fusion.3), channel_id=1, source_target_pairs={{0,64},{32,96},{64,0},{96,32},{1,65},{33,97},{65,1},{97,33},{2,66}... | collective-permute-start | bytes 49160 | tf_op jit(solution)/shard_map/ppermute | solution.py:25
  98.7 5.5 %collective-permute-start.8 = (f32[4,1024]{1,0:T(4,128)S(1)}, f32[4,1024]{1,0:T(4,128)S(1)}, u32[]{:S(2)}, u32[]{:S(2)}) collective-permute-start(f32[4,1024]{1,0:T(4,128)S(1)} %pad_maximum_fusion.3), channel_id=1, source_target_pairs={{0,32},{32,64},{64,96},{96,0},{1,33},{33,65},{65,97},{97,1},{2,34}... | collective-permute-start | bytes 49160 | tf_op jit(solution)/shard_map/ppermute | solution.py:25
  105.4 1.0 copy-start
  157.4 6.0 %copy-start.1 = (bf16[1024,594]{0,1:T(8,128)(2,1)S(1)}, bf16[1024,594]{0,1:T(8,128)(2,1)}, u32[]{:S(2)}) copy-start(bf16[1024,594]{0,1:T(8,128)(2,1)} %copy-done) | copy-start | bytes 3649540
  160.1 13.7 %all-to-all-start.2 = ((bf16[4,4,4096]{2,1,0:T(4,128)(2,1)}), bf16[4,4,4096]{2,1,0:T(4,128)(2,1)S(1)}, u32[]{:S(2)}, u32[]{:S(2)}) async-start(bf16[4,4,4096]{2,1,0:T(4,128)(2,1)} %reshape.536), calls=%async_computation.2 | async-start | bytes 262144 | tf_op jit(solution)/shard_map/all_to_all | solution.py:32
Sparse Core Ops, SparseCore 0:
  9.8 58.8 all-gather.1

commit v2 on v1

v2 whole, which is shorter than its diff:
```python
import jax
import jax.numpy as jnp
from jax import lax
from jax.sharding import Mesh, PartitionSpec as P

LOSS_SCALE = 1024
KL_WEIGHT = 0.1
ENTROPY_WEIGHT = 0.05


def combine(parts):
    top = parts[0][0]
    for part in parts[1:]:
        top = jnp.maximum(top, part[0])
    scales = [jnp.exp(part[0] - top) for part in parts]
    total = sum(part[1] * scale for part, scale in zip(parts, scales))
    logit = sum(part[2] * scale for part, scale in zip(parts, scales))
    target = sum(part[3] for part in parts)
    return jnp.stack([top, total, logit, target])


def exchange(stats, axis):
    size = lax.axis_size(axis)
    others = [
        lax.ppermute(stats, axis, [(i, (i + step) % size) for i in range(size)])
        for step in range(1, size)
    ]
    return combine([stats] + others)


def scatter_sum(parts, axis):
    got = lax.all_to_all(parts, axis, 0, 0, tiled=True)
    return jnp.sum(got.astype(jnp.float32), axis=0)


def swap(value, axis):
    return lax.ppermute(value, axis, [(0, 1), (1, 0)])


def per_device(
    hidden, head_weight, targets, segment_ids, lengths, loss_mask, advantages, ref_logprobs
):
    bf16, f32 = jnp.bfloat16, jnp.float32
    depth, width = head_weight.shape
    nz, ncore = lax.axis_size("z"), lax.axis_size("core")
    nv = lax.axis_size("x") * lax.axis_size("y")
    block = hidden.shape[0]
    z, core, place = lax.axis_index("z"), lax.axis_index("core"), lax.axis_index(("x", "y"))

    weights = [head_weight, swap(head_weight, "core")]
    gathered = lax.all_gather(hidden, ("dp", "z"), axis=0, tiled=True)
    first_columns = [((z * ncore + c) * nv + place) * width for c in (core, 1 - core)]

    seq_onehot = segment_ids[:, None] == lax.iota(jnp.int32, advantages.shape[0])[None, :]
    token_adv = jnp.sum(jnp.where(seq_onehot, advantages[None, :], 0.0), axis=1)
    token_len = jnp.sum(jnp.where(seq_onehot, lengths[None, :].astype(f32), 0.0), axis=1)
    token_weight = LOSS_SCALE * loss_mask.astype(f32) / token_len
    own = jnp.stack([token_adv, token_weight, ref_logprobs, targets.astype(f32)])
    own = own.reshape(4, nz, ncore, block)
    own = jnp.where(core == 0, own[:, :, 0], own[:, :, 1]).reshape(4, nz * block)
    other = swap(own, "dp")
    first = lax.axis_index("dp") == 0
    both = jnp.concatenate(
        [jnp.where(first, own, other), jnp.where(first, other, own)], axis=1
    )
    adv_all, weight_all, ref_all = both[0], both[1], both[2]
    targets_all = both[3].astype(jnp.int32)

    logits = [jnp.dot(gathered, w, preferred_element_type=f32) for w in weights]
    hits = [
        targets_all[:, None] == (c + lax.iota(jnp.int32, width))[None, :] for c in first_columns
    ]
    local_max = jnp.maximum(*[jnp.max(part, axis=1) for part in logits])
    shifted = [jnp.exp(part - local_max[:, None]) for part in logits]
    stats = jnp.stack(
        [
            local_max,
            sum(jnp.sum(s, axis=1) for s in shifted),
            sum(jnp.sum(s * part, axis=1) for s, part in zip(shifted, logits)),
            sum(jnp.sum(jnp.where(h, part, 0.0), axis=1) for h, part in zip(hits, logits)),
        ]
    )
    for axis in ("y", "x", "z"):
        stats = exchange(stats, axis)
    row_max, exp_total, exp_logit, target_logit = stats[0], stats[1], stats[2], stats[3]
    log_total = row_max + jnp.log(exp_total)
    target_logp = target_logit - log_total
    mean_logit = exp_logit / exp_total
    logp_grad = -adv_all + KL_WEIGHT * (target_logp - ref_all)
    grads = []
    for part, hit in zip(logits, hits):
        probs = jnp.exp(part - log_total[:, None])
        inner = logp_grad[:, None] * (hit.astype(f32) - probs)
        inner = inner + ENTROPY_WEIGHT * probs * (part - mean_logit[:, None])
        grads.append((weight_all[:, None] * inner).astype(bf16))

    rows = block // nv
    partial = 0.0
    for grad, w in zip(grads, weights):
        mine = lax.dynamic_slice_in_dim(grad, lax.axis_index("dp") * nz * block, nz * block, 0)
        mine = mine.reshape(nz, nv, rows, width).transpose(1, 0, 2, 3).reshape(nz * block, width)
        partial = partial + lax.dot_general(
            mine, w, (((1,), (1,)), ((), ())), preferred_element_type=f32
        )
    partial = partial.astype(bf16)
    partial = scatter_sum(partial.reshape(nv, -1, depth), ("x", "y")).astype(bf16)
    grad_hidden = scatter_sum(partial.reshape(nz, rows, depth), "z").astype(bf16)

    other_hidden = swap(gathered, "core")
    other_grads = swap(grads[1], "core")
    grad_head = 0.0
    for h, g in ((gathered, grads[0]), (other_hidden, other_grads)):
        grad_head = grad_head + lax.dot_general(
            h, g, (((0,), (0,)), ((), ())), preferred_element_type=f32
        )
    return grad_hidden, grad_head.astype(bf16)


def solution(mesh):
    devices = mesh.devices.reshape(2, 4, 2, 4, 4)
    fine = Mesh(devices, ("dp", "z", "core", "x", "y"))
    ctx, vocab = ("z", "core"), ("x", "y")
    return jax.shard_map(
        per_device,
        mesh=fine,
        in_specs=(
            P(("dp",) + ctx, None),
            P(None, ctx + vocab),
            P("dp"),
            P("dp"),
            P(),
            P("dp"),
            P(),
            P("dp"),
        ),
        out_specs=(P(("dp",) + ctx + vocab, None), P(None, ctx + vocab)),
        check_vma=False,
    )
```

time: 184 us -> 182 us (0.989)
  blocking collectives: 40.5 us -> 0 us
  waiting for transfers between devices: 61.8 us -> 86.3 us
  matrix products: 25.6 us -> 38.5 us
  starting transfers between devices: 23.9 us -> 29.8 us
  other arithmetic: 12.5 us -> 6.6 us
    all_to_all x2 -> x0, blocking collectives: 40.5 us -> none  [scatter_sum(): got = lax.all_to_all(parts, axis, 0, 0, tiled=True)]
    all_to_all x1 -> x2, waiting for transfers between devices: 0.01 us -> 26.7 us  [scatter_sum(): got = lax.all_to_all(parts, axis, 0, 0, tiled=True)]
    dot_general x3 -> x6, matrix products: 25.6 us -> 38.5 us  [the longest x2 17.7 us: per_device(): lax.dot_general(h, g, (((0,), (0,)), ((), ())), preferred_element_type=f32)]
    all_to_all x1 -> x2, starting transfers between devices: 3.32 us -> 9.41 us  [scatter_sum(): got = lax.all_to_all(parts, axis, 0, 0, tiled=True)]
    reduce_sum x3 -> x2, other arithmetic: 5.98 us -> 0.97 us  [scatter_sum(): return jnp.sum(got.astype(jnp.float32), axis=0)]
    ppermute x10 -> x9, waiting for transfers between devices: 11.8 us -> 10.5 us  [exchange(): lax.ppermute(stats, axis, [(i, (i + step) % size) for i in range(size)])]
    ppermute x10 -> x9, starting transfers between devices: 13.3 us -> 13.1 us  [exchange(): lax.ppermute(stats, axis, [(i, (i + step) % size) for i in range(size)])]
    ppermute x1 -> x4, starting transfers between devices: 7.28 us -> 7.31 us  [swap(): return lax.ppermute(value, axis, [(0, 1), (1, 0)])]
  transfers between devices with their start and end apart: 13 -> 16, of which waited for: 10 -> 10; matrix products, arithmetic and copies ran while one was open for 8% -> 18% of each run, Pallas kernels for 0% -> 0%
where the time goes in v2:
time: 182 us; the launch traced here: 179 us
  waiting for transfers between devices  86.3 us (47%)
  matrix products  38.5 us (21%)
  starting transfers between devices  29.8 us (16%)
  between operations  14.3 us (8%)
  other arithmetic  6.6 us (4%)
  local copies, waits for them, and re-layouts  3.51 us (2%)
    all_gather x1, waiting for transfers between devices, per_device(): gathered = lax.all_gather(hidden, ('dp', 'z'), axis=0, tiled=True)  46.8 us
    all_to_all x2, waiting for transfers between devices, scatter_sum(): got = lax.all_to_all(parts, axis, 0, 0, tiled=True)  26.7 us
    dot_general x2, matrix products, per_device(): lax.dot_general(h, g, (((0,), (0,)), ((), ())), preferred_element_type=f32)  17.7 us
    ppermute x9, starting transfers between devices, exchange(): lax.ppermute(stats, axis, [(i, (i + step) % size) for i in range(size)])  13.1 us
    dot_general x2, matrix products, per_device(): logits = [jnp.dot(gathered, w, preferred_element_type=f32) for w in weights]  11.1 us
    ppermute x9, waiting for transfers between devices, exchange(): lax.ppermute(stats, axis, [(i, (i + step) % size) for i in range(size)])  10.5 us
    dot_general x2, matrix products, per_device(): lax.dot_general(mine, w, (((1,), (1,)), ((), ())), preferred_element_type...  9.74 us
    all_to_all x2, starting transfers between devices, scatter_sum(): got = lax.all_to_all(parts, axis, 0, 0, tiled=True)  9.41 us
  transfers between devices with their start and end apart: 16, of which 10 were waited for; matrix products, arithmetic and copies ran while one was open for 18% of the time, Pallas kernels for 0%

profile of v2, /device:TPU:2, one launch (start us, length us, event | category | flops | bytes accessed | tf_op | source)
XLA Modules:
  0.0 179.0 jit_solution(16602402807630503153)
XLA Ops:
  12.0 7.2 %collective-permute-start = (f32[4,256]{1,0:T(4,128)S(1)}, f32[4,256]{1,0:T(4,128)S(1)}, u32[]{:S(2)}, u32[]{:S(2)}) collective-permute-start(f32[4,256]{1,0:T(4,128)S(1)} %select_n.47), channel_id=1, source_target_pairs={{0,128},{128,0},{1,129},{129,1},{2,130},{130,2},{3,131},{131,3},{4... | collective-permute-start | bytes 12296 | tf_op jit(solution)/shard_map/ppermute | solution.py:37
  19.2 1.6 collective-permute-done
  20.8 46.8 %all-gather.2.cloned.1.call-done = bf16[512,4096]{1,0:T(8,128)(2,1)} async-done(((bf16[64,4096]{1,0:T(8,128)(2,1)}), bf16[512,4096]{1,0:T(8,128)(2,1)}) %all-gather.2.cloned.1.call-update) | async-done | bytes 4194320 | tf_op jit(solution)/shard_map/all_gather | solution.py:51
  67.6 6.3 %fusion.25 = (f32[512]{0:T(512)S(1)}, f32[512,594]{0,1:T(8,128)S(1)}) fusion(bf16[512,4096]{1,0:T(8,128)(2,1)} %all-gather.2.cloned.1.call-done, bf16[4096,594]{0,1:T(8,128)(2,1)} %param.9), kind=kOutput, calls=%fused_computation.95 | convolution fusion | flops 2491720192 | bytes 10278912 | tf_op jit(solution)/shard_map/dot_general | solution.py:69
  73.9 4.8 %fusion.26 = (f32[512]{0:T(512)S(1)}, f32[512,594]{0,1:T(8,128)S(1)}) fusion(bf16[512,4096]{1,0:T(8,128)(2,1)S(1)} %copy-done, bf16[4096,594]{0,1:T(8,128)(2,1)} %collective-permute-done.1), kind=kOutput, calls=%fused_computation.96 | convolution fusion | flops 2491720192 | bytes 10278912 | tf_op jit(solution)/shard_map/dot_general | solution.py:69
  79.6 2.8 %collective-permute-start.4 = (f32[4,512]{1,0:T(4,128)S(1)}, f32[4,512]{1,0:T(4,128)S(1)}, u32[]{:S(2)}, u32[]{:S(2)}) collective-permute-start(f32[4,512]{1,0:T(4,128)S(1)} %pad_maximum_fusion), channel_id=1, source_target_pairs={{0,3},{1,0},{2,1},{3,2},{4,7},{5,4},{6,5},{7,6},{8,11},{9,8},{10,9... | collective-permute-start | bytes 24584 | tf_op jit(solution)/shard_map/ppermute | solution.py:25
  82.4 0.8 collective-permute-start.3
  83.2 0.9 collective-permute-start.2
  84.1 3.5 %collective-permute-done.3 = f32[4,512]{1,0:T(4,128)S(1)} collective-permute-done((f32[4,512]{1,0:T(4,128)S(1)}, f32[4,512]{1,0:T(4,128)S(1)}, u32[]{:S(2)}, u32[]{:S(2)}) %collective-permute-start.3) | collective-permute-done | bytes 8224 | tf_op jit(solution)/shard_map/ppermute | solution.py:25
  88.8 2.4 %collective-permute-start.6 = (f32[4,512]{1,0:T(4,128)S(1)}, f32[4,512]{1,0:T(4,128)S(1)}, u32[]{:S(2)}, u32[]{:S(2)}) collective-permute-start(f32[4,512]{1,0:T(4,128)S(1)} %pad_maximum_fusion.1), channel_id=1, source_target_pairs={{0,8},{4,12},{8,0},{12,4},{1,9},{5,13},{9,1},{13,5},{2,10},{6,14},... | collective-permute-start | bytes 24584 | tf_op jit(solution)/shard_map/ppermute | solution.py:25
  91.2 1.8 collective-permute-start.5
  93.0 1.0 collective-permute-done.6
  93.9 0.9 collective-permute-done.5
  94.9 3.0 %collective-permute-start.10 = (f32[4,512]{1,0:T(4,128)S(1)}, f32[4,512]{1,0:T(4,128)S(1)}, u32[]{:S(2)}, u32[]{:S(2)}) collective-permute-start(f32[4,512]{1,0:T(4,128)S(1)} %pad_maximum_fusion.2), channel_id=1, source_target_pairs={{0,96},{32,0},{64,32},{96,64},{1,97},{33,1},{65,33},{97,65},{2,98}... | collective-permute-start | bytes 24584 | tf_op jit(solution)/shard_map/ppermute | solution.py:25
  99.3 3.2 %collective-permute-done.9 = f32[4,512]{1,0:T(4,128)S(1)} collective-permute-done((f32[4,512]{1,0:T(4,128)S(1)}, f32[4,512]{1,0:T(4,128)S(1)}, u32[]{:S(2)}, u32[]{:S(2)}) %collective-permute-start.9) | collective-permute-done | bytes 8224 | tf_op jit(solution)/shard_map/ppermute | solution.py:25
  102.5 0.9 collective-permute-done.8
  103.5 1.7 fusion.13
  106.9 4.2 %fusion.27 = f32[256,4096]{1,0:T(8,128)S(1)} fusion(bf16[256,594]{1,0:T(8,128)(2,1)S(1)} %reshape.584, bf16[4096,594]{0,1:T(8,128)(2,1)} %param.9), kind=kOutput, calls=%fused_computation.97 | convolution fusion | flops 1245708288 | bytes 9364480 | tf_op jit(solution)/shard_map/dot_general | solution.py:102
  111.1 5.5 %fusion.1 = bf16[256,4096]{1,0:T(8,128)(2,1)} fusion(f32[256,4096]{1,0:T(8,128)S(1)} %fusion.27, bf16[256,594]{1,0:T(8,128)(2,1)S(1)} %reshape.586, bf16[4096,594]{0,1:T(8,128)(2,1)} %collective-permute-done.1), kind=kOutput, calls=%fused_computation.3 | convolution fusion | flops 1247805440 | bytes 11461632 | tf_op jit(solution)/shard_map/dot_general | solution.py:102
  116.7 6.1 %all-to-all-start = ((bf16[16,16,4096]{2,1,0:T(8,128)(2,1)}), bf16[16,16,4096]{2,1,0:T(8,128)(2,1)S(1)}, u32[]{:S(2)}, u32[]{:S(2)}) async-start(bf16[16,16,4096]{2,1,0:T(8,128)(2,1)} %bitcast.46), calls=%async_computation | async-start | bytes 4194304 | tf_op jit(solution)/shard_map/all_to_all | solution.py:32
  122.8 26.7 %all-to-all-done = bf16[16,16,4096]{2,1,0:T(8,128)(2,1)S(1)} async-done(((bf16[16,16,4096]{2,1,0:T(8,128)(2,1)}), bf16[16,16,4096]{2,1,0:T(8,128)(2,1)S(1)}, u32[]{:S(2)}, u32[]{:S(2)}) %all-to-all-start) | async-done | bytes 2097184 | tf_op jit(solution)/shard_map/all_to_all | solution.py:32
  150.5 3.3 %all-to-all-start.1 = ((bf16[4,4,4096]{2,1,0:T(4,128)(2,1)}), bf16[4,4,4096]{2,1,0:T(4,128)(2,1)S(1)}, u32[]{:S(2)}, u32[]{:S(2)}) async-start(bf16[4,4,4096]{2,1,0:T(4,128)(2,1)} %reshape.588), calls=%async_computation.1 | async-start | bytes 262144 | tf_op jit(solution)/shard_map/all_to_all | solution.py:32
  153.8 7.5 %fusion.28 = f32[594,4096]{1,0:T(8,128)} fusion(bf16[512,594]{0,1:T(8,128)(2,1)S(1)} %get-tuple-element.24, bf16[512,4096]{1,0:T(8,128)(2,1)} %all-gather.2.cloned.1.call-done), kind=kOutput, calls=%fused_computation.98 | convolution fusion | flops 2491416576 | bytes 14534656 | tf_op jit(solution)/shard_map/dot_general | solution.py:113
  162.0 10.2 %fusion = bf16[4096,594]{0,1:T(8,128)(2,1)} fusion(f32[594,4096]{1,0:T(8,128)} %fusion.28, bf16[512,594]{0,1:T(8,128)(2,1)} %collective-permute-done.11, bf16[512,4096]{1,0:T(8,128)(2,1)} %collective-permute-done.12), kind=kOutput, calls=%fused_computation.1 | convolution fusion | flops 2496282624 | bytes 19400704 | tf_op jit(solution)/shard_map/dot_general | solution.py:113
  (67 shorter events, 11.8 us)
Async XLA Ops:
  7.2 60.4 %all-gather.2.cloned.1.call-start = ((), (), s32[]{:S(2)}) async-start(), calls=%async_computation.2 | async-start | bytes 4718592 | tf_op jit(solution)/shard_map/all_gather | solution.py:51
  7.9 66.0 %collective-permute-start.1 = (bf16[4096,594]{0,1:T(8,128)(2,1)}, bf16[4096,594]{0,1:T(8,128)(2,1)}, u32[]{:S(2)}, u32[]{:S(2)}) collective-permute-start(bf16[4096,594]{0,1:T(8,128)(2,1)} %param.9), channel_id=1, source_target_pairs={{0,16},{16,0},{1,17},{17,1},{2,18},{18,2},{3,19},{19,3},{4,20},{20... | collective-permute-start | bytes 14598152 | tf_op jit(solution)/shard_map/ppermute | solution.py:37
  12.0 8.8 %collective-permute-start = (f32[4,256]{1,0:T(4,128)S(1)}, f32[4,256]{1,0:T(4,128)S(1)}, u32[]{:S(2)}, u32[]{:S(2)}) collective-permute-start(f32[4,256]{1,0:T(4,128)S(1)} %select_n.47), channel_id=1, source_target_pairs={{0,128},{128,0},{1,129},{129,1},{2,130},{130,2},{3,131},{131,3},{4... | collective-permute-start | bytes 12296 | tf_op jit(solution)/shard_map/ppermute | solution.py:37
  67.6 6.3 %copy-start = (bf16[512,4096]{1,0:T(8,128)(2,1)S(1)}, bf16[512,4096]{1,0:T(8,128)(2,1)}, u32[]{:S(2)}) copy-start(bf16[512,4096]{1,0:T(8,128)(2,1)} %all-gather.2.cloned.1.call-done) | copy-start | bytes 12582916
  79.6 4.5 %collective-permute-start.4 = (f32[4,512]{1,0:T(4,128)S(1)}, f32[4,512]{1,0:T(4,128)S(1)}, u32[]{:S(2)}, u32[]{:S(2)}) collective-permute-start(f32[4,512]{1,0:T(4,128)S(1)} %pad_maximum_fusion), channel_id=1, source_target_pairs={{0,3},{1,0},{2,1},{3,2},{4,7},{5,4},{6,5},{7,6},{8,11},{9,8},{10,9... | collective-permute-start | bytes 24584 | tf_op jit(solution)/shard_map/ppermute | solution.py:25
  82.4 5.2 %collective-permute-start.3 = (f32[4,512]{1,0:T(4,128)S(1)}, f32[4,512]{1,0:T(4,128)S(1)}, u32[]{:S(2)}, u32[]{:S(2)}) collective-permute-start(f32[4,512]{1,0:T(4,128)S(1)} %pad_maximum_fusion), channel_id=1, source_target_pairs={{0,2},{1,3},{2,0},{3,1},{4,6},{5,7},{6,4},{7,5},{8,10},{9,11},{10,... | collective-permute-start | bytes 24584 | tf_op jit(solution)/shard_map/ppermute | solution.py:25
  83.2 4.9 %collective-permute-start.2 = (f32[4,512]{1,0:T(4,128)S(1)}, f32[4,512]{1,0:T(4,128)S(1)}, u32[]{:S(2)}, u32[]{:S(2)}) collective-permute-start(f32[4,512]{1,0:T(4,128)S(1)} %pad_maximum_fusion), channel_id=1, source_target_pairs={{0,1},{1,2},{2,3},{3,0},{4,5},{5,6},{6,7},{7,4},{8,9},{9,10},{10,1... | collective-permute-start | bytes 24584 | tf_op jit(solution)/shard_map/ppermute | solution.py:25
  88.1 4.8 %collective-permute-start.7 = (f32[4,512]{1,0:T(4,128)S(1)}, f32[4,512]{1,0:T(4,128)S(1)}, u32[]{:S(2)}, u32[]{:S(2)}) collective-permute-start(f32[4,512]{1,0:T(4,128)S(1)} %pad_maximum_fusion.1), channel_id=1, source_target_pairs={{0,12},{4,0},{8,4},{12,8},{1,13},{5,1},{9,5},{13,9},{2,14},{6,2},{... | collective-permute-start | bytes 24584 | tf_op jit(solution)/shard_map/ppermute | solution.py:25
  88.8 5.2 %collective-permute-start.6 = (f32[4,512]{1,0:T(4,128)S(1)}, f32[4,512]{1,0:T(4,128)S(1)}, u32[]{:S(2)}, u32[]{:S(2)}) collective-permute-start(f32[4,512]{1,0:T(4,128)S(1)} %pad_maximum_fusion.1), channel_id=1, source_target_pairs={{0,8},{4,12},{8,0},{12,4},{1,9},{5,13},{9,1},{13,5},{2,10},{6,14},... | collective-permute-start | bytes 24584 | tf_op jit(solution)/shard_map/ppermute | solution.py:25
  91.2 3.7 %collective-permute-start.5 = (f32[4,512]{1,0:T(4,128)S(1)}, f32[4,512]{1,0:T(4,128)S(1)}, u32[]{:S(2)}, u32[]{:S(2)}) collective-permute-start(f32[4,512]{1,0:T(4,128)S(1)} %pad_maximum_fusion.1), channel_id=1, source_target_pairs={{0,4},{4,8},{8,12},{12,0},{1,5},{5,9},{9,13},{13,1},{2,6},{6,10},{... | collective-permute-start | bytes 24584 | tf_op jit(solution)/shard_map/ppermute | solution.py:25
  94.9 4.4 %collective-permute-start.10 = (f32[4,512]{1,0:T(4,128)S(1)}, f32[4,512]{1,0:T(4,128)S(1)}, u32[]{:S(2)}, u32[]{:S(2)}) collective-permute-start(f32[4,512]{1,0:T(4,128)S(1)} %pad_maximum_fusion.2), channel_id=1, source_target_pairs={{0,96},{32,0},{64,32},{96,64},{1,97},{33,1},{65,33},{97,65},{2,98}... | collective-permute-start | bytes 24584 | tf_op jit(solution)/shard_map/ppermute | solution.py:25
  97.9 64.0 %collective-permute-start.12 = (bf16[512,4096]{1,0:T(8,128)(2,1)}, bf16[512,4096]{1,0:T(8,128)(2,1)}, u32[]{:S(2)}, u32[]{:S(2)}) collective-permute-start(bf16[512,4096]{1,0:T(8,128)(2,1)} %all-gather.2.cloned.1.call-done), channel_id=1, source_target_pairs={{0,16},{16,0},{1,17},{17,1},{2,18},{18,2},{3,19},{19,3},{4,20},{20... | collective-permute-start | bytes 12582920 | tf_op jit(solution)/shard_map/ppermute | solution.py:37
  97.9 4.5 %collective-permute-start.9 = (f32[4,512]{1,0:T(4,128)S(1)}, f32[4,512]{1,0:T(4,128)S(1)}, u32[]{:S(2)}, u32[]{:S(2)}) collective-permute-start(f32[4,512]{1,0:T(4,128)S(1)} %pad_maximum_fusion.2), channel_id=1, source_target_pairs={{0,64},{32,96},{64,0},{96,32},{1,65},{33,97},{65,1},{97,33},{2,66}... | collective-permute-start | bytes 24584 | tf_op jit(solution)/shard_map/ppermute | solution.py:25
  97.9 5.5 %collective-permute-start.8 = (f32[4,512]{1,0:T(4,128)S(1)}, f32[4,512]{1,0:T(4,128)S(1)}, u32[]{:S(2)}, u32[]{:S(2)}) collective-permute-start(f32[4,512]{1,0:T(4,128)S(1)} %pad_maximum_fusion.2), channel_id=1, source_target_pairs={{0,32},{32,64},{64,96},{96,0},{1,33},{33,65},{65,97},{97,1},{2,34}... | collective-permute-start | bytes 24584 | tf_op jit(solution)/shard_map/ppermute | solution.py:25
  105.2 1.1 copy-start.1
  116.7 32.8 %all-to-all-start = ((bf16[16,16,4096]{2,1,0:T(8,128)(2,1)}), bf16[16,16,4096]{2,1,0:T(8,128)(2,1)S(1)}, u32[]{:S(2)}, u32[]{:S(2)}) async-start(bf16[16,16,4096]{2,1,0:T(8,128)(2,1)} %bitcast.46), calls=%async_computation | async-start | bytes 4194304 | tf_op jit(solution)/shard_map/all_to_all | solution.py:32
  122.8 39.2 %collective-permute-start.11 = (bf16[512,594]{0,1:T(8,128)(2,1)}, bf16[512,594]{0,1:T(8,128)(2,1)}, u32[]{:S(2)}, u32[]{:S(2)}) collective-permute-start(bf16[512,594]{0,1:T(8,128)(2,1)} %get-tuple-element.23), channel_id=1, source_target_pairs={{0,16},{16,0},{1,17},{17,1},{2,18},{18,2},{3,19},{19,3},{4,20},{20... | collective-permute-start | bytes 1824776 | tf_op jit(solution)/shard_map/ppermute | solution.py:37
  150.5 10.8 %all-to-all-start.1 = ((bf16[4,4,4096]{2,1,0:T(4,128)(2,1)}), bf16[4,4,4096]{2,1,0:T(4,128)(2,1)S(1)}, u32[]{:S(2)}, u32[]{:S(2)}) async-start(bf16[4,4,4096]{2,1,0:T(4,128)(2,1)} %reshape.588), calls=%async_computation.1 | async-start | bytes 262144 | tf_op jit(solution)/shard_map/all_to_all | solution.py:32
Sparse Core Ops, SparseCore 0:
  9.8 57.7 all-gather.1

commit v3 on v2

v3 whole, which is shorter than its diff:
```python
import jax
import jax.numpy as jnp
from jax import lax
from jax.experimental import pallas as pl
from jax.experimental.pallas import tpu as pltpu
from jax.sharding import Mesh, PartitionSpec as P

LOSS_SCALE = 1024
KL_WEIGHT = 0.1
ENTROPY_WEIGHT = 0.05


def combine(parts):
    top = parts[0][0]
    for part in parts[1:]:
        top = jnp.maximum(top, part[0])
    scales = [jnp.exp(part[0] - top) for part in parts]
    total = sum(part[1] * scale for part, scale in zip(parts, scales))
    logit = sum(part[2] * scale for part, scale in zip(parts, scales))
    target = sum(part[3] for part in parts)
    return jnp.stack([top, total, logit, target])


def exchange(stats, axis):
    size = lax.axis_size(axis)
    others = [
        lax.ppermute(stats, axis, [(i, (i + step) % size) for i in range(size)])
        for step in range(1, size)
    ]
    return combine([stats] + others)


def scatter_sum(parts, axis):
    got = lax.all_to_all(parts, axis, 0, 0, tiled=True)
    return jnp.sum(got.astype(jnp.float32), axis=0)


def swap(value, axis):
    return lax.ppermute(value, axis, [(0, 1), (1, 0)])


def rows_kernel(order, grad0, grad1, weight0, weight1, out, held0, held1):
    @pl.when(pl.program_id(0) == 0)
    def _():
        for grad, held in ((grad0, held0), (grad1, held1)):
            held[...] = lax.dot_general(
                order[...], grad[...], (((1,), (1,)), ((), ())), preferred_element_type=jnp.float32
            ).astype(jnp.bfloat16)

    out[...] = (
        jnp.dot(held0[...], weight0[...], preferred_element_type=jnp.float32)
        + jnp.dot(held1[...], weight1[...], preferred_element_type=jnp.float32)
    ).astype(jnp.bfloat16)


def hidden_partial(order, grads, weights):
    width, depth = weights[0].shape
    rows, tokens = order.shape
    tile = 512
    whole = lambda *shape: pl.BlockSpec(shape, lambda i: (0, 0))
    return pl.pallas_call(
        rows_kernel,
        grid=(depth // tile,),
        in_specs=[whole(rows, tokens)]
        + [whole(width, tokens)] * 2
        + [pl.BlockSpec((width, tile), lambda i: (0, i))] * 2,
        out_specs=pl.BlockSpec((rows, tile), lambda i: (0, i)),
        out_shape=jax.ShapeDtypeStruct((rows, depth), jnp.bfloat16),
        scratch_shapes=[pltpu.VMEM((rows, width), jnp.bfloat16)] * 2,
        compiler_params=pltpu.CompilerParams(vmem_limit_bytes=32 * 2**20),
        name="grad_hidden_partial",
    )(order, *grads, *weights)


def head_kernel(*refs):
    out, half = refs[-1], (len(refs) - 1) // 2
    total = 0.0
    for grad, hidden in zip(refs[:half], refs[half:-1]):
        total = total + jnp.dot(grad[...], hidden[...], preferred_element_type=jnp.float32)
    out[...] = total.astype(jnp.bfloat16)


def head_gradient(grads, hiddens):
    width, tokens = grads[0].shape
    depth = hiddens[0].shape[1]
    tile, count = 512, len(grads)
    return pl.pallas_call(
        head_kernel,
        grid=(depth // tile,),
        in_specs=[pl.BlockSpec((width, tokens), lambda i: (0, 0))] * count
        + [pl.BlockSpec((tokens, tile), lambda i: (0, i))] * count,
        out_specs=pl.BlockSpec((width, tile), lambda i: (0, i)),
        out_shape=jax.ShapeDtypeStruct((width, depth), jnp.bfloat16),
        compiler_params=pltpu.CompilerParams(vmem_limit_bytes=32 * 2**20),
        cost_estimate=pl.CostEstimate(
            flops=2 * count * tokens * width * depth,
            bytes_accessed=2 * depth * (width + count * tokens),
            transcendentals=0,
        ),
        name="grad_head",
    )(*grads, *hiddens)


CHUNKS = 2


def per_device(
    hidden, head_weight, targets, segment_ids, lengths, loss_mask, advantages, ref_logprobs
):
    bf16, f32 = jnp.bfloat16, jnp.float32
    depth, width = head_weight.shape
    ndp, nz, ncore = lax.axis_size("dp"), lax.axis_size("z"), lax.axis_size("core")
    nv = lax.axis_size("x") * lax.axis_size("y")
    block = hidden.shape[0]
    rows = block // nv // CHUNKS
    dp, z, core = lax.axis_index("dp"), lax.axis_index("z"), lax.axis_index("core")
    place = lax.axis_index(("x", "y"))

    pieces = hidden.reshape(nv, CHUNKS, rows, depth)
    gathered = []
    for k in range(CHUNKS):
        piece = pieces[:, k].reshape(nv * rows, depth)
        if k:
            piece, gathered[-1] = lax.optimization_barrier((piece, gathered[-1]))
        gathered.append(lax.all_gather(piece, ("dp", "z"), axis=0, tiled=True))
    weights = [head_weight, swap(head_weight, "core")]
    first_columns = [((z * ncore + c) * nv + place) * width for c in (core, 1 - core)]

    seq_onehot = segment_ids[:, None] == lax.iota(jnp.int32, advantages.shape[0])[None, :]
    token_adv = jnp.sum(jnp.where(seq_onehot, advantages[None, :], 0.0), axis=1)
    token_len = jnp.sum(jnp.where(seq_onehot, lengths[None, :].astype(f32), 0.0), axis=1)
    token_weight = LOSS_SCALE * loss_mask.astype(f32) / token_len
    own = jnp.stack([token_adv, token_weight, ref_logprobs, targets.astype(f32)])
    own = own.reshape(4, nz, ncore, block)
    own = jnp.where(core == 0, own[:, :, 0], own[:, :, 1]).reshape(4, nz * block)
    other = swap(own, "dp")
    both = jnp.stack(
        [jnp.where(dp == 0, own, other), jnp.where(dp == 0, other, own)], axis=1
    ).reshape(4, ndp * nz * nv, CHUNKS, rows)

    tokens, mine = ndp * nz * nv * rows, nz * nv * rows
    row = lax.iota(jnp.int32, mine)
    source = ((dp * nz + row // rows % nz) * nv + row // (rows * nz)) * rows + row % rows
    order = (source[:, None] == lax.iota(jnp.int32, tokens)[None, :]).astype(bf16)

    sums, head_grads, head_hidden = [], [], []
    for k in range(CHUNKS):
        adv, weight, ref = [both[i, :, k].reshape(tokens) for i in range(3)]
        target = both[3, :, k].reshape(tokens).astype(jnp.int32)
        logits = [jnp.dot(gathered[k], w, preferred_element_type=f32) for w in weights]
        hits = [
            target[:, None] == (c + lax.iota(jnp.int32, width))[None, :] for c in first_columns
        ]
        local_max = jnp.maximum(*[jnp.max(part, axis=1) for part in logits])
        shifted = [jnp.exp(part - local_max[:, None]) for part in logits]
        stats = jnp.stack(
            [
                local_max,
                sum(jnp.sum(s, axis=1) for s in shifted),
                sum(jnp.sum(s * part, axis=1) for s, part in zip(shifted, logits)),
                sum(jnp.sum(jnp.where(h, part, 0.0), axis=1) for h, part in zip(hits, logits)),
            ]
        )
        for axis in ("z", "y", "x"):
            if k and axis == "y":
                stats, sums[-1] = lax.optimization_barrier((stats, sums[-1]))
            stats = exchange(stats, axis)
        row_max, exp_total, exp_logit, target_logit = stats[0], stats[1], stats[2], stats[3]
        log_total = row_max + jnp.log(exp_total)
        target_logp = target_logit - log_total
        mean_logit = exp_logit / exp_total
        logp_grad = -adv + KL_WEIGHT * (target_logp - ref)
        grads = []
        for part, hit in zip(logits, hits):
            probs = jnp.exp(part - log_total[:, None])
            inner = logp_grad[:, None] * (hit.astype(f32) - probs)
            inner = inner + ENTROPY_WEIGHT * probs * (part - mean_logit[:, None])
            grads.append((weight[:, None] * inner).astype(bf16).T)
        partial = hidden_partial(order, grads, [w.T for w in weights])
        partial, other_grads = lax.optimization_barrier((partial, swap(grads[1], "core")))
        head_grads += [grads[0], other_grads]
        head_hidden += [gathered[k], swap(gathered[k], "core")]
        if k + 1 < CHUNKS:
            gathered[k + 1], partial = lax.optimization_barrier((gathered[k + 1], partial))
        got = lax.all_to_all(
            partial.reshape(nv, nz * rows, depth), ("x", "y"), 0, 0, tiled=True
        )
        sums.append(got)

    grad_head = head_gradient(head_grads, head_hidden)
    sums[-1], grad_head = lax.optimization_barrier((sums[-1], grad_head))
    sums = [jnp.sum(got.astype(f32), axis=0).astype(bf16).reshape(nz, rows, depth) for got in sums]
    grad_hidden = scatter_sum(jnp.concatenate(sums, axis=1), "z").astype(bf16)
    return grad_hidden, grad_head.T


def solution(mesh):
    devices = mesh.devices.reshape(2, 4, 2, 4, 4)
    fine = Mesh(devices, ("dp", "z", "core", "x", "y"))
    ctx, vocab = ("z", "core"), ("x", "y")
    return jax.shard_map(
        per_device,
        mesh=fine,
        in_specs=(
            P(("dp",) + ctx, None),
            P(None, ctx + vocab),
            P("dp"),
            P("dp"),
            P(),
            P("dp"),
            P(),
            P("dp"),
        ),
        out_specs=(P(("dp",) + ctx + vocab, None), P(None, ctx + vocab)),
        check_vma=False,
    )
```

time: 182 us -> 198 us (1.088)
  waiting for transfers between devices: 86.3 us -> 53.5 us
  Pallas kernels: 0 us -> 25.5 us
  matrix products: 38.5 us -> 18.2 us
  starting transfers between devices: 29.8 us -> 46.4 us
  local copies, waits for them, and re-layouts: 3.51 us -> 12.9 us
  other arithmetic: 6.6 us -> 15.7 us
  blocking collectives: 0 us -> 8.45 us
    pallas_call x0 -> x3, Pallas kernels: none -> 25.5 us  [the longest x2 15.6 us: hidden_partial(): pl.pallas_call(rows_kernel, grid=(depth // tile,), in_specs=[whole(rows,...]
    all_to_all x2, waiting for transfers between devices: 26.7 us -> 3.77 us  [per_device(): lax.all_to_all(partial.reshape(nv, nz * rows, depth), ('x', 'y'), 0, 0, t...]
    dot_general x6 -> x4, matrix products: 38.5 us -> 18.2 us  [per_device(): jnp.dot(gathered[k], w, preferred_element_type=f32)]
    all_gather x1 -> x2, waiting for transfers between devices: 46.8 us -> 29.9 us  [per_device(): gathered.append(lax.all_gather(piece, ('dp', 'z'), axis=0, tiled=True))]
    ppermute x9 -> x18, starting transfers between devices: 13.1 us -> 25.6 us  [exchange(): lax.ppermute(stats, axis, [(i, (i + step) % size) for i in range(size)])]
    ppermute x9 -> x18, waiting for transfers between devices: 10.5 us -> 19 us  [exchange(): lax.ppermute(stats, axis, [(i, (i + step) % size) for i in range(size)])]
    all_to_all x0 -> x1, blocking collectives: none -> 8.45 us  [scatter_sum(): got = lax.all_to_all(parts, axis, 0, 0, tiled=True)]
    unnamed x7 -> x32, local copies, waits for them, and re-layouts: 0.5 us -> 7.28 us
  transfers between devices with their start and end apart: 16 -> 28, of which waited for: 10 -> 16; matrix products, arithmetic and copies ran while one was open for 18% -> 19% of each run, Pallas kernels for 0% -> 13%
where the time goes in v3:
time: 198 us; the launch traced here: 195 us
  waiting for transfers between devices  53.5 us (27%)
  starting transfers between devices  46.4 us (23%)
  Pallas kernels  25.5 us (13%)
  matrix products  18.2 us (9%)
  other arithmetic  15.7 us (8%)
  between operations  14.5 us (7%)
  local copies, waits for them, and re-layouts  12.9 us (7%)
  blocking collectives  8.45 us (4%)
    all_gather x2, waiting for transfers between devices, per_device(): gathered.append(lax.all_gather(piece, ('dp', 'z'), axis=0, tiled=True))  29.9 us
    ppermute x18, starting transfers between devices, exchange(): lax.ppermute(stats, axis, [(i, (i + step) % size) for i in range(size)])  25.6 us
    ppermute x18, waiting for transfers between devices, exchange(): lax.ppermute(stats, axis, [(i, (i + step) % size) for i in range(size)])  19 us
    dot_general x4, matrix products, per_device(): jnp.dot(gathered[k], w, preferred_element_type=f32)  18.2 us
    pallas_call x2, Pallas kernels, hidden_partial(): pl.pallas_call(rows_kernel, grid=(depth // tile,), in_specs=[whole(rows,...  15.6 us
    all_to_all x2, starting transfers between devices, per_device(): lax.all_to_all(partial.reshape(nv, nz * rows, depth), ('x', 'y'), 0, 0, t...  12.7 us
    pallas_call x1, Pallas kernels, head_gradient(): pl.pallas_call(head_kernel, grid=(depth // tile,), in_specs=[pl.BlockSpec...  9.92 us
    all_to_all x1, blocking collectives, scatter_sum(): got = lax.all_to_all(parts, axis, 0, 0, tiled=True)  8.45 us
  transfers between devices with their start and end apart: 28, of which 16 were waited for; matrix products, arithmetic and copies ran while one was open for 19% of the time, Pallas kernels for 13%

profile of v3, /device:TPU:2, one launch (start us, length us, event | category | flops | bytes accessed | tf_op | source)
XLA Modules:
  0.0 195.2 jit_solution(7706429267836512999)
XLA Ops:
  10.8 7.2 %collective-permute-start = (f32[4,256]{1,0:T(4,128)S(1)}, f32[4,256]{1,0:T(4,128)S(1)}, u32[]{:S(2)}, u32[]{:S(2)}) collective-permute-start(f32[4,256]{1,0:T(4,128)S(1)} %select_n.88), channel_id=1, source_target_pairs={{0,128},{128,0},{1,129},{129,1},{2,130},{130,2},{3,131},{131,3},{4... | collective-permute-start | bytes 12296 | tf_op jit(solution)/shard_map/ppermute | solution.py:39
  19.7 4.7 %fusion.21 = (s32[128,2]{1,0:T(8,128)}, s32[128,2]{1,0:T(8,128)S(1)}) fusion(f32[4,128,2,2]{0,3,2,1:T(2,128)S(1)} %bitcast.162), kind=kLoop, calls=%fused_computation.51 | loop fusion | flops 512 | bytes 4096 | tf_op jit(solution)/shard_map/convert_element_type | solution.py:149
  24.5 29.9 %all-gather.3.cloned.1.call-done.refs_4_ = bf16[256,4096]{1,0:T(8,128)(2,1)} async-done(((bf16[32,4096]{1,0:T(8,128)(2,1)}), bf16[256,4096]{1,0:T(8,128)(2,1)}) %all-gather.3.cloned.1.call-update) | async-done | bytes 2097168 | tf_op jit(solution)/shard_map/all_gather | solution.py:125
  54.5 4.7 %fusion.42 = (f32[256]{0:T(256)S(1)}, f32[256,594]{0,1:T(8,128)S(1)}) fusion(bf16[256,4096]{1,0:T(8,128)(2,1)} %all-gather.3.cloned.1.call-done.refs_4_, bf16[4096,594]{0,1:T(8,128)(2,1)} %param.9), kind=kOutput, calls=%fused_computation.185 | convolution fusion | flops 1245860096 | bytes 7572480 | tf_op jit(solution)/shard_map/dot_general | solution.py:150
  59.2 4.7 %fusion.43 = (f32[256]{0:T(256)S(1)}, f32[256,594]{0,1:T(8,128)}) fusion(bf16[256,4096]{1,0:T(8,128)(2,1)S(1)} %copy-done.2, bf16[4096,594]{0,1:T(8,128)(2,1)} %collective-permute-done.1), kind=kOutput, calls=%fused_computation.186 | convolution fusion | flops 1245860096 | bytes 7572480 | tf_op jit(solution)/shard_map/dot_general | solution.py:150
  65.4 2.8 %collective-permute-start.4 = (f32[4,256]{1,0:T(4,128)S(1)}, f32[4,256]{1,0:T(4,128)S(1)}, u32[]{:S(2)}, u32[]{:S(2)}) collective-permute-start(f32[4,256]{1,0:T(4,128)S(1)} %pad_maximum_fusion.2), channel_id=1, source_target_pairs={{0,96},{32,0},{64,32},{96,64},{1,97},{33,1},{65,33},{97,65},{2,98}... | collective-permute-start | bytes 12296 | tf_op jit(solution)/shard_map/ppermute | solution.py:27
  69.6 3.3 %collective-permute-done.3 = f32[4,256]{1,0:T(4,128)S(1)} collective-permute-done((f32[4,256]{1,0:T(4,128)S(1)}, f32[4,256]{1,0:T(4,128)S(1)}, u32[]{:S(2)}, u32[]{:S(2)}) %collective-permute-start.3) | collective-permute-done | bytes 4128 | tf_op jit(solution)/shard_map/ppermute | solution.py:27
  73.9 2.8 %collective-permute-start.7 = (f32[4,256]{1,0:T(4,128)S(1)}, f32[4,256]{1,0:T(4,128)S(1)}, u32[]{:S(2)}, u32[]{:S(2)}) collective-permute-start(f32[4,256]{1,0:T(4,128)S(1)} %pad_maximum_fusion.3), channel_id=1, source_target_pairs={{0,3},{1,0},{2,1},{3,2},{4,7},{5,4},{6,5},{7,6},{8,11},{9,8},{10,9... | collective-permute-start | bytes 12296 | tf_op jit(solution)/shard_map/ppermute | solution.py:27
  78.4 3.4 %collective-permute-done.6 = f32[4,256]{1,0:T(4,128)S(1)} collective-permute-done((f32[4,256]{1,0:T(4,128)S(1)}, f32[4,256]{1,0:T(4,128)S(1)}, u32[]{:S(2)}, u32[]{:S(2)}) %collective-permute-start.6) | collective-permute-done | bytes 4128 | tf_op jit(solution)/shard_map/ppermute | solution.py:27
  85.0 2.5 %collective-permute-start.9 = (f32[4,256]{1,0:T(4,128)S(1)}, f32[4,256]{1,0:T(4,128)S(1)}, u32[]{:S(2)}, u32[]{:S(2)}) collective-permute-start(f32[4,256]{1,0:T(4,128)S(1)} %pad_maximum_fusion.4), channel_id=1, source_target_pairs={{0,8},{4,12},{8,0},{12,4},{1,9},{5,13},{9,1},{13,5},{2,10},{6,14},... | collective-permute-start | bytes 12296 | tf_op jit(solution)/shard_map/ppermute | solution.py:27
  93.9 2.4 %copy-done = bf16[4096,594]{0,1:T(8,128)(2,1)S(1)} copy-done((bf16[4096,594]{0,1:T(8,128)(2,1)S(1)}, bf16[4096,594]{0,1:T(8,128)(2,1)}, u32[]{:S(2)}) %copy-start) | copy-done | bytes 4866072
  96.3 7.8 %grad_hidden_partial.2 = bf16[128,4096]{1,0:T(8,128)(2,1)} custom-call(bf16[128,256]{1,0:T(8,128)(2,1)S(1)} %fusion.24.order, bf16[594,256]{1,0:T(8,128)(2,1)S(1)} %get-tuple-element.83.grad0.refs_0_, bf16[594,256]{1,0:T(8,128)(2,1)S(1)} %get-tuple-element.82.grad1, bf16[594,4096]{1,0:T(8,128)(2,1)S(1)} %bitcast.160, bf16[594,4096]{1,0:T(8,128)(2,1)} %bitcast.48.weight1), custom_call_target="tpu_custom_call" | custom-call | tf_op jit(solution)/shard_map/grad_hidden_partial/pallas_call | solution.py:61
  104.1 6.4 %all-to-all-start = ((bf16[16,8,4096]{2,1,0:T(8,128)(2,1)}), bf16[16,8,4096]{2,1,0:T(8,128)(2,1)}, u32[]{:S(2)}, u32[]{:S(2)}) async-start(bf16[16,8,4096]{2,1,0:T(8,128)(2,1)} %bitcast.53), calls=%async_computation | async-start | bytes 2097152 | tf_op jit(solution)/shard_map/all_to_all | solution.py:185
  110.5 4.7 %fusion.44 = (f32[256]{0:T(256)S(1)}, f32[256,594]{0,1:T(8,128)S(1)}) fusion(bf16[256,4096]{1,0:T(8,128)(2,1)} %all-gather.5.cloned.1.call-done.refs_6_, bf16[4096,594]{0,1:T(8,128)(2,1)} %param.9), kind=kOutput, calls=%fused_computation.187 | convolution fusion | flops 1245860096 | bytes 7572480 | tf_op jit(solution)/shard_map/dot_general | solution.py:150
  115.2 4.2 %fusion.45 = (f32[256]{0:T(256)S(1)}, f32[256,594]{0,1:T(8,128)S(1)}) fusion(bf16[256,4096]{1,0:T(8,128)(2,1)S(1)} %copy-done.3, bf16[4096,594]{0,1:T(8,128)(2,1)} %collective-permute-done.1), kind=kOutput, calls=%fused_computation.188 | convolution fusion | flops 1245860096 | bytes 7572480 | tf_op jit(solution)/shard_map/dot_general | solution.py:150
  121.7 1.9 collective-permute-start.12
  127.2 2.8 %collective-permute-start.17 = (f32[4,256]{1,0:T(4,128)S(1)}, f32[4,256]{1,0:T(4,128)S(1)}, u32[]{:S(2)}, u32[]{:S(2)}) collective-permute-start(f32[4,256]{1,0:T(4,128)S(1)} %pad_maximum_fusion.6), channel_id=1, source_target_pairs={{0,3},{1,0},{2,1},{3,2},{4,7},{5,4},{6,5},{7,6},{8,11},{9,8},{10,9... | collective-permute-start | bytes 12296 | tf_op jit(solution)/shard_map/ppermute | solution.py:27
  132.2 2.9 %collective-permute-done.16 = f32[4,256]{1,0:T(4,128)S(1)} collective-permute-done((f32[4,256]{1,0:T(4,128)S(1)}, f32[4,256]{1,0:T(4,128)S(1)}, u32[]{:S(2)}, u32[]{:S(2)}) %collective-permute-start.16) | collective-permute-done | bytes 4128 | tf_op jit(solution)/shard_map/ppermute | solution.py:27
  144.4 2.4 %copy-done.1 = bf16[4096,594]{0,1:T(8,128)(2,1)S(1)} copy-done((bf16[4096,594]{0,1:T(8,128)(2,1)S(1)}, bf16[4096,594]{0,1:T(8,128)(2,1)}, u32[]{:S(2)}) %copy-start.1) | copy-done | bytes 4866072
  146.8 7.8 %grad_hidden_partial.3 = bf16[128,4096]{1,0:T(8,128)(2,1)} custom-call(bf16[128,256]{1,0:T(8,128)(2,1)S(1)} %fusion.24.order, bf16[594,256]{1,0:T(8,128)(2,1)S(1)} %get-tuple-element.81.grad0.refs_2_, bf16[594,256]{1,0:T(8,128)(2,1)S(1)} %get-tuple-element.80.grad1, bf16[594,4096]{1,0:T(8,128)(2,1)S(1)} %bitcast.161, bf16[594,4096]{1,0:T(8,128)(2,1)} %bitcast.48.weight1), custom_call_target="tpu_custom_call" | custom-call | tf_op jit(solution)/shard_map/grad_hidden_partial/pallas_call | solution.py:61
  154.6 6.3 %all-to-all-start.1 = ((bf16[16,8,4096]{2,1,0:T(8,128)(2,1)}), bf16[16,8,4096]{2,1,0:T(8,128)(2,1)}, u32[]{:S(2)}, u32[]{:S(2)}) async-start(bf16[16,8,4096]{2,1,0:T(8,128)(2,1)} %bitcast.80), calls=%async_computation.1 | async-start | bytes 2097152 | tf_op jit(solution)/shard_map/all_to_all | solution.py:185
  164.0 9.9 %grad_head.1 = bf16[594,4096]{1,0:T(8,128)(2,1)} custom-call(bf16[594,256]{1,0:T(8,128)(2,1)S(1)} %get-tuple-element.83.grad0.refs_0_, bf16[594,256]{1,0:T(8,128)(2,1)S(1)} %collective-permute-done.11.refs_1_, bf16[594,256]{1,0:T(8,128)(2,1)S(1)} %get-tuple-element.81.grad0.refs_2_, bf16[594,256]{1,0:T(8,128)(2,1)S(1)} %collective-permute-done.21.refs_3_, ...), custom_call_target="tpu_custom_call" | custom-call | flops 4982833152 | bytes 13254656 | tf_op jit(solution)/shard_map/grad_head/pallas_call | solution.py:87
  173.9 3.7 %all-to-all-done.1 = bf16[16,8,4096]{2,1,0:T(8,128)(2,1)} async-done(((bf16[16,8,4096]{2,1,0:T(8,128)(2,1)}), bf16[16,8,4096]{2,1,0:T(8,128)(2,1)}, u32[]{:S(2)}, u32[]{:S(2)}) %all-to-all-start.1) | async-done | bytes 1048608 | tf_op jit(solution)/shard_map/all_to_all | solution.py:185
  179.2 8.4 %all_to_all.15 = bf16[4,4,4096]{2,1,0:T(4,128)(2,1)S(1)} all-to-all(bf16[4,4,4096]{2,1,0:T(4,128)(2,1)S(1)} %pad_maximum_fusion), channel_id=1, replica_groups=mesh['dp'=2,'z'=4,'core'=2,'x'=4,'y'=4] {'z'}, dimensions={0} | all-to-all | bytes 262144 | tf_op jit(solution)/shard_map/all_to_all | solution.py:34
  (144 shorter events, 43.0 us)
Async XLA Ops:
  7.2 47.2 %all-gather.3.cloned.1.call-start = ((), (), s32[]{:S(2)}) async-start(), calls=%async_computation.3 | async-start | bytes 2359296 | tf_op jit(solution)/shard_map/all_gather | solution.py:125
  7.3 51.9 %collective-permute-start.1 = (bf16[4096,594]{0,1:T(8,128)(2,1)}, bf16[4096,594]{0,1:T(8,128)(2,1)}, u32[]{:S(2)}, u32[]{:S(2)}) collective-permute-start(bf16[4096,594]{0,1:T(8,128)(2,1)} %param.9), channel_id=1, source_target_pairs={{0,16},{16,0},{1,17},{17,1},{2,18},{18,2},{3,19},{19,3},{4,20},{20... | collective-permute-start | bytes 14598152 | tf_op jit(solution)/shard_map/ppermute | solution.py:39
  10.0 94.1 %all-gather.5.cloned.1.call-start = ((), (), s32[]{:S(2)}) async-start(), calls=%async_computation.4 | async-start | bytes 2359296 | tf_op jit(solution)/shard_map/all_gather | solution.py:125
  10.8 8.8 %collective-permute-start = (f32[4,256]{1,0:T(4,128)S(1)}, f32[4,256]{1,0:T(4,128)S(1)}, u32[]{:S(2)}, u32[]{:S(2)}) collective-permute-start(f32[4,256]{1,0:T(4,128)S(1)} %select_n.88), channel_id=1, source_target_pairs={{0,128},{128,0},{1,129},{129,1},{2,130},{130,2},{3,131},{131,3},{4... | collective-permute-start | bytes 12296 | tf_op jit(solution)/shard_map/ppermute | solution.py:39
  68.3 4.6 %collective-permute-start.3 = (f32[4,256]{1,0:T(4,128)S(1)}, f32[4,256]{1,0:T(4,128)S(1)}, u32[]{:S(2)}, u32[]{:S(2)}) collective-permute-start(f32[4,256]{1,0:T(4,128)S(1)} %pad_maximum_fusion.2), channel_id=1, source_target_pairs={{0,64},{32,96},{64,0},{96,32},{1,65},{33,97},{65,1},{97,33},{2,66}... | collective-permute-start | bytes 12296 | tf_op jit(solution)/shard_map/ppermute | solution.py:27
  68.3 5.5 %collective-permute-start.2 = (f32[4,256]{1,0:T(4,128)S(1)}, f32[4,256]{1,0:T(4,128)S(1)}, u32[]{:S(2)}, u32[]{:S(2)}) collective-permute-start(f32[4,256]{1,0:T(4,128)S(1)} %pad_maximum_fusion.2), channel_id=1, source_target_pairs={{0,32},{32,64},{64,96},{96,0},{1,33},{33,65},{65,97},{97,1},{2,34}... | collective-permute-start | bytes 12296 | tf_op jit(solution)/shard_map/ppermute | solution.py:27
  73.9 4.5 %collective-permute-start.7 = (f32[4,256]{1,0:T(4,128)S(1)}, f32[4,256]{1,0:T(4,128)S(1)}, u32[]{:S(2)}, u32[]{:S(2)}) collective-permute-start(f32[4,256]{1,0:T(4,128)S(1)} %pad_maximum_fusion.3), channel_id=1, source_target_pairs={{0,3},{1,0},{2,1},{3,2},{4,7},{5,4},{6,5},{7,6},{8,11},{9,8},{10,9... | collective-permute-start | bytes 12296 | tf_op jit(solution)/shard_map/ppermute | solution.py:27
  76.7 5.1 %collective-permute-start.6 = (f32[4,256]{1,0:T(4,128)S(1)}, f32[4,256]{1,0:T(4,128)S(1)}, u32[]{:S(2)}, u32[]{:S(2)}) collective-permute-start(f32[4,256]{1,0:T(4,128)S(1)} %pad_maximum_fusion.3), channel_id=1, source_target_pairs={{0,2},{1,3},{2,0},{3,1},{4,6},{5,7},{6,4},{7,5},{8,10},{9,11},{10,... | collective-permute-start | bytes 12296 | tf_op jit(solution)/shard_map/ppermute | solution.py:27
  77.5 4.8 %collective-permute-start.5 = (f32[4,256]{1,0:T(4,128)S(1)}, f32[4,256]{1,0:T(4,128)S(1)}, u32[]{:S(2)}, u32[]{:S(2)}) collective-permute-start(f32[4,256]{1,0:T(4,128)S(1)} %pad_maximum_fusion.3), channel_id=1, source_target_pairs={{0,1},{1,2},{2,3},{3,0},{4,5},{5,6},{6,7},{7,4},{8,9},{9,10},{10,1... | collective-permute-start | bytes 12296 | tf_op jit(solution)/shard_map/ppermute | solution.py:27
  82.4 6.8 %collective-permute-start.10 = (f32[4,256]{1,0:T(4,128)S(1)}, f32[4,256]{1,0:T(4,128)S(1)}, u32[]{:S(2)}, u32[]{:S(2)}) collective-permute-start(f32[4,256]{1,0:T(4,128)S(1)} %pad_maximum_fusion.4), channel_id=1, source_target_pairs={{0,12},{4,0},{8,4},{12,8},{1,13},{5,1},{9,5},{13,9},{2,14},{6,2},{... | collective-permute-start | bytes 12296 | tf_op jit(solution)/shard_map/ppermute | solution.py:27
  85.0 5.2 %collective-permute-start.9 = (f32[4,256]{1,0:T(4,128)S(1)}, f32[4,256]{1,0:T(4,128)S(1)}, u32[]{:S(2)}, u32[]{:S(2)}) collective-permute-start(f32[4,256]{1,0:T(4,128)S(1)} %pad_maximum_fusion.4), channel_id=1, source_target_pairs={{0,8},{4,12},{8,0},{12,4},{1,9},{5,13},{9,1},{13,5},{2,10},{6,14},... | collective-permute-start | bytes 12296 | tf_op jit(solution)/shard_map/ppermute | solution.py:27
  92.7 11.4 %collective-permute-start.11 = (bf16[594,256]{1,0:T(8,128)(2,1)S(1)}, bf16[594,256]{1,0:T(8,128)(2,1)S(1)}, u32[]{:S(2)}, u32[]{:S(2)}) collective-permute-start(bf16[594,256]{1,0:T(8,128)(2,1)S(1)} %get-tuple-element.82.grad1), channel_id=1, source_target_pairs={{0,16},{16,0},{1,17},{17,1},{2,18},{18,2},{3,19},{19,3},{4,20},{20... | collective-permute-start | bytes 912392 | tf_op jit(solution)/shard_map/ppermute | solution.py:39
  104.1 23.1 %all-to-all-start = ((bf16[16,8,4096]{2,1,0:T(8,128)(2,1)}), bf16[16,8,4096]{2,1,0:T(8,128)(2,1)}, u32[]{:S(2)}, u32[]{:S(2)}) async-start(bf16[16,8,4096]{2,1,0:T(8,128)(2,1)} %bitcast.53), calls=%async_computation | async-start | bytes 2097152 | tf_op jit(solution)/shard_map/all_to_all | solution.py:185
  121.1 4.5 %collective-permute-start.13 = (f32[4,256]{1,0:T(4,128)S(1)}, f32[4,256]{1,0:T(4,128)S(1)}, u32[]{:S(2)}, u32[]{:S(2)}) collective-permute-start(f32[4,256]{1,0:T(4,128)S(1)} %pad_maximum_fusion.5), channel_id=1, source_target_pairs={{0,64},{32,96},{64,0},{96,32},{1,65},{33,97},{65,1},{97,33},{2,66}... | collective-permute-start | bytes 12296 | tf_op jit(solution)/shard_map/ppermute | solution.py:27
  121.7 5.4 %collective-permute-start.12 = (f32[4,256]{1,0:T(4,128)S(1)}, f32[4,256]{1,0:T(4,128)S(1)}, u32[]{:S(2)}, u32[]{:S(2)}) collective-permute-start(f32[4,256]{1,0:T(4,128)S(1)} %pad_maximum_fusion.5), channel_id=1, source_target_pairs={{0,32},{32,64},{64,96},{96,0},{1,33},{33,65},{65,97},{97,1},{2,34}... | collective-permute-start | bytes 12296 | tf_op jit(solution)/shard_map/ppermute | solution.py:27
  127.2 5.0 %collective-permute-start.17 = (f32[4,256]{1,0:T(4,128)S(1)}, f32[4,256]{1,0:T(4,128)S(1)}, u32[]{:S(2)}, u32[]{:S(2)}) collective-permute-start(f32[4,256]{1,0:T(4,128)S(1)} %pad_maximum_fusion.6), channel_id=1, source_target_pairs={{0,3},{1,0},{2,1},{3,2},{4,7},{5,4},{6,5},{7,6},{8,11},{9,8},{10,9... | collective-permute-start | bytes 12296 | tf_op jit(solution)/shard_map/ppermute | solution.py:27
  130.0 5.1 %collective-permute-start.16 = (f32[4,256]{1,0:T(4,128)S(1)}, f32[4,256]{1,0:T(4,128)S(1)}, u32[]{:S(2)}, u32[]{:S(2)}) collective-permute-start(f32[4,256]{1,0:T(4,128)S(1)} %pad_maximum_fusion.6), channel_id=1, source_target_pairs={{0,2},{1,3},{2,0},{3,1},{4,6},{5,7},{6,4},{7,5},{8,10},{9,11},{10,... | collective-permute-start | bytes 12296 | tf_op jit(solution)/shard_map/ppermute | solution.py:27
  130.8 4.8 %collective-permute-start.15 = (f32[4,256]{1,0:T(4,128)S(1)}, f32[4,256]{1,0:T(4,128)S(1)}, u32[]{:S(2)}, u32[]{:S(2)}) collective-permute-start(f32[4,256]{1,0:T(4,128)S(1)} %pad_maximum_fusion.6), channel_id=1, source_target_pairs={{0,1},{1,2},{2,3},{3,0},{4,5},{5,6},{6,7},{7,4},{8,9},{9,10},{10,1... | collective-permute-start | bytes 12296 | tf_op jit(solution)/shard_map/ppermute | solution.py:27
  131.7 30.7 %collective-permute-start.22 = (bf16[256,4096]{1,0:T(8,128)(2,1)S(1)}, bf16[256,4096]{1,0:T(8,128)(2,1)}, u32[]{:S(2)}, u32[]{:S(2)}) collective-permute-start(bf16[256,4096]{1,0:T(8,128)(2,1)S(1)} %copy-done.2), channel_id=1, source_target_pairs={{0,16},{16,0},{1,17},{17,1},{2,18},{18,2},{3,19},{19,3},{4,20},{20... | collective-permute-start | bytes 6291464 | tf_op jit(solution)/shard_map/ppermute | solution.py:39
  131.7 30.7 %collective-permute-start.23 = (bf16[256,4096]{1,0:T(8,128)(2,1)}, bf16[256,4096]{1,0:T(8,128)(2,1)}, u32[]{:S(2)}, u32[]{:S(2)}) collective-permute-start(bf16[256,4096]{1,0:T(8,128)(2,1)} %all-gather.5.cloned.1.call-done.refs_6_), channel_id=1, source_target_pairs={{0,16},{16,0},{1,17},{17,1},{2,18},{18,2},{3,19},{19,3},{4,20},{20... | collective-permute-start | bytes 6291464 | tf_op jit(solution)/shard_map/ppermute | solution.py:39
  135.7 5.3 %collective-permute-start.20 = (f32[4,256]{1,0:T(4,128)S(1)}, f32[4,256]{1,0:T(4,128)S(1)}, u32[]{:S(2)}, u32[]{:S(2)}) collective-permute-start(f32[4,256]{1,0:T(4,128)S(1)} %pad_maximum_fusion.7), channel_id=1, source_target_pairs={{0,12},{4,0},{8,4},{12,8},{1,13},{5,1},{9,5},{13,9},{2,14},{6,2},{... | collective-permute-start | bytes 12296 | tf_op jit(solution)/shard_map/ppermute | solution.py:27
  137.4 5.1 %collective-permute-start.19 = (f32[4,256]{1,0:T(4,128)S(1)}, f32[4,256]{1,0:T(4,128)S(1)}, u32[]{:S(2)}, u32[]{:S(2)}) collective-permute-start(f32[4,256]{1,0:T(4,128)S(1)} %pad_maximum_fusion.7), channel_id=1, source_target_pairs={{0,8},{4,12},{8,0},{12,4},{1,9},{5,13},{9,1},{13,5},{2,10},{6,14},... | collective-permute-start | bytes 12296 | tf_op jit(solution)/shard_map/ppermute | solution.py:27
  144.3 10.3 %collective-permute-start.21 = (bf16[594,256]{1,0:T(8,128)(2,1)S(1)}, bf16[594,256]{1,0:T(8,128)(2,1)S(1)}, u32[]{:S(2)}, u32[]{:S(2)}) collective-permute-start(bf16[594,256]{1,0:T(8,128)(2,1)S(1)} %get-tuple-element.80.grad1), channel_id=1, source_target_pairs={{0,16},{16,0},{1,17},{17,1},{2,18},{18,2},{3,19},{19,3},{4,20},{20... | collective-permute-start | bytes 912392 | tf_op jit(solution)/shard_map/ppermute | solution.py:39
  154.6 23.0 %all-to-all-start.1 = ((bf16[16,8,4096]{2,1,0:T(8,128)(2,1)}), bf16[16,8,4096]{2,1,0:T(8,128)(2,1)}, u32[]{:S(2)}, u32[]{:S(2)}) async-start(bf16[16,8,4096]{2,1,0:T(8,128)(2,1)} %bitcast.80), calls=%async_computation.1 | async-start | bytes 2097152 | tf_op jit(solution)/shard_map/all_to_all | solution.py:185
  (18 other events, 79.9 us)
Sparse Core Ops, SparseCore 0:
  10.4 44.0 all-gather.2
  56.3 39.5 all-gather.4

commit v4 on v2

v4 whole, which is shorter than its diff:
```python
import jax
import jax.numpy as jnp
from jax import lax
from jax.experimental import pallas as pl
from jax.experimental.pallas import tpu as pltpu
from jax.sharding import Mesh, PartitionSpec as P

LOSS_SCALE = 1024
KL_WEIGHT = 0.1
ENTROPY_WEIGHT = 0.05


def combine(parts):
    top = parts[0][0]
    for part in parts[1:]:
        top = jnp.maximum(top, part[0])
    scales = [jnp.exp(part[0] - top) for part in parts]
    total = sum(part[1] * scale for part, scale in zip(parts, scales))
    logit = sum(part[2] * scale for part, scale in zip(parts, scales))
    target = sum(part[3] for part in parts)
    return [top, total, logit, target]


def exchange(stats, axis):
    size = lax.axis_size(axis)
    others = [
        lax.ppermute(stats, axis, [(i, (i + step) % size) for i in range(size)])
        for step in range(1, size)
    ]
    return [stats] + others


def scatter_sum(parts, axis):
    got = lax.all_to_all(parts, axis, 0, 0, tiled=True)
    return jnp.sum(got.astype(jnp.float32), axis=0)


def swap(value, axis):
    return lax.ppermute(value, axis, [(0, 1), (1, 0)])


TILE = 512
PARAMS = pltpu.CompilerParams(vmem_limit_bytes=40 * 2**20)


def whole(*shape):
    return pl.BlockSpec(shape, lambda i: (0,) * len(shape))


def columns_of(step, straight, pieces, use):
    lead = pl.num_programs(0) // 2

    @pl.when(step < lead)
    def _():
        use([ref[...] for ref in straight])

    @pl.when(step >= lead)
    def _():
        use([jnp.concatenate([ref[j] for j in range(ref.shape[0])], axis=1) for ref in pieces])


def hidden_specs(tokens, depth, piece):
    lead = depth // TILE // 2
    return (
        pl.BlockSpec((tokens, TILE), lambda i: (0, jnp.minimum(i, lead - 1))),
        pl.BlockSpec((TILE // piece, tokens, piece), lambda i: (jnp.maximum(i - lead, 0), 0, 0)),
    )


def logits_kernel(first, target, straight, pieces, weight0, weight1, logits0, logits1, stats):
    step = pl.program_id(0)

    @pl.when(step == 0)
    def _():
        logits0[...] = jnp.zeros_like(logits0)
        logits1[...] = jnp.zeros_like(logits1)

    def use(tiles):
        for weight, logits in ((weight0, logits0), (weight1, logits1)):
            logits[...] += lax.dot_general(
                weight[...],
                tiles[0],
                (((1,), (1,)), ((), ())),
                preferred_element_type=jnp.float32,
            )

    columns_of(step, [straight], [pieces], use)

    @pl.when(step == pl.num_programs(0) - 1)
    def _():
        top = jnp.maximum(
            jnp.max(logits0[...], axis=0, keepdims=True),
            jnp.max(logits1[...], axis=0, keepdims=True),
        )
        stats[0:1, :] = top
        total, weighted, hit_sum = 0.0, 0.0, 0.0
        for k, logits in enumerate((logits0, logits1)):
            value = logits[...]
            shifted = jnp.exp(value - top)
            column = first[k] + lax.broadcasted_iota(jnp.int32, value.shape, 0)
            hit = jnp.where(column == target[...], value, 0.0)
            total += jnp.sum(shifted, axis=0, keepdims=True)
            weighted += jnp.sum(shifted * value, axis=0, keepdims=True)
            hit_sum += jnp.sum(hit, axis=0, keepdims=True)
        stats[1:2, :] = total
        stats[2:3, :] = weighted
        stats[3:4, :] = hit_sum


def logits_and_stats(first, target, straight, pieces, weights):
    width, depth = weights[0].shape
    tokens = straight.shape[0]
    return pl.pallas_call(
        logits_kernel,
        grid=(depth // TILE,),
        in_specs=[pl.BlockSpec(memory_space=pltpu.SMEM), whole(1, tokens)]
        + list(hidden_specs(tokens, depth, pieces.shape[2]))
        + [pl.BlockSpec((width, TILE), lambda i: (0, i))] * 2,
        out_specs=[whole(width, tokens)] * 2 + [whole(4, tokens)],
        out_shape=[jax.ShapeDtypeStruct((width, tokens), jnp.float32)] * 2
        + [jax.ShapeDtypeStruct((4, tokens), jnp.float32)],
        compiler_params=PARAMS,
        name="logits",
    )(first, target, straight, pieces, *weights)


def partial_kernel(
    first, target, order, info, part0, part1, part2, part3, logits0, logits1, weight0, weight1,
    out, grad0, grad1, held0, held1,
):
    @pl.when(pl.program_id(0) == 0)
    def _():
        parts = [[ref[i : i + 1, :] for i in range(4)] for ref in (part0, part1, part2, part3)]
        row_max, exp_total, exp_logit, target_logit = combine(parts)
        adv, weight, ref_logp = [info[i : i + 1, :] for i in range(3)]
        log_total = row_max + jnp.log(exp_total)
        target_logp = target_logit - log_total
        mean_logit = exp_logit / exp_total
        logp_grad = -adv + KL_WEIGHT * (target_logp - ref_logp)
        sets = ((logits0, grad0, held0), (logits1, grad1, held1))
        for k, (logits, grad, held) in enumerate(sets):
            value = logits[...]
            column = first[k] + lax.broadcasted_iota(jnp.int32, value.shape, 0)
            hit = jnp.where(column == target[...], 1.0, 0.0)
            probs = jnp.exp(value - log_total)
            inner = logp_grad * (hit - probs)
            inner = inner + ENTROPY_WEIGHT * probs * (value - mean_logit)
            result = (weight * inner).astype(jnp.bfloat16)
            grad[...] = result
            held[...] = lax.dot_general(
                order[...], result, (((1,), (1,)), ((), ())), preferred_element_type=jnp.float32
            ).astype(jnp.bfloat16)

    out[...] = (
        jnp.dot(held0[...], weight0[...], preferred_element_type=jnp.float32)
        + jnp.dot(held1[...], weight1[...], preferred_element_type=jnp.float32)
    ).astype(jnp.bfloat16)


def gradient_partial(first, target, order, info, parts, logits, weights):
    width, depth = weights[0].shape
    rows, tokens = order.shape
    return pl.pallas_call(
        partial_kernel,
        grid=(depth // TILE,),
        in_specs=[pl.BlockSpec(memory_space=pltpu.SMEM), whole(1, tokens), whole(rows, tokens)]
        + [whole(4, tokens)] * 5
        + [whole(width, tokens)] * 2
        + [pl.BlockSpec((width, TILE), lambda i: (0, i))] * 2,
        out_specs=[pl.BlockSpec((rows, TILE), lambda i: (0, i))] + [whole(width, tokens)] * 2,
        out_shape=[jax.ShapeDtypeStruct((rows, depth), jnp.bfloat16)]
        + [jax.ShapeDtypeStruct((width, tokens), jnp.bfloat16)] * 2,
        scratch_shapes=[pltpu.VMEM((rows, width), jnp.bfloat16)] * 2,
        compiler_params=PARAMS,
        name="grad_hidden_partial",
    )(first, target, order, info, *parts, *logits, *weights)


def head_kernel(grad0, grad1, straight0, pieces0, straight1, pieces1, out):
    def use(tiles):
        out[...] = (
            jnp.dot(grad0[...], tiles[0], preferred_element_type=jnp.float32)
            + jnp.dot(grad1[...], tiles[1], preferred_element_type=jnp.float32)
        ).astype(jnp.bfloat16)

    columns_of(pl.program_id(0), [straight0, straight1], [pieces0, pieces1], use)


def head_gradient(grads, hiddens):
    width, tokens = grads[0].shape
    depth = 2 * hiddens[0][0].shape[1]
    return pl.pallas_call(
        head_kernel,
        grid=(depth // TILE,),
        in_specs=[whole(width, tokens)] * 2
        + list(hidden_specs(tokens, depth, hiddens[0][1].shape[2])) * 2,
        out_specs=pl.BlockSpec((width, TILE), lambda i: (0, i)),
        out_shape=jax.ShapeDtypeStruct((width, depth), jnp.bfloat16),
        compiler_params=PARAMS,
        cost_estimate=pl.CostEstimate(
            flops=4 * tokens * width * depth,
            bytes_accessed=2 * depth * (width + 2 * tokens),
            transcendentals=0,
        ),
        name="grad_head",
    )(*grads, *hiddens[0], *hiddens[1])


def per_device(
    hidden, head_weight, targets, segment_ids, lengths, loss_mask, advantages, ref_logprobs
):
    bf16, f32 = jnp.bfloat16, jnp.float32
    depth, width = head_weight.shape
    ndp, nz, ncore = lax.axis_size("dp"), lax.axis_size("z"), lax.axis_size("core")
    nv = lax.axis_size("x") * lax.axis_size("y")
    block = hidden.shape[0]
    rows = block // nv
    dp, z, core = lax.axis_index("dp"), lax.axis_index("z"), lax.axis_index("core")
    place = lax.axis_index(("x", "y"))
    half, piece = depth // 2, depth // 2 // nv

    straight = lax.all_gather(hidden[:, :half], ("dp", "z"), axis=0, tiled=True)
    share = lax.dynamic_slice_in_dim(hidden, half + place * piece, piece, 1)
    share = lax.all_gather(share, ("dp", "z"), axis=0, tiled=True)
    pieces = lax.all_to_all(
        jnp.broadcast_to(share[None], (nv,) + share.shape), ("x", "y"), 0, 0, tiled=True
    )
    weights = [head_weight.T, swap(head_weight.T, "core")]
    first = jnp.stack([((z * ncore + c) * nv + place) * width for c in (core, 1 - core)])

    seq_onehot = segment_ids[:, None] == lax.iota(jnp.int32, advantages.shape[0])[None, :]
    token_adv = jnp.sum(jnp.where(seq_onehot, advantages[None, :], 0.0), axis=1)
    token_len = jnp.sum(jnp.where(seq_onehot, lengths[None, :].astype(f32), 0.0), axis=1)
    token_weight = LOSS_SCALE * loss_mask.astype(f32) / token_len
    own = jnp.stack([token_adv, token_weight, ref_logprobs, targets.astype(f32)])
    own = own.reshape(4, nz, ncore, block)
    own = jnp.where(core == 0, own[:, :, 0], own[:, :, 1]).reshape(4, nz * block)
    other = swap(own, "dp")
    info = jnp.concatenate(
        [jnp.where(dp == 0, own, other), jnp.where(dp == 0, other, own)], axis=1
    )
    target = info[3:4].astype(jnp.int32)

    tokens, mine = ndp * nz * block, nz * block
    row = lax.iota(jnp.int32, mine)
    source = ((dp * nz + row // rows % nz) * nv + row // (rows * nz)) * rows + row % rows
    order = (source[:, None] == lax.iota(jnp.int32, tokens)[None, :]).astype(bf16)

    *logits, stats = logits_and_stats(first, target, straight, pieces, weights)
    for axis in ("y", "x"):
        stats = jnp.stack(combine(exchange(stats, axis)))
    parts = exchange(stats, "z")
    partial, grad_own, grad_other = gradient_partial(
        first, target, order, info, parts, logits, weights
    )
    got = lax.all_to_all(partial.reshape(nv, nz * rows, depth), ("x", "y"), 0, 0, tiled=True)
    grad_head = head_gradient(
        (grad_own, swap(grad_other, "core")),
        ((straight, pieces), (swap(straight, "core"), swap(pieces, "core"))),
    )
    got, grad_head = lax.optimization_barrier((got, grad_head))
    got = jnp.sum(got.astype(f32), axis=0).astype(bf16)
    grad_hidden = scatter_sum(got.reshape(nz, rows, depth), "z").astype(bf16)
    return grad_hidden, grad_head.T


def solution(mesh):
    devices = mesh.devices.reshape(2, 4, 2, 4, 4)
    fine = Mesh(devices, ("dp", "z", "core", "x", "y"))
    ctx, vocab = ("z", "core"), ("x", "y")
    return jax.shard_map(
        per_device,
        mesh=fine,
        in_specs=(
            P(("dp",) + ctx, None),
            P(None, ctx + vocab),
            P("dp"),
            P("dp"),
            P(),
            P("dp"),
            P(),
            P("dp"),
        ),
        out_specs=(P(("dp",) + ctx + vocab, None), P(None, ctx + vocab)),
        check_vma=False,
    )
```

time: 182 us -> 166 us (0.912)
  waiting for transfers between devices: 86.3 us -> 38 us
  blocking collectives: 0 us -> 39.3 us
  matrix products: 38.5 us -> 0 us
  Pallas kernels: 0 us -> 30 us
  local copies, waits for them, and re-layouts: 3.51 us -> 8.34 us
  other arithmetic: 6.6 us -> 3.08 us
    all_gather x1, waiting for transfers between devices: 46.8 us -> 0.01 us  [per_device(): straight = lax.all_gather(hidden[:, :half], ('dp', 'z'), axis=0, tiled=True)]
    dot_general x6 -> x0, matrix products: 38.5 us -> none  [the longest x2 17.7 us: per_device(): lax.dot_general(h, g, (((0,), (0,)), ((), ())), preferred_element_type=f32)]
    pallas_call x0 -> x3, Pallas kernels: none -> 30 us  [the longest x1 10.5 us: logits_and_stats(): pl.pallas_call(logits_kernel, grid=(depth // TILE,), in_specs=[pl.BlockSp...]
    all_gather x0 -> x1, blocking collectives: none -> 28.4 us  [per_device(): share = lax.all_gather(share, ('dp', 'z'), axis=0, tiled=True)]
    all_to_all x0 -> x1, blocking collectives: none -> 10.9 us  [scatter_sum(): got = lax.all_to_all(parts, axis, 0, 0, tiled=True)]
    ppermute x4 -> x5, waiting for transfers between devices: 1.59 us -> 5.99 us  [swap(): return lax.ppermute(value, axis, [(0, 1), (1, 0)])]
    all_to_all x2, starting transfers between devices: 9.41 us -> 13.7 us  [the longest x1 7.63 us: per_device(): lax.all_to_all(jnp.broadcast_to(share[None], (nv,) + share.shape), ('x',...]
    ppermute x9, waiting for transfers between devices: 10.5 us -> 6.67 us  [exchange(): lax.ppermute(stats, axis, [(i, (i + step) % size) for i in range(size)])]
  transfers between devices with their start and end apart: 16 -> 17, of which waited for: 10 -> 11; matrix products, arithmetic and copies ran while one was open for 18% -> 3% of each run, Pallas kernels for 0% -> 12%
where the time goes in v4:
time: 166 us; the launch traced here: 164 us
  blocking collectives  39.3 us (24%)
  waiting for transfers between devices  38 us (23%)
  starting transfers between devices  31.5 us (19%)
  Pallas kernels  30 us (18%)
  between operations  14.2 us (9%)
  local copies, waits for them, and re-layouts  8.34 us (5%)
  other arithmetic  3.08 us (2%)
    all_gather x1, blocking collectives, per_device(): share = lax.all_gather(share, ('dp', 'z'), axis=0, tiled=True)  28.4 us
    all_to_all x1, waiting for transfers between devices, per_device(): lax.all_to_all(jnp.broadcast_to(share[None], (nv,) + share.shape), ('x',...  14 us
    ppermute x9, starting transfers between devices, exchange(): lax.ppermute(stats, axis, [(i, (i + step) % size) for i in range(size)])  13.6 us
    all_to_all x1, waiting for transfers between devices, per_device(): lax.all_to_all(partial.reshape(nv, nz * rows, depth), ('x', 'y'), 0, 0, t...  11.3 us
    all_to_all x1, blocking collectives, scatter_sum(): got = lax.all_to_all(parts, axis, 0, 0, tiled=True)  10.9 us
    pallas_call x1, Pallas kernels, logits_and_stats(): pl.pallas_call(logits_kernel, grid=(depth // TILE,), in_specs=[pl.BlockSp...  10.5 us
    pallas_call x1, Pallas kernels, head_gradient(): pl.pallas_call(head_kernel, grid=(depth // TILE,), in_specs=[whole(width,...  10.4 us
    pallas_call x1, Pallas kernels, gradient_partial(): pl.pallas_call(partial_kernel, grid=(depth // TILE,), in_specs=[pl.BlockS...  9.09 us
  transfers between devices with their start and end apart: 17, of which 11 were waited for; matrix products, arithmetic and copies ran while one was open for 3% of the time, Pallas kernels for 12%

profile of v4, /device:TPU:2, one launch (start us, length us, event | category | flops | bytes accessed | tf_op | source)
XLA Modules:
  0.0 164.5 jit_solution(14608116771649310417)
XLA Ops:
  7.3 1.7 %slice.106 = bf16[64,2048]{1,0:T(8,128)(2,1)} slice(bf16[64,4096]{1,0:T(8,128)(2,1)} %param.8), slice={[0:64], [0:2048]} | slice | bytes 524288 | tf_op jit(solution)/shard_map/slice | solution.py:222
  9.7 28.4 %all_gather.7 = bf16[512,128]{1,0:T(8,128)(2,1)S(1)} all-gather(bf16[64,128]{1,0:T(8,128)(2,1)S(1)} %constant_dynamic-slice_fusion), channel_id=1, replica_groups=mesh['dp'=2,'z'=4,'core'=2,'x'=4,'y'=4] {'dp','z'}, dimensions={0}, use_global_device_ids=true | all-gather | bytes 147456 | tf_op jit(solution)/shard_map/all_gather | solution.py:224
  38.1 1.7 %broadcast_in_dim.33 = bf16[16,512,128]{2,1,0:T(8,128)(2,1)} broadcast(bf16[512,128]{1,0:T(8,128)(2,1)S(1)} %all_gather.7), dimensions={1,2} | broadcast | bytes 2228224 | tf_op jit(solution)/shard_map/broadcast_in_dim | solution.py:226
  39.9 7.6 %all-to-all-start = ((bf16[16,512,128]{2,1,0:T(8,128)(2,1)}), bf16[16,512,128]{2,1,0:T(8,128)(2,1)S(1)}, u32[]{:S(2)}, u32[]{:S(2)}) async-start(bf16[16,512,128]{2,1,0:T(8,128)(2,1)} %broadcast_in_dim.33), calls=%async_computation | async-start | bytes 4194304 | tf_op jit(solution)/shard_map/all_to_all | solution.py:225
  48.1 3.5 %collective-permute-start = (f32[4,256]{1,0:T(4,128)S(1)}, f32[4,256]{1,0:T(4,128)S(1)}, u32[]{:S(2)}, u32[]{:S(2)}) collective-permute-start(f32[4,256]{1,0:T(4,128)S(1)} %select_n.74), channel_id=1, source_target_pairs={{0,128},{128,0},{1,129},{129,1},{2,130},{130,2},{3,131},{131,3},{4... | collective-permute-start | bytes 12296 | tf_op jit(solution)/shard_map/ppermute | solution.py:39
  51.7 4.0 %collective-permute-done = f32[4,256]{1,0:T(4,128)S(1)} collective-permute-done((f32[4,256]{1,0:T(4,128)S(1)}, f32[4,256]{1,0:T(4,128)S(1)}, u32[]{:S(2)}, u32[]{:S(2)}) %collective-permute-start) | collective-permute-done | bytes 4128 | tf_op jit(solution)/shard_map/ppermute | solution.py:39
  55.7 14.0 %all-to-all-done.pieces.pieces0 = bf16[16,512,128]{2,1,0:T(8,128)(2,1)S(1)} async-done(((bf16[16,512,128]{2,1,0:T(8,128)(2,1)}), bf16[16,512,128]{2,1,0:T(8,128)(2,1)S(1)}, u32[]{:S(2)}, u32[]{:S(2)}) %all-to-all-start) | async-done | bytes 2097184 | tf_op jit(solution)/shard_map/all_to_all | solution.py:225
  69.7 2.4 %copy-done = bf16[4096,594]{0,1:T(8,128)(2,1)S(1)} copy-done((bf16[4096,594]{0,1:T(8,128)(2,1)S(1)}, bf16[4096,594]{0,1:T(8,128)(2,1)}, u32[]{:S(2)}) %copy-start) | copy-done | bytes 4866072
  72.1 10.5 %logits.1 = (f32[594,512]{1,0:T(8,128)S(1)}, f32[594,512]{1,0:T(8,128)S(1)}, f32[4,512]{1,0:T(4,128)S(1)}) custom-call(s32[2]{0:T(128)S(1)} %pad_add_fusion.first, s32[1,512]{1,0:T(1,128)S(1)} %fusion.15.target, bf16[512,2048]{1,0:T(8,128)(2,1)} %all-gather.2.cloned.1.call-done.straight.straight0, bf16[16,512,128]{2,1,0:T(8,128)(2,1)S(1)} %all-to-all-done.pieces.pieces0, ...), custom_call_target="tpu_custom_call" | custom-call | tf_op jit(solution)/shard_map/logits/pallas_call | solution.py:113
  82.7 1.5 collective-permute-start.4
  86.4 2.9 %collective-permute-done.3 = f32[4,512]{1,0:T(4,128)S(1)} collective-permute-done((f32[4,512]{1,0:T(4,128)S(1)}, f32[4,512]{1,0:T(4,128)S(1)}, u32[]{:S(2)}, u32[]{:S(2)}) %collective-permute-start.3) | collective-permute-done | bytes 8224 | tf_op jit(solution)/shard_map/ppermute | solution.py:27
  91.2 1.9 %collective-permute-start.6 = (f32[4,512]{1,0:T(4,128)S(1)}, f32[4,512]{1,0:T(4,128)S(1)}, u32[]{:S(2)}, u32[]{:S(2)}) collective-permute-start(f32[4,512]{1,0:T(4,128)S(1)} %pad_maximum_fusion.1), channel_id=1, source_target_pairs={{0,8},{4,12},{8,0},{12,4},{1,9},{5,13},{9,1},{13,5},{2,10},{6,14},... | collective-permute-start | bytes 24584 | tf_op jit(solution)/shard_map/ppermute | solution.py:27
  93.0 2.1 %collective-permute-start.5 = (f32[4,512]{1,0:T(4,128)S(1)}, f32[4,512]{1,0:T(4,128)S(1)}, u32[]{:S(2)}, u32[]{:S(2)}) collective-permute-start(f32[4,512]{1,0:T(4,128)S(1)} %pad_maximum_fusion.1), channel_id=1, source_target_pairs={{0,4},{4,8},{8,12},{12,0},{1,5},{5,9},{9,13},{13,1},{2,6},{6,10},{... | collective-permute-start | bytes 24584 | tf_op jit(solution)/shard_map/ppermute | solution.py:27
  96.8 2.0 %collective-permute-start.8 = (f32[4,512]{1,0:T(4,128)S(1)}, f32[4,512]{1,0:T(4,128)S(1)}, u32[]{:S(2)}, u32[]{:S(2)}) collective-permute-start(f32[4,512]{1,0:T(4,128)S(1)} %pad_maximum_fusion.2.part0), channel_id=1, source_target_pairs={{0,32},{32,64},{64,96},{96,0},{1,33},{33,65},{65,97},{97,1},{2,34}... | collective-permute-start | bytes 24584 | tf_op jit(solution)/shard_map/ppermute | solution.py:27
  98.8 1.3 collective-permute-start.9
  100.1 2.3 %collective-permute-start.10 = (f32[4,512]{1,0:T(4,128)S(1)}, f32[4,512]{1,0:T(4,128)S(1)}, u32[]{:S(2)}, u32[]{:S(2)}) collective-permute-start(f32[4,512]{1,0:T(4,128)S(1)} %pad_maximum_fusion.2.part0), channel_id=1, source_target_pairs={{0,96},{32,0},{64,32},{96,64},{1,97},{33,1},{65,33},{97,65},{2,98}... | collective-permute-start | bytes 24584 | tf_op jit(solution)/shard_map/ppermute | solution.py:27
  103.8 9.1 %grad_hidden_partial.1 = (bf16[256,4096]{1,0:T(8,128)(2,1)S(1)}, bf16[594,512]{1,0:T(8,128)(2,1)S(1)}, bf16[594,512]{1,0:T(8,128)(2,1)S(1)}) custom-call(s32[2]{0:T(128)S(1)} %pad_add_fusion.first, s32[1,512]{1,0:T(1,128)S(1)} %fusion.15.target, bf16[256,512]{1,0:T(8,128)(2,1)S(1)} %fusion.order, f32[4,512]{1,0:T(4,128)S(1)} %pad_maximum_fusion.info, ...), custom_call_target="tpu_custom_call" | custom-call | tf_op jit(solution)/shard_map/grad_hidden_partial/pallas_call | solution.py:163
  112.9 1.3 copy-done.1
  114.2 6.1 %all-to-all-start.1 = ((bf16[16,16,4096]{2,1,0:T(8,128)(2,1)}), bf16[16,16,4096]{2,1,0:T(8,128)(2,1)}, u32[]{:S(2)}, u32[]{:S(2)}) async-start(bf16[16,16,4096]{2,1,0:T(8,128)(2,1)} %bitcast.8), calls=%async_computation.1 | async-start | bytes 4194304 | tf_op jit(solution)/shard_map/all_to_all | solution.py:256
  120.3 2.0 %collective-permute-done.11.grad1 = bf16[594,512]{1,0:T(8,128)(2,1)S(1)} collective-permute-done((bf16[594,512]{1,0:T(8,128)(2,1)S(1)}, bf16[594,512]{1,0:T(8,128)(2,1)S(1)}, u32[]{:S(2)}, u32[]{:S(2)}) %collective-permute-start.11) | collective-permute-done | bytes 608288 | tf_op jit(solution)/shard_map/ppermute | solution.py:39
  122.3 10.4 %grad_head.1 = bf16[594,4096]{1,0:T(8,128)(2,1)} custom-call(bf16[594,512]{1,0:T(8,128)(2,1)S(1)} %get-tuple-element.14.grad0, bf16[594,512]{1,0:T(8,128)(2,1)S(1)} %collective-permute-done.11.grad1, bf16[512,2048]{1,0:T(8,128)(2,1)} %all-gather.2.cloned.1.call-done.straight.straight0, bf16[16,512,128]{2,1,0:T(8,128)(2,1)S(1)} %all-to-all-done.pieces.pieces0, ...), custom_call_target="tpu_custom_call" | custom-call | flops 4982833152 | bytes 13254656 | tf_op jit(solution)/shard_map/grad_head/pallas_call | solution.py:192
  132.7 11.3 %all-to-all-done.1 = bf16[16,16,4096]{2,1,0:T(8,128)(2,1)} async-done(((bf16[16,16,4096]{2,1,0:T(8,128)(2,1)}), bf16[16,16,4096]{2,1,0:T(8,128)(2,1)}, u32[]{:S(2)}, u32[]{:S(2)}) %all-to-all-start.1) | async-done | bytes 2097184 | tf_op jit(solution)/shard_map/all_to_all | solution.py:256
  144.0 1.9 %reduce_sum.44 = bf16[16,4096]{1,0:T(8,128)(2,1)S(1)} reduce(bf16[16,16,4096]{2,1,0:T(8,128)(2,1)} %all-to-all-done.1, bf16[]{:T(256)} %constant.90.clone.1), dimensions={0}, to_apply=%region_2.3 | reduce | flops 983040 | bytes 2228226 | tf_op jit(solution)/shard_map/reduce_sum | solution.py:262
  146.0 10.9 %all_to_all.15 = bf16[4,4,4096]{2,1,0:T(4,128)(2,1)S(1)} all-to-all(bf16[4,4,4096]{2,1,0:T(4,128)(2,1)S(1)} %reshape.74), channel_id=1, replica_groups=mesh['dp'=2,'z'=4,'core'=2,'x'=4,'y'=4] {'z'}, dimensions={0} | all-to-all | bytes 262144 | tf_op jit(solution)/shard_map/all_to_all | solution.py:34
  (64 shorter events, 9.4 us)
Async XLA Ops:
  7.2 62.5 %all-gather.2.cloned.1.call-start = ((), (), s32[]{:S(2)}) async-start(), calls=%async_computation.3 | async-start | bytes 2359296 | tf_op jit(solution)/shard_map/all_gather | solution.py:222
  7.2 62.5 %collective-permute-start.1 = (bf16[594,4096]{1,0:T(8,128)(2,1)}, bf16[594,4096]{1,0:T(8,128)(2,1)}, u32[]{:S(2)}, u32[]{:S(2)}) collective-permute-start(bf16[594,4096]{1,0:T(8,128)(2,1)} %bitcast.5), channel_id=1, source_target_pairs={{0,16},{16,0},{1,17},{17,1},{2,18},{18,2},{3,19},{19,3},{4,20},{20... | collective-permute-start | bytes 14598152 | tf_op jit(solution)/shard_map/ppermute | solution.py:39
  39.8 7.7 %copy-start.7 = (s32[64]{0:T(128)S(1)}, s32[64]{0:T(128)}, u32[]{:S(2)}) copy-start(s32[64]{0:T(128)} %param.12) | copy-start | bytes 772
  39.8 7.7 %copy-start.2 = (s32[512]{0:T(512)S(1)}, s32[512]{0:T(512)}, u32[]{:S(2)}) copy-start(s32[512]{0:T(512)} %param.11) | copy-start | bytes 6148
  39.8 7.7 %copy-start.6 = (f32[64]{0:T(128)S(1)}, f32[64]{0:T(128)}, u32[]{:S(2)}) copy-start(f32[64]{0:T(128)} %param.14) | copy-start | bytes 772
  39.8 7.9 %copy-start.3 = (s32[512]{0:T(512)S(1)}, s32[512]{0:T(512)}, u32[]{:S(2)}) copy-start(s32[512]{0:T(512)} %param.13) | copy-start | bytes 6148
  39.8 8.0 %copy-start.4 = (f32[512]{0:T(512)S(1)}, f32[512]{0:T(512)}, u32[]{:S(2)}) copy-start(f32[512]{0:T(512)} %param.15) | copy-start | bytes 6148
  39.8 8.0 %copy-start.5 = (s32[512]{0:T(512)S(1)}, s32[512]{0:T(512)}, u32[]{:S(2)}) copy-start(s32[512]{0:T(512)} %param.10) | copy-start | bytes 6148
  39.9 29.8 %all-to-all-start = ((bf16[16,512,128]{2,1,0:T(8,128)(2,1)}), bf16[16,512,128]{2,1,0:T(8,128)(2,1)S(1)}, u32[]{:S(2)}, u32[]{:S(2)}) async-start(bf16[16,512,128]{2,1,0:T(8,128)(2,1)} %broadcast_in_dim.33), calls=%async_computation | async-start | bytes 4194304 | tf_op jit(solution)/shard_map/all_to_all | solution.py:225
  48.1 7.5 %collective-permute-start = (f32[4,256]{1,0:T(4,128)S(1)}, f32[4,256]{1,0:T(4,128)S(1)}, u32[]{:S(2)}, u32[]{:S(2)}) collective-permute-start(f32[4,256]{1,0:T(4,128)S(1)} %select_n.74), channel_id=1, source_target_pairs={{0,128},{128,0},{1,129},{129,1},{2,130},{130,2},{3,131},{131,3},{4... | collective-permute-start | bytes 12296 | tf_op jit(solution)/shard_map/ppermute | solution.py:39
  69.7 2.4 %copy-start = (bf16[4096,594]{0,1:T(8,128)(2,1)S(1)}, bf16[4096,594]{0,1:T(8,128)(2,1)}, u32[]{:S(2)}) copy-start(bf16[4096,594]{0,1:T(8,128)(2,1)} %param.9) | copy-start | bytes 14598148
  82.7 3.7 %collective-permute-start.4 = (f32[4,512]{1,0:T(4,128)S(1)}, f32[4,512]{1,0:T(4,128)S(1)}, u32[]{:S(2)}, u32[]{:S(2)}) collective-permute-start(f32[4,512]{1,0:T(4,128)S(1)} %get-tuple-element.10), channel_id=1, source_target_pairs={{0,3},{1,0},{2,1},{3,2},{4,7},{5,4},{6,5},{7,6},{8,11},{9,8},{10,9... | collective-permute-start | bytes 24584 | tf_op jit(solution)/shard_map/ppermute | solution.py:27
  84.1 5.2 %collective-permute-start.3 = (f32[4,512]{1,0:T(4,128)S(1)}, f32[4,512]{1,0:T(4,128)S(1)}, u32[]{:S(2)}, u32[]{:S(2)}) collective-permute-start(f32[4,512]{1,0:T(4,128)S(1)} %get-tuple-element.10), channel_id=1, source_target_pairs={{0,2},{1,3},{2,0},{3,1},{4,6},{5,7},{6,4},{7,5},{8,10},{9,11},{10,... | collective-permute-start | bytes 24584 | tf_op jit(solution)/shard_map/ppermute | solution.py:27
  85.3 4.9 %collective-permute-start.2 = (f32[4,512]{1,0:T(4,128)S(1)}, f32[4,512]{1,0:T(4,128)S(1)}, u32[]{:S(2)}, u32[]{:S(2)}) collective-permute-start(f32[4,512]{1,0:T(4,128)S(1)} %get-tuple-element.10), channel_id=1, source_target_pairs={{0,1},{1,2},{2,3},{3,0},{4,5},{5,6},{6,7},{7,4},{8,9},{9,10},{10,1... | collective-permute-start | bytes 24584 | tf_op jit(solution)/shard_map/ppermute | solution.py:27
  90.2 5.6 %collective-permute-start.7 = (f32[4,512]{1,0:T(4,128)S(1)}, f32[4,512]{1,0:T(4,128)S(1)}, u32[]{:S(2)}, u32[]{:S(2)}) collective-permute-start(f32[4,512]{1,0:T(4,128)S(1)} %pad_maximum_fusion.1), channel_id=1, source_target_pairs={{0,12},{4,0},{8,4},{12,8},{1,13},{5,1},{9,5},{13,9},{2,14},{6,2},{... | collective-permute-start | bytes 24584 | tf_op jit(solution)/shard_map/ppermute | solution.py:27
  91.2 5.2 %collective-permute-start.6 = (f32[4,512]{1,0:T(4,128)S(1)}, f32[4,512]{1,0:T(4,128)S(1)}, u32[]{:S(2)}, u32[]{:S(2)}) collective-permute-start(f32[4,512]{1,0:T(4,128)S(1)} %pad_maximum_fusion.1), channel_id=1, source_target_pairs={{0,8},{4,12},{8,0},{12,4},{1,9},{5,13},{9,1},{13,5},{2,10},{6,14},... | collective-permute-start | bytes 24584 | tf_op jit(solution)/shard_map/ppermute | solution.py:27
  93.0 3.7 %collective-permute-start.5 = (f32[4,512]{1,0:T(4,128)S(1)}, f32[4,512]{1,0:T(4,128)S(1)}, u32[]{:S(2)}, u32[]{:S(2)}) collective-permute-start(f32[4,512]{1,0:T(4,128)S(1)} %pad_maximum_fusion.1), channel_id=1, source_target_pairs={{0,4},{4,8},{8,12},{12,0},{1,5},{5,9},{9,13},{13,1},{2,6},{6,10},{... | collective-permute-start | bytes 24584 | tf_op jit(solution)/shard_map/ppermute | solution.py:27
  95.2 25.1 %collective-permute-start.13 = (bf16[16,512,128]{2,1,0:T(8,128)(2,1)S(1)}, bf16[16,512,128]{2,1,0:T(8,128)(2,1)}, u32[]{:S(2)}, u32[]{:S(2)}) collective-permute-start(bf16[16,512,128]{2,1,0:T(8,128)(2,1)S(1)} %all-to-all-done.pieces.pieces0), channel_id=1, source_target_pairs={{0,16},{16,0},{1,17},{17,1},{2,18},{18,2},{3,19},{19,3},{4,20},{20... | collective-permute-start | bytes 6291464 | tf_op jit(solution)/shard_map/ppermute | solution.py:39
  95.3 27.0 %collective-permute-start.12 = (bf16[512,2048]{1,0:T(8,128)(2,1)}, bf16[512,2048]{1,0:T(8,128)(2,1)}, u32[]{:S(2)}, u32[]{:S(2)}) collective-permute-start(bf16[512,2048]{1,0:T(8,128)(2,1)} %all-gather.2.cloned.1.call-done.straight.straight0), channel_id=1, source_target_pairs={{0,16},{16,0},{1,17},{17,1},{2,18},{18,2},{3,19},{19,3},{4,20},{20... | collective-permute-start | bytes 6291464 | tf_op jit(solution)/shard_map/ppermute | solution.py:39
  96.8 5.7 %collective-permute-start.8 = (f32[4,512]{1,0:T(4,128)S(1)}, f32[4,512]{1,0:T(4,128)S(1)}, u32[]{:S(2)}, u32[]{:S(2)}) collective-permute-start(f32[4,512]{1,0:T(4,128)S(1)} %pad_maximum_fusion.2.part0), channel_id=1, source_target_pairs={{0,32},{32,64},{64,96},{96,0},{1,33},{33,65},{65,97},{97,1},{2,34}... | collective-permute-start | bytes 24584 | tf_op jit(solution)/shard_map/ppermute | solution.py:27
  98.8 4.5 %collective-permute-start.9 = (f32[4,512]{1,0:T(4,128)S(1)}, f32[4,512]{1,0:T(4,128)S(1)}, u32[]{:S(2)}, u32[]{:S(2)}) collective-permute-start(f32[4,512]{1,0:T(4,128)S(1)} %pad_maximum_fusion.2.part0), channel_id=1, source_target_pairs={{0,64},{32,96},{64,0},{96,32},{1,65},{33,97},{65,1},{97,33},{2,66}... | collective-permute-start | bytes 24584 | tf_op jit(solution)/shard_map/ppermute | solution.py:27
  100.1 3.7 %collective-permute-start.10 = (f32[4,512]{1,0:T(4,128)S(1)}, f32[4,512]{1,0:T(4,128)S(1)}, u32[]{:S(2)}, u32[]{:S(2)}) collective-permute-start(f32[4,512]{1,0:T(4,128)S(1)} %pad_maximum_fusion.2.part0), channel_id=1, source_target_pairs={{0,96},{32,0},{64,32},{96,64},{1,97},{33,1},{65,33},{97,65},{2,98}... | collective-permute-start | bytes 24584 | tf_op jit(solution)/shard_map/ppermute | solution.py:27
  114.2 29.8 %all-to-all-start.1 = ((bf16[16,16,4096]{2,1,0:T(8,128)(2,1)}), bf16[16,16,4096]{2,1,0:T(8,128)(2,1)}, u32[]{:S(2)}, u32[]{:S(2)}) async-start(bf16[16,16,4096]{2,1,0:T(8,128)(2,1)} %bitcast.8), calls=%async_computation.1 | async-start | bytes 4194304 | tf_op jit(solution)/shard_map/all_to_all | solution.py:256
  120.3 2.0 %collective-permute-start.11 = (bf16[594,512]{1,0:T(8,128)(2,1)S(1)}, bf16[594,512]{1,0:T(8,128)(2,1)S(1)}, u32[]{:S(2)}, u32[]{:S(2)}) collective-permute-start(bf16[594,512]{1,0:T(8,128)(2,1)S(1)} %get-tuple-element.15), channel_id=1, source_target_pairs={{0,16},{16,0},{1,17},{17,1},{2,18},{18,2},{3,19},{19,3},{4,20},{20... | collective-permute-start | bytes 1824776 | tf_op jit(solution)/shard_map/ppermute | solution.py:39
  (1 other events, 1.3 us)
Sparse Core Ops, SparseCore 0:
  9.8 44.5 all-gather.1

commit v5 on v4

--- a/solution.py
+++ b/solution.py
@@ -35,12 +35,18 @@
     return jnp.sum(got.astype(jnp.float32), axis=0)
 
 
+def spread(value, axis):
+    count = lax.axis_size(axis)
+    copies = jnp.broadcast_to(value[None], (count,) + value.shape)
+    return lax.all_to_all(copies, axis, 0, 0, tiled=True)
+
+
 def swap(value, axis):
     return lax.ppermute(value, axis, [(0, 1), (1, 0)])
 
 
-TILE = 512
-PARAMS = pltpu.CompilerParams(vmem_limit_bytes=40 * 2**20)
+TILE = 1024
+PARAMS = pltpu.CompilerParams(vmem_limit_bytes=24 * 2**20)
 
 
 def whole(*shape):
@@ -124,14 +130,16 @@
     )(first, target, straight, pieces, *weights)
 
 
-def partial_kernel(
-    first, target, order, info, part0, part1, part2, part3, logits0, logits1, weight0, weight1,
+def gradient_kernel(
+    first, target, order, info, parts, logits0, logits1, weight0, weight1,
     out, grad0, grad1, held0, held1,
 ):
     @pl.when(pl.program_id(0) == 0)
     def _():
-        parts = [[ref[i : i + 1, :] for i in range(4)] for ref in (part0, part1, part2, part3)]
-        row_max, exp_total, exp_logit, target_logit = combine(parts)
+        count = parts.shape[0]
+        row_max, exp_total, exp_logit, target_logit = combine(
+            [[parts[j, i : i + 1, :] for i in range(4)] for j in range(count)]
+        )
         adv, weight, ref_logp = [info[i : i + 1, :] for i in range(3)]
         log_total = row_max + jnp.log(exp_total)
         target_logp = target_logit - log_total
@@ -161,19 +169,19 @@
     width, depth = weights[0].shape
     rows, tokens = order.shape
     return pl.pallas_call(
-        partial_kernel,
+        gradient_kernel,
         grid=(depth // TILE,),
         in_specs=[pl.BlockSpec(memory_space=pltpu.SMEM), whole(1, tokens), whole(rows, tokens)]
-        + [whole(4, tokens)] * 5
+        + [whole(4, tokens), whole(*parts.shape)]
         + [whole(width, tokens)] * 2
         + [pl.BlockSpec((width, TILE), lambda i: (0, i))] * 2,
         out_specs=[pl.BlockSpec((rows, TILE), lambda i: (0, i))] + [whole(width, tokens)] * 2,
-        out_shape=[jax.ShapeDtypeStruct((rows, depth), jnp.bfloat16)]
-        + [jax.ShapeDtypeStruct((width, tokens), jnp.bfloat16)] * 2,
+        out_shape=[pltpu.HBM((rows, depth), jnp.bfloat16)]
+        + [pltpu.HBM((width, tokens), jnp.bfloat16)] * 2,
         scratch_shapes=[pltpu.VMEM((rows, width), jnp.bfloat16)] * 2,
         compiler_params=PARAMS,
         name="grad_hidden_partial",
-    )(first, target, order, info, *parts, *logits, *weights)
+    )(first, target, order, info, parts, *logits, *weights)
 
 
 def head_kernel(grad0, grad1, straight0, pieces0, straight1, pieces1, out):
@@ -221,11 +229,12 @@
 
     straight = lax.all_gather(hidden[:, :half], ("dp", "z"), axis=0, tiled=True)
     share = lax.dynamic_slice_in_dim(hidden, half + place * piece, piece, 1)
-    share = lax.all_gather(share, ("dp", "z"), axis=0, tiled=True)
-    pieces = lax.all_to_all(
-        jnp.broadcast_to(share[None], (nv,) + share.shape), ("x", "y"), 0, 0, tiled=True
-    )
-    weights = [head_weight.T, swap(head_weight.T, "core")]
+    share = spread(share, ("dp", "z")).reshape(ndp * nz * block, piece)
+    pieces = spread(share, ("x", "y"))
+    weights = [
+        pltpu.with_memory_space_constraint(w, pltpu.HBM)
+        for w in (head_weight.T, swap(head_weight.T, "core"))
+    ]
     first = jnp.stack([((z * ncore + c) * nv + place) * width for c in (core, 1 - core)])
 
     seq_onehot = segment_ids[:, None] == lax.iota(jnp.int32, advantages.shape[0])[None, :]
@@ -247,9 +256,8 @@
     order = (source[:, None] == lax.iota(jnp.int32, tokens)[None, :]).astype(bf16)
 
     *logits, stats = logits_and_stats(first, target, straight, pieces, weights)
-    for axis in ("y", "x"):
-        stats = jnp.stack(combine(exchange(stats, axis)))
-    parts = exchange(stats, "z")
+    stats = jnp.stack(combine(exchange(stats, "z")))
+    parts = spread(stats, ("x", "y"))
     partial, grad_own, grad_other = gradient_partial(
         first, target, order, info, parts, logits, weights
     )

time: 166 us -> 156 us (0.940)
  blocking collectives: 39.3 us -> 28 us
  waiting for transfers between devices: 38 us -> 48.6 us
  starting transfers between devices: 31.5 us -> 23.4 us
  Pallas kernels: 30 us -> 27.7 us
    all_gather x1 -> x0, blocking collectives: 28.4 us -> none  [per_device(): share = lax.all_gather(share, ('dp', 'z'), axis=0, tiled=True)]
    all_to_all x0 -> x1, blocking collectives: none -> 18 us  [spread(): return lax.all_to_all(copies, axis, 0, 0, tiled=True)]
    ppermute x9 -> x3, starting transfers between devices: 13.6 us -> 2.03 us  [exchange(): lax.ppermute(stats, axis, [(i, (i + step) % size) for i in range(size)])]
    all_to_all x1 -> x2, waiting for transfers between devices: 14 us -> 23.5 us  [spread(): return lax.all_to_all(copies, axis, 0, 0, tiled=True)]
    all_to_all x1 -> x2, starting transfers between devices: 7.63 us -> 14 us  [spread(): return lax.all_to_all(copies, axis, 0, 0, tiled=True)]
    ppermute x5, waiting for transfers between devices: 5.99 us -> 9.03 us  [swap(): return lax.ppermute(value, axis, [(0, 1), (1, 0)])]
    ppermute x5, starting transfers between devices: 4.18 us -> 1.44 us  [swap(): return lax.ppermute(value, axis, [(0, 1), (1, 0)])]
    ppermute x9 -> x3, waiting for transfers between devices: 6.67 us -> 4.75 us  [exchange(): lax.ppermute(stats, axis, [(i, (i + step) % size) for i in range(size)])]
  transfers between devices with their start and end apart: 17 -> 12, of which waited for: 11 -> 8; matrix products, arithmetic and copies ran while one was open for 3% -> 4% of each run, Pallas kernels for 12% -> 12%
where the time goes in v5:
time: 156 us; the launch traced here: 154 us
  waiting for transfers between devices  48.6 us (31%)
  blocking collectives  28 us (18%)
  Pallas kernels  27.7 us (18%)
  starting transfers between devices  23.4 us (15%)
  between operations  14.2 us (9%)
  local copies, waits for them, and re-layouts  8.6 us (6%)
  other arithmetic  3.72 us (2%)
    all_to_all x2, waiting for transfers between devices, spread(): return lax.all_to_all(copies, axis, 0, 0, tiled=True)  23.5 us
    all_to_all x1, blocking collectives, spread(): return lax.all_to_all(copies, axis, 0, 0, tiled=True)  18 us
    all_to_all x2, starting transfers between devices, spread(): return lax.all_to_all(copies, axis, 0, 0, tiled=True)  14 us
    all_to_all x1, waiting for transfers between devices, per_device(): lax.all_to_all(partial.reshape(nv, nz * rows, depth), ('x', 'y'), 0, 0, t...  11.4 us
    all_to_all x1, blocking collectives, scatter_sum(): got = lax.all_to_all(parts, axis, 0, 0, tiled=True)  10 us
    pallas_call x1, Pallas kernels, logits_and_stats(): pl.pallas_call(logits_kernel, grid=(depth // TILE,), in_specs=[pl.BlockSp...  9.76 us
    ppermute x5, waiting for transfers between devices, swap(): return lax.ppermute(value, axis, [(0, 1), (1, 0)])  9.03 us
    pallas_call x1, Pallas kernels, head_gradient(): pl.pallas_call(head_kernel, grid=(depth // TILE,), in_specs=[whole(width,...  9.01 us
  transfers between devices with their start and end apart: 12, of which 8 were waited for; matrix products, arithmetic and copies ran while one was open for 4% of the time, Pallas kernels for 12%

profile of v5, /device:TPU:2, one launch (start us, length us, event | category | flops | bytes accessed | tf_op | source)
XLA Modules:
  0.0 154.3 jit_solution(13894542510630948887)
XLA Ops:
  7.3 1.7 %slice.67 = bf16[64,2048]{1,0:T(8,128)(2,1)} slice(bf16[64,4096]{1,0:T(8,128)(2,1)} %param.8), slice={[0:64], [0:2048]} | slice | bytes 524288 | tf_op jit(solution)/shard_map/slice | solution.py:230
  9.8 18.0 %all_to_all.25 = bf16[8,64,128]{2,1,0:T(8,128)(2,1)S(1)} all-to-all(bf16[8,64,128]{2,1,0:T(8,128)(2,1)S(1)} %broadcast_in_dim.46), channel_id=1, replica_groups=mesh['dp'=2,'z'=4,'core'=2,'x'=4,'y'=4] {'dp','z'}, dimensions={0} | all-to-all | bytes 262144 | tf_op jit(solution)/shard_map/all_to_all | solution.py:41
  27.8 1.7 %broadcast_in_dim.48 = bf16[16,512,128]{2,1,0:T(8,128)(2,1)} broadcast(bf16[512,128]{1,0:T(8,128)(2,1)S(1)} %bitcast.10), dimensions={1,2} | broadcast | bytes 2228224 | tf_op jit(solution)/shard_map/broadcast_in_dim | solution.py:40
  29.5 7.6 %all-to-all-start.1 = ((bf16[16,512,128]{2,1,0:T(8,128)(2,1)}), bf16[16,512,128]{2,1,0:T(8,128)(2,1)S(1)}, u32[]{:S(2)}, u32[]{:S(2)}) async-start(bf16[16,512,128]{2,1,0:T(8,128)(2,1)} %broadcast_in_dim.48), calls=%async_computation.1 | async-start | bytes 4194304 | tf_op jit(solution)/shard_map/all_to_all | solution.py:41
  38.4 7.0 %collective-permute-done = f32[4,256]{1,0:T(4,128)S(1)} collective-permute-done((f32[4,256]{1,0:T(4,128)S(1)}, f32[4,256]{1,0:T(4,128)S(1)}, u32[]{:S(2)}, u32[]{:S(2)}) %collective-permute-start) | collective-permute-done | bytes 4128 | tf_op jit(solution)/shard_map/ppermute | solution.py:45
  45.5 17.9 %all-to-all-done.1.pieces.pieces0 = bf16[16,512,128]{2,1,0:T(8,128)(2,1)S(1)} async-done(((bf16[16,512,128]{2,1,0:T(8,128)(2,1)}), bf16[16,512,128]{2,1,0:T(8,128)(2,1)S(1)}, u32[]{:S(2)}, u32[]{:S(2)}) %all-to-all-start.1) | async-done | bytes 2097184 | tf_op jit(solution)/shard_map/all_to_all | solution.py:41
  63.4 9.8 %logits.1 = (f32[594,512]{1,0:T(8,128)S(1)}, f32[594,512]{1,0:T(8,128)S(1)}, f32[4,512]{1,0:T(4,128)S(1)}) custom-call(s32[2]{0:T(128)S(1)} %pad_add_fusion.first, s32[1,512]{1,0:T(1,128)S(1)} %fusion.9.target, bf16[512,2048]{1,0:T(8,128)(2,1)} %all-gather.2.cloned.1.call-done.straight.straight0, bf16[16,512,128]{2,1,0:T(8,128)(2,1)S(1)} %all-to-all-done.1.pieces.pieces0, ...), custom_call_target="tpu_custom_call" | custom-call | tf_op jit(solution)/shard_map/logits/pallas_call | solution.py:119
  73.2 1.0 copy-done
  74.2 0.9 collective-permute-start.4
  75.1 0.9 collective-permute-start.3
  76.7 1.1 collective-permute-done.4
  77.8 1.8 %collective-permute-done.3 = f32[4,512]{1,0:T(4,128)S(1)} collective-permute-done((f32[4,512]{1,0:T(4,128)S(1)}, f32[4,512]{1,0:T(4,128)S(1)}, u32[]{:S(2)}, u32[]{:S(2)}) %collective-permute-start.3) | collective-permute-done | bytes 8224 | tf_op jit(solution)/shard_map/ppermute | solution.py:27
  79.6 1.8 %collective-permute-done.2 = f32[4,512]{1,0:T(4,128)S(1)} collective-permute-done((f32[4,512]{1,0:T(4,128)S(1)}, f32[4,512]{1,0:T(4,128)S(1)}, u32[]{:S(2)}, u32[]{:S(2)}) %collective-permute-start.2) | collective-permute-done | bytes 8224 | tf_op jit(solution)/shard_map/ppermute | solution.py:27
  82.2 6.4 %all-to-all-start.2 = ((f32[16,4,512]{2,1,0:T(4,128)}), f32[16,4,512]{2,1,0:T(4,128)S(1)}, u32[]{:S(2)}, u32[]{:S(2)}) async-start(f32[16,4,512]{2,1,0:T(4,128)} %broadcast_in_dim.49), calls=%async_computation.2 | async-start | bytes 262144 | tf_op jit(solution)/shard_map/all_to_all | solution.py:41
  89.4 5.6 %all-to-all-done.2.parts = f32[16,4,512]{2,1,0:T(4,128)S(1)} async-done(((f32[16,4,512]{2,1,0:T(4,128)}), f32[16,4,512]{2,1,0:T(4,128)S(1)}, u32[]{:S(2)}, u32[]{:S(2)}) %all-to-all-start.2) | async-done | bytes 131104 | tf_op jit(solution)/shard_map/all_to_all | solution.py:41
  95.0 1.3 copy-done.1
  96.3 0.9 copy-done.2
  97.2 9.0 %grad_hidden_partial.1 = (bf16[256,4096]{1,0:T(8,128)(2,1)}, bf16[594,512]{1,0:T(8,128)(2,1)}, bf16[594,512]{1,0:T(8,128)(2,1)}) custom-call(s32[2]{0:T(128)S(1)} %pad_add_fusion.first, s32[1,512]{1,0:T(1,128)S(1)} %fusion.9.target, bf16[256,512]{1,0:T(8,128)(2,1)S(1)} %copy-done.2, f32[4,512]{1,0:T(4,128)S(1)} %pad_maximum_fusion.info, ...), custom_call_target="tpu_custom_call" | custom-call | tf_op jit(solution)/shard_map/grad_hidden_partial/pallas_call | solution.py:171
  106.2 5.9 %all-to-all-start.3 = ((bf16[16,16,4096]{2,1,0:T(8,128)(2,1)}), bf16[16,16,4096]{2,1,0:T(8,128)(2,1)}, u32[]{:S(2)}, u32[]{:S(2)}) async-start(bf16[16,16,4096]{2,1,0:T(8,128)(2,1)} %bitcast.9), calls=%async_computation.3 | async-start | bytes 4194304 | tf_op jit(solution)/shard_map/all_to_all | solution.py:264
  112.4 2.0 %collective-permute-done.5.grad1 = bf16[594,512]{1,0:T(8,128)(2,1)S(1)} collective-permute-done((bf16[594,512]{1,0:T(8,128)(2,1)S(1)}, bf16[594,512]{1,0:T(8,128)(2,1)S(1)}, u32[]{:S(2)}, u32[]{:S(2)}) %collective-permute-start.5) | collective-permute-done | bytes 608288 | tf_op jit(solution)/shard_map/ppermute | solution.py:45
  114.4 9.0 %grad_head.1 = bf16[594,4096]{1,0:T(8,128)(2,1)} custom-call(bf16[594,512]{1,0:T(8,128)(2,1)S(1)} %copy-done.3, bf16[594,512]{1,0:T(8,128)(2,1)S(1)} %collective-permute-done.5.grad1, bf16[512,2048]{1,0:T(8,128)(2,1)} %all-gather.2.cloned.1.call-done.straight.straight0, bf16[16,512,128]{2,1,0:T(8,128)(2,1)S(1)} %all-to-all-done.1.pieces.pieces0, ...), custom_call_target="tpu_custom_call" | custom-call | flops 4982833152 | bytes 13254656 | tf_op jit(solution)/shard_map/grad_head/pallas_call | solution.py:200
  123.4 11.4 %all-to-all-done.3 = bf16[16,16,4096]{2,1,0:T(8,128)(2,1)} async-done(((bf16[16,16,4096]{2,1,0:T(8,128)(2,1)}), bf16[16,16,4096]{2,1,0:T(8,128)(2,1)}, u32[]{:S(2)}, u32[]{:S(2)}) %all-to-all-start.3) | async-done | bytes 2097184 | tf_op jit(solution)/shard_map/all_to_all | solution.py:264
  134.8 1.9 %reduce_sum.44 = bf16[16,4096]{1,0:T(8,128)(2,1)S(1)} reduce(bf16[16,16,4096]{2,1,0:T(8,128)(2,1)} %all-to-all-done.3, bf16[]{:T(256)} %constant.90.clone.1), dimensions={0}, to_apply=%region_2.3 | reduce | flops 983040 | bytes 2228226 | tf_op jit(solution)/shard_map/reduce_sum | solution.py:270
  136.7 10.0 %all_to_all.26 = bf16[4,4,4096]{2,1,0:T(4,128)(2,1)S(1)} all-to-all(bf16[4,4,4096]{2,1,0:T(4,128)(2,1)S(1)} %reshape.76), channel_id=1, replica_groups=mesh['dp'=2,'z'=4,'core'=2,'x'=4,'y'=4] {'z'}, dimensions={0} | all-to-all | bytes 262144 | tf_op jit(solution)/shard_map/all_to_all | solution.py:34
  (59 shorter events, 5.5 us)
Async XLA Ops:
  7.2 56.2 %all-gather.2.cloned.1.call-start = ((), (), s32[]{:S(2)}) async-start(), calls=%async_computation.5 | async-start | bytes 2359296 | tf_op jit(solution)/shard_map/all_gather | solution.py:230
  7.2 56.2 %collective-permute-start.1 = (bf16[594,4096]{1,0:T(8,128)(2,1)}, bf16[594,4096]{1,0:T(8,128)(2,1)}, u32[]{:S(2)}, u32[]{:S(2)}) collective-permute-start(bf16[594,4096]{1,0:T(8,128)(2,1)} %bitcast.6), channel_id=1, source_target_pairs={{0,16},{16,0},{1,17},{17,1},{2,18},{18,2},{3,19},{19,3},{4,20},{20... | collective-permute-start | bytes 14598152 | tf_op jit(solution)/shard_map/ppermute | solution.py:45
  29.5 7.7 %copy-start.10 = (s32[64]{0:T(128)S(1)}, s32[64]{0:T(128)}, u32[]{:S(2)}) copy-start(s32[64]{0:T(128)} %param.12) | copy-start | bytes 772
  29.5 7.7 %copy-start.4 = (s32[512]{0:T(512)S(1)}, s32[512]{0:T(512)}, u32[]{:S(2)}) copy-start(s32[512]{0:T(512)} %param.11) | copy-start | bytes 6148
  29.5 7.7 %copy-start.8 = (f32[64]{0:T(128)S(1)}, f32[64]{0:T(128)}, u32[]{:S(2)}) copy-start(f32[64]{0:T(128)} %param.14) | copy-start | bytes 772
  29.5 7.9 %copy-start.5 = (s32[512]{0:T(512)S(1)}, s32[512]{0:T(512)}, u32[]{:S(2)}) copy-start(s32[512]{0:T(512)} %param.13) | copy-start | bytes 6148
  29.5 8.0 %copy-start.6 = (f32[512]{0:T(512)S(1)}, f32[512]{0:T(512)}, u32[]{:S(2)}) copy-start(f32[512]{0:T(512)} %param.15) | copy-start | bytes 6148
  29.5 8.0 %copy-start.7 = (s32[512]{0:T(512)S(1)}, s32[512]{0:T(512)}, u32[]{:S(2)}) copy-start(s32[512]{0:T(512)} %param.10) | copy-start | bytes 6148
  29.5 33.8 %all-to-all-start.1 = ((bf16[16,512,128]{2,1,0:T(8,128)(2,1)}), bf16[16,512,128]{2,1,0:T(8,128)(2,1)S(1)}, u32[]{:S(2)}, u32[]{:S(2)}) async-start(bf16[16,512,128]{2,1,0:T(8,128)(2,1)} %broadcast_in_dim.48), calls=%async_computation.1 | async-start | bytes 4194304 | tf_op jit(solution)/shard_map/all_to_all | solution.py:41
  37.8 7.6 %collective-permute-start = (f32[4,256]{1,0:T(4,128)S(1)}, f32[4,256]{1,0:T(4,128)S(1)}, u32[]{:S(2)}, u32[]{:S(2)}) collective-permute-start(f32[4,256]{1,0:T(4,128)S(1)} %select_n.74), channel_id=1, source_target_pairs={{0,128},{128,0},{1,129},{129,1},{2,130},{130,2},{3,131},{131,3},{4... | collective-permute-start | bytes 12296 | tf_op jit(solution)/shard_map/ppermute | solution.py:45
  73.1 1.0 copy-start
  74.2 3.7 %collective-permute-start.4 = (f32[4,512]{1,0:T(4,128)S(1)}, f32[4,512]{1,0:T(4,128)S(1)}, u32[]{:S(2)}, u32[]{:S(2)}) collective-permute-start(f32[4,512]{1,0:T(4,128)S(1)} %get-tuple-element.10), channel_id=1, source_target_pairs={{0,96},{32,0},{64,32},{96,64},{1,97},{33,1},{65,33},{97,65},{2,98}... | collective-permute-start | bytes 24584 | tf_op jit(solution)/shard_map/ppermute | solution.py:27
  75.1 4.5 %collective-permute-start.3 = (f32[4,512]{1,0:T(4,128)S(1)}, f32[4,512]{1,0:T(4,128)S(1)}, u32[]{:S(2)}, u32[]{:S(2)}) collective-permute-start(f32[4,512]{1,0:T(4,128)S(1)} %get-tuple-element.10), channel_id=1, source_target_pairs={{0,64},{32,96},{64,0},{96,32},{1,65},{33,97},{65,1},{97,33},{2,66}... | collective-permute-start | bytes 24584 | tf_op jit(solution)/shard_map/ppermute | solution.py:27
  76.0 5.4 %collective-permute-start.2 = (f32[4,512]{1,0:T(4,128)S(1)}, f32[4,512]{1,0:T(4,128)S(1)}, u32[]{:S(2)}, u32[]{:S(2)}) collective-permute-start(f32[4,512]{1,0:T(4,128)S(1)} %get-tuple-element.10), channel_id=1, source_target_pairs={{0,32},{32,64},{64,96},{96,0},{1,33},{33,65},{65,97},{97,1},{2,34}... | collective-permute-start | bytes 24584 | tf_op jit(solution)/shard_map/ppermute | solution.py:27
  76.2 36.2 %collective-permute-start.7 = (bf16[16,512,128]{2,1,0:T(8,128)(2,1)S(1)}, bf16[16,512,128]{2,1,0:T(8,128)(2,1)}, u32[]{:S(2)}, u32[]{:S(2)}) collective-permute-start(bf16[16,512,128]{2,1,0:T(8,128)(2,1)S(1)} %all-to-all-done.1.pieces.pieces0), channel_id=1, source_target_pairs={{0,16},{16,0},{1,17},{17,1},{2,18},{18,2},{3,19},{19,3},{4,20},{20... | collective-permute-start | bytes 6291464 | tf_op jit(solution)/shard_map/ppermute | solution.py:45
  76.2 38.2 %collective-permute-start.6 = (bf16[512,2048]{1,0:T(8,128)(2,1)}, bf16[512,2048]{1,0:T(8,128)(2,1)}, u32[]{:S(2)}, u32[]{:S(2)}) collective-permute-start(bf16[512,2048]{1,0:T(8,128)(2,1)} %all-gather.2.cloned.1.call-done.straight.straight0), channel_id=1, source_target_pairs={{0,16},{16,0},{1,17},{17,1},{2,18},{18,2},{3,19},{19,3},{4,20},{20... | collective-permute-start | bytes 6291464 | tf_op jit(solution)/shard_map/ppermute | solution.py:45
  82.2 12.8 %all-to-all-start.2 = ((f32[16,4,512]{2,1,0:T(4,128)}), f32[16,4,512]{2,1,0:T(4,128)S(1)}, u32[]{:S(2)}, u32[]{:S(2)}) async-start(f32[16,4,512]{2,1,0:T(4,128)} %broadcast_in_dim.49), calls=%async_computation.2 | async-start | bytes 262144 | tf_op jit(solution)/shard_map/all_to_all | solution.py:41
  95.0 1.3 copy-start.1
  96.3 0.9 copy-start.2
  106.2 5.9 %copy-start.9 = (bf16[594,512]{1,0:T(8,128)(2,1)S(1)}, bf16[594,512]{1,0:T(8,128)(2,1)}, u32[]{:S(2)}) copy-start(bf16[594,512]{1,0:T(8,128)(2,1)} %get-tuple-element.15) | copy-start | bytes 1824772
  106.2 8.2 %copy-start.3 = (bf16[594,512]{1,0:T(8,128)(2,1)S(1)}, bf16[594,512]{1,0:T(8,128)(2,1)}, u32[]{:S(2)}) copy-start(bf16[594,512]{1,0:T(8,128)(2,1)} %get-tuple-element.14.grad0) | copy-start | bytes 1824772
  106.2 28.6 %all-to-all-start.3 = ((bf16[16,16,4096]{2,1,0:T(8,128)(2,1)}), bf16[16,16,4096]{2,1,0:T(8,128)(2,1)}, u32[]{:S(2)}, u32[]{:S(2)}) async-start(bf16[16,16,4096]{2,1,0:T(8,128)(2,1)} %bitcast.9), calls=%async_computation.3 | async-start | bytes 4194304 | tf_op jit(solution)/shard_map/all_to_all | solution.py:264
  112.1 2.3 %collective-permute-start.5 = (bf16[594,512]{1,0:T(8,128)(2,1)S(1)}, bf16[594,512]{1,0:T(8,128)(2,1)S(1)}, u32[]{:S(2)}, u32[]{:S(2)}) collective-permute-start(bf16[594,512]{1,0:T(8,128)(2,1)S(1)} %copy-done.9), channel_id=1, source_target_pairs={{0,16},{16,0},{1,17},{17,1},{2,18},{18,2},{3,19},{19,3},{4,20},{20... | collective-permute-start | bytes 1824776 | tf_op jit(solution)/shard_map/ppermute | solution.py:45
Sparse Core Ops, SparseCore 0:
  9.8 44.0 all-gather.1

commit v6 on v5

v6 whole, which is shorter than its diff:
```python
import functools

import jax
import jax.numpy as jnp
from jax import lax
from jax.experimental import pallas as pl
from jax.experimental.pallas import tpu as pltpu
from jax.sharding import Mesh, PartitionSpec as P

LOSS_SCALE = 1024
KL_WEIGHT = 0.1
ENTROPY_WEIGHT = 0.05


def combine(parts):
    top = parts[0][0]
    for part in parts[1:]:
        top = jnp.maximum(top, part[0])
    scales = [jnp.exp(part[0] - top) for part in parts]
    total = sum(part[1] * scale for part, scale in zip(parts, scales))
    logit = sum(part[2] * scale for part, scale in zip(parts, scales))
    target = sum(part[3] for part in parts)
    return [top, total, logit, target]


def exchange(stats, axis):
    size = lax.axis_size(axis)
    others = [
        lax.ppermute(stats, axis, [(i, (i + step) % size) for i in range(size)])
        for step in range(1, size)
    ]
    return [stats] + others


def scatter_sum(parts, axis):
    got = lax.all_to_all(parts, axis, 0, 0, tiled=True)
    return jnp.sum(got.astype(jnp.float32), axis=0)


def spread(value, axis):
    count = lax.axis_size(axis)
    copies = jnp.broadcast_to(value[None], (count,) + value.shape)
    return lax.all_to_all(copies, axis, 0, 0, tiled=True)


def swap(value, axis):
    return lax.ppermute(value, axis, [(0, 1), (1, 0)])


TILE = 1024
PARAMS = pltpu.CompilerParams(vmem_limit_bytes=24 * 2**20)


def whole(*shape):
    return pl.BlockSpec(shape, lambda i, s: (0,) * len(shape))


def tiles(rows):
    return pl.BlockSpec((rows, TILE), lambda i, s: (0, i))


def hidden_specs(tokens, depth, group):
    lead = depth // TILE // 2
    return [
        pl.BlockSpec((tokens, TILE), lambda i, s: (s[group], jnp.minimum(i, lead - 1))),
        pl.BlockSpec((tokens, TILE), lambda i, s: (s[group], jnp.maximum(i - lead, 0))),
    ]


def call(kernel, name, depth, in_specs, out_specs, out_shape, scratch=(), flops=0):
    return pl.pallas_call(
        kernel,
        grid_spec=pltpu.PrefetchScalarGridSpec(
            num_scalar_prefetch=1,
            grid=(depth // TILE,),
            in_specs=in_specs,
            out_specs=out_specs,
            scratch_shapes=list(scratch),
        ),
        out_shape=out_shape,
        compiler_params=PARAMS,
        cost_estimate=pl.CostEstimate(flops=flops, bytes_accessed=flops // 500, transcendentals=0),
        name=name,
    )


def halves(use_first, use_second):
    step, lead = pl.program_id(0), pl.num_programs(0) // 2
    pl.when(step < lead)(use_first)
    pl.when(step >= lead)(use_second)


def add_logits(tile, weights, logits):
    for weight, out in zip(weights, logits):
        out[...] += lax.dot_general(
            weight[...], tile, (((1,), (1,)), ((), ())), preferred_element_type=jnp.float32
        )


def hits(value, first, target):
    return first + lax.broadcasted_iota(jnp.int32, value.shape, 0) == target[...]


def logits_kernel(s, target, straight, pieces, weight0, weight1, logits0, logits1, stats):
    step = pl.program_id(0)

    @pl.when(step == 0)
    def _():
        logits0[...] = jnp.zeros_like(logits0)
        logits1[...] = jnp.zeros_like(logits1)

    def use_second():
        tile = jnp.concatenate([pieces[j] for j in range(pieces.shape[0])], axis=1)
        add_logits(tile, (weight0, weight1), (logits0, logits1))

    halves(
        lambda: add_logits(straight[...], (weight0, weight1), (logits0, logits1)), use_second
    )

    @pl.when(step == pl.num_programs(0) - 1)
    def _():
        top = jnp.maximum(
            jnp.max(logits0[...], axis=0, keepdims=True),
            jnp.max(logits1[...], axis=0, keepdims=True),
        )
        stats[0:1, :] = top
        total, weighted, hit_sum = 0.0, 0.0, 0.0
        for k, logits in enumerate((logits0, logits1)):
            value = logits[...]
            shifted = jnp.exp(value - top)
            hit = jnp.where(hits(value, s[2 + k], target), value, 0.0)
            total += jnp.sum(shifted, axis=0, keepdims=True)
            weighted += jnp.sum(shifted * value, axis=0, keepdims=True)
            hit_sum += jnp.sum(hit, axis=0, keepdims=True)
        stats[1:2, :] = total
        stats[2:3, :] = weighted
        stats[3:4, :] = hit_sum


def logits_and_stats(scalars, target, straight, pieces, weights):
    width, depth = weights[0].shape
    tokens, piece = pieces.shape[1:]
    lead = depth // TILE // 2
    return call(
        logits_kernel,
        "logits",
        depth,
        [
            whole(1, tokens),
            hidden_specs(tokens, depth, 0)[0],
            pl.BlockSpec(
                (TILE // piece, tokens, piece), lambda i, s: (jnp.maximum(i - lead, 0), 0, 0)
            ),
            tiles(width),
            tiles(width),
        ],
        [whole(width, tokens)] * 2 + [whole(4, tokens)],
        [pltpu.HBM((width, tokens), jnp.float32)] * 2
        + [jax.ShapeDtypeStruct((4, tokens), jnp.float32)],
        flops=4 * tokens * width * depth,
    )(scalars, target, straight, pieces, *weights)


def logit_gradient(value, first, target, info, final):
    adv, weight, ref_logp = [info[i : i + 1, :] for i in range(3)]
    log_total, target_logp, mean_logit = final
    logp_grad = -adv + KL_WEIGHT * (target_logp - ref_logp)
    hit = jnp.where(hits(value, first, target), 1.0, 0.0)
    probs = jnp.exp(value - log_total)
    inner = logp_grad * (hit - probs)
    inner = inner + ENTROPY_WEIGHT * probs * (value - mean_logit)
    return (weight * inner).astype(jnp.bfloat16)


def gradient_kernel(
    s, target, info, parts, logits0, logits1, weight0, weight1,
    out, grad0, grad1, final, held0, held1, *, nz, nv,
):
    @pl.when(pl.program_id(0) == 0)
    def _():
        count, tokens = parts.shape[0], parts.shape[2]
        row_max, exp_total, exp_logit, target_logit = combine(
            [[parts[j, i : i + 1, :] for i in range(4)] for j in range(count)]
        )
        log_total = row_max + jnp.log(exp_total)
        ends = (log_total, target_logit - log_total, exp_logit / exp_total)
        for i, end in enumerate(ends):
            final[i : i + 1, :] = end
        rows = tokens // (nz * nv)
        row = lax.broadcasted_iota(jnp.int32, (tokens, tokens), 0)
        token = lax.broadcasted_iota(jnp.int32, (tokens, tokens), 1)
        source = (row // rows % nz * nv + row // (rows * nz)) * rows + row % rows
        order = jnp.where(token == source, 1.0, 0.0).astype(jnp.bfloat16)
        sets = ((logits0, grad0, held0), (logits1, grad1, held1))
        for k, (logits, grad, held) in enumerate(sets):
            result = logit_gradient(logits[...], s[2 + k], target, info, ends)
            grad[...] = result
            held[...] = lax.dot_general(
                order, result, (((1,), (1,)), ((), ())), preferred_element_type=jnp.float32
            ).astype(jnp.bfloat16)

    out[...] = (
        jnp.dot(held0[...], weight0[...], preferred_element_type=jnp.float32)
        + jnp.dot(held1[...], weight1[...], preferred_element_type=jnp.float32)
    ).astype(jnp.bfloat16)


def gradient_partial(scalars, target, info, parts, logits, weights, nz, nv):
    width, depth = weights[0].shape
    tokens = info.shape[1]
    return call(
        functools.partial(gradient_kernel, nz=nz, nv=nv),
        "grad_hidden_partial",
        depth,
        [whole(1, tokens), whole(4, tokens), whole(*parts.shape)]
        + [whole(width, tokens)] * 2
        + [tiles(width)] * 2,
        [tiles(tokens)] + [whole(width, tokens)] * 2 + [whole(3, tokens)],
        [pltpu.HBM((tokens, depth), jnp.bfloat16)]
        + [pltpu.HBM((width, tokens), jnp.bfloat16)] * 2
        + [jax.ShapeDtypeStruct((3, tokens), jnp.float32)],
        [pltpu.VMEM((tokens, width), jnp.bfloat16)] * 2,
        flops=4 * tokens * width * depth,
    )(scalars, target, info, parts, *logits, *weights)


def other_kernel(
    s, target, info, final, straight, straight2, weight0, weight1, grad0, grad1, logits0, logits1
):
    step = pl.program_id(0)

    @pl.when(step == 0)
    def _():
        logits0[...] = jnp.zeros_like(logits0)
        logits1[...] = jnp.zeros_like(logits1)

    halves(
        lambda: add_logits(straight[...], (weight0, weight1), (logits0, logits1)),
        lambda: add_logits(straight2[...], (weight0, weight1), (logits0, logits1)),
    )

    @pl.when(step == pl.num_programs(0) - 1)
    def _():
        ends = [final[i : i + 1, :] for i in range(3)]
        for k, (logits, grad) in enumerate(((logits0, grad0), (logits1, grad1))):
            grad[...] = logit_gradient(logits[...], s[2 + k], target, info, ends)


def other_gradient(scalars, target, info, final, straights, weights):
    width, depth = weights[0].shape
    tokens = info.shape[1]
    return call(
        other_kernel,
        "other_group_grad_logits",
        depth,
        [whole(1, tokens), whole(4, tokens), whole(3, tokens)]
        + hidden_specs(tokens, depth, 1)
        + [tiles(width)] * 2,
        [whole(width, tokens)] * 2,
        [pltpu.HBM((width, tokens), jnp.bfloat16)] * 2,
        [pltpu.VMEM((width, tokens), jnp.float32)] * 2,
        flops=4 * tokens * width * depth,
    )(scalars, target, info, final, *straights, *weights)


def head_kernel(s, *refs):
    out, count = refs[-1], (len(refs) - 1) // 3
    grads, firsts, seconds = refs[:count], refs[count:-1:2], refs[count + 1 : -1 : 2]

    def use(hiddens):
        total = 0.0
        for grad, hidden in zip(grads, hiddens):
            total = total + jnp.dot(grad[...], hidden[...], preferred_element_type=jnp.float32)
        out[...] = total.astype(jnp.bfloat16)

    halves(lambda: use(firsts), lambda: use(seconds))


def head_gradient(scalars, grads, hiddens):
    width, tokens = grads[0].shape
    depth = 2 * hiddens[0][0].shape[1]
    return call(
        head_kernel,
        "grad_head",
        depth,
        [whole(width, tokens)] * 4
        + (hidden_specs(tokens, depth, 0) + hidden_specs(tokens, depth, 1)) * 2,
        tiles(width),
        jax.ShapeDtypeStruct((width, depth), jnp.bfloat16),
        flops=8 * tokens * width * depth,
    )(scalars, *grads, *[h for pair in hiddens for h in (*pair, *pair)])


def in_hbm(value):
    return pltpu.with_memory_space_constraint(value, pltpu.HBM)


def per_device(
    hidden, head_weight, targets, segment_ids, lengths, loss_mask, advantages, ref_logprobs
):
    bf16, f32 = jnp.bfloat16, jnp.float32
    depth, width = head_weight.shape
    nz, ncore = lax.axis_size("z"), lax.axis_size("core")
    nv = lax.axis_size("x") * lax.axis_size("y")
    block = hidden.shape[0]
    rows = block // nv
    dp, z, core = lax.axis_index("dp"), lax.axis_index("z"), lax.axis_index("core")
    place = lax.axis_index(("x", "y"))
    half, piece = depth // 2, depth // 2 // nv

    straight = lax.all_gather(hidden[:, :half], ("dp", "z"), axis=0, tiled=True)
    share = lax.dynamic_slice_in_dim(hidden, half + place * piece, piece, 1)
    share = spread(share, "z").reshape(nz * block, piece)
    pieces = spread(share, ("x", "y"))
    weights = [in_hbm(w) for w in (head_weight.T, swap(head_weight.T, "core"))]
    scalars = jnp.stack(
        [dp, 1 - dp] + [((z * ncore + c) * nv + place) * width for c in (core, 1 - core)]
    )

    seq_onehot = segment_ids[:, None] == lax.iota(jnp.int32, advantages.shape[0])[None, :]
    token_adv = jnp.sum(jnp.where(seq_onehot, advantages[None, :], 0.0), axis=1)
    token_len = jnp.sum(jnp.where(seq_onehot, lengths[None, :].astype(f32), 0.0), axis=1)
    token_weight = LOSS_SCALE * loss_mask.astype(f32) / token_len
    own = jnp.stack([token_adv, token_weight, ref_logprobs, targets.astype(f32)])
    own = own.reshape(4, nz, ncore, block)
    own = jnp.where(core == 0, own[:, :, 0], own[:, :, 1]).reshape(4, nz * block)
    other = swap(own, "dp")
    later, straight, pieces, other = lax.optimization_barrier(
        (hidden[:, half:], straight, pieces, other)
    )
    straight2 = lax.all_gather(later, ("dp", "z"), axis=0, tiled=True)
    own_target, other_target = own[3:4].astype(jnp.int32), other[3:4].astype(jnp.int32)

    *logits, stats = logits_and_stats(
        scalars, own_target, in_hbm(straight), pieces, weights
    )
    stats = jnp.stack(combine(exchange(stats, "z")))
    parts = spread(stats, ("x", "y"))
    logits = [in_hbm(value) for value in logits]
    partial, own0, own1, final = gradient_partial(
        scalars, own_target, own, parts, logits, weights, nz, nv
    )
    got = lax.all_to_all(partial.reshape(nv, nz * rows, depth), ("x", "y"), 0, 0, tiled=True)
    straight, straight2, final = lax.optimization_barrier(
        (straight, straight2, swap(final, "dp"))
    )
    gathered = (in_hbm(straight), in_hbm(straight2))
    other0, other1 = other_gradient(
        scalars, other_target, other, final, gathered, weights
    )
    grad_head = head_gradient(
        scalars,
        (own0, other0, swap(own1, "core"), swap(other1, "core")),
        (gathered, (in_hbm(swap(straight, "core")), in_hbm(swap(straight2, "core")))),
    )
    got, grad_head = lax.optimization_barrier((got, grad_head))
    got = jnp.sum(got.astype(f32), axis=0).astype(bf16)
    grad_hidden = scatter_sum(got.reshape(nz, rows, depth), "z").astype(bf16)
    return grad_hidden, grad_head.T


def solution(mesh):
    devices = mesh.devices.reshape(2, 4, 2, 4, 4)
    fine = Mesh(devices, ("dp", "z", "core", "x", "y"))
    ctx, vocab = ("z", "core"), ("x", "y")
    return jax.shard_map(
        per_device,
        mesh=fine,
        in_specs=(
            P(("dp",) + ctx, None),
            P(None, ctx + vocab),
            P("dp"),
            P("dp"),
            P(),
            P("dp"),
            P(),
            P("dp"),
        ),
        out_specs=(P(("dp",) + ctx + vocab, None), P(None, ctx + vocab)),
        check_vma=False,
    )
```

time: 156 us -> 156 us (level)
  waiting for transfers between devices: 48.6 us -> 39.1 us
  Pallas kernels: 27.7 us -> 36.9 us
  starting transfers between devices: 23.4 us -> 31.3 us
  blocking collectives: 28 us -> 21.5 us
  local copies, waits for them, and re-layouts: 8.6 us -> 6.48 us
    all_to_all x2, waiting for transfers between devices: 23.5 us -> 9.48 us  [spread(): return lax.all_to_all(copies, axis, 0, 0, tiled=True)]
    pallas_call x3 -> x4, Pallas kernels: 27.7 us -> 36.9 us  [the longest x1 10.3 us: head_gradient(): call(head_kernel, 'grad_head', depth, [whole(width, tokens)] * 4 + (hidde...]
    all_gather x1, waiting for transfers between devices: 0.01 us -> 8.73 us  [per_device(): straight = lax.all_gather(hidden[:, :half], ('dp', 'z'), axis=0, tiled=True)]
    ppermute x5 -> x7, starting transfers between devices: 1.44 us -> 8.91 us  [swap(): return lax.ppermute(value, axis, [(0, 1), (1, 0)])]
    all_to_all x1, blocking collectives: 18 us -> 13.2 us  [spread(): return lax.all_to_all(copies, axis, 0, 0, tiled=True)]
    all_to_all x1, waiting for transfers between devices: 11.4 us -> 6.77 us  [per_device(): lax.all_to_all(partial.reshape(nv, nz * rows, depth), ('x', 'y'), 0, 0, t...]
    unnamed x25 -> x19, local copies, waits for them, and re-layouts: 3.31 us -> 1 us
    all_to_all x1, blocking collectives: 10 us -> 8.31 us  [scatter_sum(): got = lax.all_to_all(parts, axis, 0, 0, tiled=True)]
  transfers between devices with their start and end apart: 12 -> 15, of which waited for: 8 -> 10; matrix products, arithmetic and copies ran while one was open for 4% -> 4% of each run, Pallas kernels for 12% -> 24%
where the time goes in v6:
time: 156 us; the launch traced here: 154 us
  waiting for transfers between devices  39.1 us (25%)
  Pallas kernels  36.9 us (24%)
  starting transfers between devices  31.3 us (20%)
  blocking collectives  21.5 us (14%)
  between operations  14.2 us (9%)
  local copies, waits for them, and re-layouts  6.48 us (4%)
  other arithmetic  4.86 us (3%)
    all_to_all x2, starting transfers between devices, spread(): return lax.all_to_all(copies, axis, 0, 0, tiled=True)  13.4 us
    all_to_all x1, blocking collectives, spread(): return lax.all_to_all(copies, axis, 0, 0, tiled=True)  13.2 us
    pallas_call x1, Pallas kernels, head_gradient(): call(head_kernel, 'grad_head', depth, [whole(width, tokens)] * 4 + (hidde...  10.3 us
    all_to_all x2, waiting for transfers between devices, spread(): return lax.all_to_all(copies, axis, 0, 0, tiled=True)  9.48 us
    pallas_call x1, Pallas kernels, gradient_partial(): call(functools.partial(gradient_kernel, nz=nz, nv=nv), 'grad_hidden_parti...  9.43 us
    ppermute x7, waiting for transfers between devices, swap(): return lax.ppermute(value, axis, [(0, 1), (1, 0)])  9.16 us
    ppermute x7, starting transfers between devices, swap(): return lax.ppermute(value, axis, [(0, 1), (1, 0)])  8.91 us
    all_gather x1, waiting for transfers between devices, per_device(): straight = lax.all_gather(hidden[:, :half], ('dp', 'z'), axis=0, tiled=True)  8.73 us
  transfers between devices with their start and end apart: 15, of which 10 were waited for; matrix products, arithmetic and copies ran while one was open for 4% of the time, Pallas kernels for 24%

profile of v6, /device:TPU:2, one launch (start us, length us, event | category | flops | bytes accessed | tf_op | source)
XLA Modules:
  0.0 154.3 jit_solution(11348693095946460040)
XLA Ops:
  7.2 1.9 %fusion.8 = (bf16[64,2048]{1,0:T(8,128)(2,1)}, bf16[64,2048]{1,0:T(8,128)(2,1)}) fusion(bf16[64,4096]{1,0:T(8,128)(2,1)} %param.8), kind=kLoop, calls=%fused_computation.36 | loop fusion | bytes 1048576 | tf_op jit(solution)/shard_map/slice | solution.py:311
  10.6 5.9 %all-to-all-start = ((bf16[4,64,128]{2,1,0:T(8,128)(2,1)}), bf16[4,64,128]{2,1,0:T(8,128)(2,1)S(1)}, u32[]{:S(2)}, u32[]{:S(2)}) async-start(bf16[4,64,128]{2,1,0:T(8,128)(2,1)} %broadcast_in_dim.44), calls=%async_computation | async-start | bytes 131072 | tf_op jit(solution)/shard_map/all_to_all | solution.py:43
  17.9 4.3 %all-to-all-done = bf16[4,64,128]{2,1,0:T(8,128)(2,1)S(1)} async-done(((bf16[4,64,128]{2,1,0:T(8,128)(2,1)}), bf16[4,64,128]{2,1,0:T(8,128)(2,1)S(1)}, u32[]{:S(2)}, u32[]{:S(2)}) %all-to-all-start) | async-done | bytes 65568 | tf_op jit(solution)/shard_map/all_to_all | solution.py:43
  22.2 1.2 broadcast_in_dim.46
  23.4 7.5 %all-to-all-start.1 = ((bf16[16,256,128]{2,1,0:T(8,128)(2,1)}), bf16[16,256,128]{2,1,0:T(8,128)(2,1)S(1)}, u32[]{:S(2)}, u32[]{:S(2)}) async-start(bf16[16,256,128]{2,1,0:T(8,128)(2,1)} %broadcast_in_dim.46), calls=%async_computation.1 | async-start | bytes 2097152 | tf_op jit(solution)/shard_map/all_to_all | solution.py:43
  32.6 4.6 %collective-permute-start = (f32[4,256]{1,0:T(4,128)S(1)}, f32[4,256]{1,0:T(4,128)S(1)}, u32[]{:S(2)}, u32[]{:S(2)}) collective-permute-start(f32[4,256]{1,0:T(4,128)S(1)} %select_n.27.info), channel_id=1, source_target_pairs={{0,128},{128,0},{1,129},{129,1},{2,130},{130,2},{3,131},{131,3},{4... | collective-permute-start | bytes 12296 | tf_op jit(solution)/shard_map/ppermute | solution.py:47
  37.2 3.1 %collective-permute-done.info = f32[4,256]{1,0:T(4,128)S(1)} collective-permute-done((f32[4,256]{1,0:T(4,128)S(1)}, f32[4,256]{1,0:T(4,128)S(1)}, u32[]{:S(2)}, u32[]{:S(2)}) %collective-permute-start) | collective-permute-done | bytes 4128 | tf_op jit(solution)/shard_map/ppermute | solution.py:47
  40.4 5.2 %all-to-all-done.1.pieces = bf16[16,256,128]{2,1,0:T(8,128)(2,1)S(1)} async-done(((bf16[16,256,128]{2,1,0:T(8,128)(2,1)}), bf16[16,256,128]{2,1,0:T(8,128)(2,1)S(1)}, u32[]{:S(2)}, u32[]{:S(2)}) %all-to-all-start.1) | async-done | bytes 1048608 | tf_op jit(solution)/shard_map/all_to_all | solution.py:43
  45.5 8.7 %all-gather.3.cloned.1.call-done.straight.refs_4_.refs_6_ = bf16[512,2048]{1,0:T(8,128)(2,1)} async-done(((bf16[64,2048]{1,0:T(8,128)(2,1)}), bf16[512,2048]{1,0:T(8,128)(2,1)}) %all-gather.3.cloned.1.call-update) | async-done | bytes 2097168 | tf_op jit(solution)/shard_map/all_gather | solution.py:311
  54.5 8.5 %logits.1 = (f32[594,256]{1,0:T(8,128)}, f32[594,256]{1,0:T(8,128)}, f32[4,256]{1,0:T(4,128)S(1)}) custom-call(s32[4]{0:T(128)S(1)} %pad_add_fusion.s, s32[1,256]{1,0:T(1,128)S(1)} %convert_element_type.26.target, bf16[512,2048]{1,0:T(8,128)(2,1)} %all-gather.3.cloned.1.call-done.straight.refs_4_.refs_6_, bf16[16,256,128]{2,1,0:T(8,128)(2,1)S(1)} %all-to-all-done.1.pieces, ...), custom_call_target="tpu_custom_call" | custom-call | flops 2491416576 | bytes 4982833 | tf_op jit(solution)/shard_map/logits/pallas_call | solution.py:144
  63.0 2.4 %collective-permute-start.4 = (f32[4,256]{1,0:T(4,128)S(1)}, f32[4,256]{1,0:T(4,128)S(1)}, u32[]{:S(2)}, u32[]{:S(2)}) collective-permute-start(f32[4,256]{1,0:T(4,128)S(1)} %get-tuple-element.22), channel_id=1, source_target_pairs={{0,96},{32,0},{64,32},{96,64},{1,97},{33,1},{65,33},{97,65},{2,98}... | collective-permute-start | bytes 12296 | tf_op jit(solution)/shard_map/ppermute | solution.py:29
  66.8 3.3 %collective-permute-done.3 = f32[4,256]{1,0:T(4,128)S(1)} collective-permute-done((f32[4,256]{1,0:T(4,128)S(1)}, f32[4,256]{1,0:T(4,128)S(1)}, u32[]{:S(2)}, u32[]{:S(2)}) %collective-permute-start.3) | collective-permute-done | bytes 4128 | tf_op jit(solution)/shard_map/ppermute | solution.py:29
  70.1 1.0 collective-permute-done.2
  71.1 13.2 %all_to_all.25.parts = f32[16,4,256]{2,1,0:T(4,128)S(1)} all-to-all(f32[16,4,256]{2,1,0:T(4,128)S(1)} %broadcast_in_dim.47), channel_id=1, replica_groups=mesh['dp'=2,'z'=4,'core'=2,'x'=4,'y'=4] {'x','y'}, dimensions={0} | all-to-all | bytes 131072 | tf_op jit(solution)/shard_map/all_to_all | solution.py:43
  84.4 9.4 %grad_hidden_partial.1 = (bf16[256,4096]{1,0:T(8,128)(2,1)}, bf16[594,256]{1,0:T(8,128)(2,1)}, bf16[594,256]{1,0:T(8,128)(2,1)}, f32[3,256]{1,0:T(4,128)S(1)}) custom-call(s32[4]{0:T(128)S(1)} %pad_add_fusion.s, s32[1,256]{1,0:T(1,128)S(1)} %convert_element_type.26.target, f32[4,256]{1,0:T(4,128)S(1)} %select_n.27.info, f32[16,4,256]{2,1,0:T(4,128)S(1)} %all_to_all.25.parts, ...), custom_call_target="tpu_custom_call" | custom-call | flops 2491416576 | bytes 4982833 | tf_op jit(solution)/shard_map/grad_hidden_partial/pallas_call | solution.py:211
  93.8 2.9 %collective-permute-start.5 = (f32[3,256]{1,0:T(4,128)S(1)}, f32[3,256]{1,0:T(4,128)S(1)}, u32[]{:S(2)}, u32[]{:S(2)}) collective-permute-start(f32[3,256]{1,0:T(4,128)S(1)} %get-tuple-element.29), channel_id=1, source_target_pairs={{0,128},{128,0},{1,129},{129,1},{2,130},{130,2},{3,131},{131,3},{4... | collective-permute-start | bytes 9224 | tf_op jit(solution)/shard_map/ppermute | solution.py:47
  96.7 4.6 %collective-permute-done.5.final = f32[3,256]{1,0:T(4,128)S(1)} collective-permute-done((f32[3,256]{1,0:T(4,128)S(1)}, f32[3,256]{1,0:T(4,128)S(1)}, u32[]{:S(2)}, u32[]{:S(2)}) %collective-permute-start.5) | collective-permute-done | bytes 3104 | tf_op jit(solution)/shard_map/ppermute | solution.py:47
  101.8 5.8 %all-to-all-start.3 = ((bf16[16,16,4096]{2,1,0:T(8,128)(2,1)}), bf16[16,16,4096]{2,1,0:T(8,128)(2,1)}, u32[]{:S(2)}, u32[]{:S(2)}) async-start(bf16[16,16,4096]{2,1,0:T(8,128)(2,1)} %bitcast.13), calls=%async_computation.3 | async-start | bytes 4194304 | tf_op jit(solution)/shard_map/all_to_all | solution.py:343
  108.0 8.6 %other_group_grad_logits.1 = (bf16[594,256]{1,0:T(8,128)(2,1)}, bf16[594,256]{1,0:T(8,128)(2,1)}) custom-call(s32[4]{0:T(128)S(1)} %pad_add_fusion.s, s32[1,256]{1,0:T(1,128)S(1)} %slice_convert_fusion.1.target, f32[4,256]{1,0:T(4,128)S(1)} %collective-permute-done.info, f32[3,256]{1,0:T(4,128)S(1)} %collective-permute-done.5.final, ...), custom_call_target="tpu_custom_call" | custom-call | flops 2491416576 | bytes 4982833 | tf_op jit(solution)/shard_map/other_group_grad_logits/pallas_call | solution.py:252
  117.1 1.4 collective-permute-done.7.refs_3_
  119.5 10.3 %grad_head.1 = bf16[594,4096]{1,0:T(8,128)(2,1)} custom-call(s32[4]{0:T(128)S(1)} %pad_add_fusion.s, bf16[594,256]{1,0:T(8,128)(2,1)S(1)} %copy-done, bf16[594,256]{1,0:T(8,128)(2,1)S(1)} %copy-done.1, bf16[594,256]{1,0:T(8,128)(2,1)S(1)} %collective-permute-done.6.refs_2_, bf16[594,256]{1,0:T(8,128)(2,1)S(1)} %collective-permute-done.7.refs_3_, ...), custom_call_target="tpu_custom_call" | custom-call | flops 4982833152 | bytes 9965666 | tf_op jit(solution)/shard_map/grad_head/pallas_call | solution.py:282
  129.8 6.8 %all-to-all-done.3 = bf16[16,16,4096]{2,1,0:T(8,128)(2,1)} async-done(((bf16[16,16,4096]{2,1,0:T(8,128)(2,1)}), bf16[16,16,4096]{2,1,0:T(8,128)(2,1)}, u32[]{:S(2)}, u32[]{:S(2)}) %all-to-all-start.3) | async-done | bytes 2097184 | tf_op jit(solution)/shard_map/all_to_all | solution.py:343
  136.5 1.9 %reduce_sum.44 = bf16[16,4096]{1,0:T(8,128)(2,1)S(1)} reduce(bf16[16,16,4096]{2,1,0:T(8,128)(2,1)} %all-to-all-done.3, bf16[]{:T(256)} %constant.46.clone.1), dimensions={0}, to_apply=%region_2.3 | reduce | flops 983040 | bytes 2228226 | tf_op jit(solution)/shard_map/reduce_sum | solution.py:357
  138.5 8.3 %all_to_all.26 = bf16[4,4,4096]{2,1,0:T(4,128)(2,1)S(1)} all-to-all(bf16[4,4,4096]{2,1,0:T(4,128)(2,1)S(1)} %reshape.51), channel_id=1, replica_groups=mesh['dp'=2,'z'=4,'core'=2,'x'=4,'y'=4] {'z'}, dimensions={0} | all-to-all | bytes 262144 | tf_op jit(solution)/shard_map/all_to_all | solution.py:36
  (60 shorter events, 9.2 us)
Async XLA Ops:
  7.2 47.1 %all-gather.3.cloned.1.call-start = ((), (), s32[]{:S(2)}) async-start(), calls=%async_computation.5 | async-start | bytes 2359296 | tf_op jit(solution)/shard_map/all_gather | solution.py:311
  9.1 21.9 %copy-start.3 = (s32[512]{0:T(512)S(1)}, s32[512]{0:T(512)}, u32[]{:S(2)}) copy-start(s32[512]{0:T(512)} %param.11) | copy-start | bytes 6148
  9.1 21.9 %copy-start.6 = (f32[64]{0:T(128)S(1)}, f32[64]{0:T(128)}, u32[]{:S(2)}) copy-start(f32[64]{0:T(128)} %param.14) | copy-start | bytes 772
  9.1 22.0 %copy-start.4 = (s32[512]{0:T(512)S(1)}, s32[512]{0:T(512)}, u32[]{:S(2)}) copy-start(s32[512]{0:T(512)} %param.13) | copy-start | bytes 6148
  9.1 22.2 %copy-start.5 = (f32[512]{0:T(512)S(1)}, f32[512]{0:T(512)}, u32[]{:S(2)}) copy-start(f32[512]{0:T(512)} %param.15) | copy-start | bytes 6148
  9.1 45.4 %collective-permute-start.1 = (bf16[594,4096]{1,0:T(8,128)(2,1)}, bf16[594,4096]{1,0:T(8,128)(2,1)}, u32[]{:S(2)}, u32[]{:S(2)}) collective-permute-start(bf16[594,4096]{1,0:T(8,128)(2,1)} %bitcast.8), channel_id=1, source_target_pairs={{0,16},{16,0},{1,17},{17,1},{2,18},{18,2},{3,19},{19,3},{4,20},{20... | collective-permute-start | bytes 14598152 | tf_op jit(solution)/shard_map/ppermute | solution.py:47
  10.6 11.6 %all-to-all-start = ((bf16[4,64,128]{2,1,0:T(8,128)(2,1)}), bf16[4,64,128]{2,1,0:T(8,128)(2,1)S(1)}, u32[]{:S(2)}, u32[]{:S(2)}) async-start(bf16[4,64,128]{2,1,0:T(8,128)(2,1)} %broadcast_in_dim.44), calls=%async_computation | async-start | bytes 131072 | tf_op jit(solution)/shard_map/all_to_all | solution.py:43
  23.4 22.1 %all-to-all-start.1 = ((bf16[16,256,128]{2,1,0:T(8,128)(2,1)}), bf16[16,256,128]{2,1,0:T(8,128)(2,1)S(1)}, u32[]{:S(2)}, u32[]{:S(2)}) async-start(bf16[16,256,128]{2,1,0:T(8,128)(2,1)} %broadcast_in_dim.46), calls=%async_computation.1 | async-start | bytes 2097152 | tf_op jit(solution)/shard_map/all_to_all | solution.py:43
  30.9 70.4 %all-gather.5.cloned.1.call-start = ((), (), s32[]{:S(2)}) async-start(), calls=%async_computation.6 | async-start | bytes 2359296 | tf_op jit(solution)/shard_map/all_gather | solution.py:331
  32.6 7.7 %collective-permute-start = (f32[4,256]{1,0:T(4,128)S(1)}, f32[4,256]{1,0:T(4,128)S(1)}, u32[]{:S(2)}, u32[]{:S(2)}) collective-permute-start(f32[4,256]{1,0:T(4,128)S(1)} %select_n.27.info), channel_id=1, source_target_pairs={{0,128},{128,0},{1,129},{129,1},{2,130},{130,2},{3,131},{131,3},{4... | collective-permute-start | bytes 12296 | tf_op jit(solution)/shard_map/ppermute | solution.py:47
  63.0 3.7 %collective-permute-start.4 = (f32[4,256]{1,0:T(4,128)S(1)}, f32[4,256]{1,0:T(4,128)S(1)}, u32[]{:S(2)}, u32[]{:S(2)}) collective-permute-start(f32[4,256]{1,0:T(4,128)S(1)} %get-tuple-element.22), channel_id=1, source_target_pairs={{0,96},{32,0},{64,32},{96,64},{1,97},{33,1},{65,33},{97,65},{2,98}... | collective-permute-start | bytes 12296 | tf_op jit(solution)/shard_map/ppermute | solution.py:29
  65.4 4.6 %collective-permute-start.3 = (f32[4,256]{1,0:T(4,128)S(1)}, f32[4,256]{1,0:T(4,128)S(1)}, u32[]{:S(2)}, u32[]{:S(2)}) collective-permute-start(f32[4,256]{1,0:T(4,128)S(1)} %get-tuple-element.22), channel_id=1, source_target_pairs={{0,64},{32,96},{64,0},{96,32},{1,65},{33,97},{65,1},{97,33},{2,66}... | collective-permute-start | bytes 12296 | tf_op jit(solution)/shard_map/ppermute | solution.py:29
  65.4 5.6 %collective-permute-start.2 = (f32[4,256]{1,0:T(4,128)S(1)}, f32[4,256]{1,0:T(4,128)S(1)}, u32[]{:S(2)}, u32[]{:S(2)}) collective-permute-start(f32[4,256]{1,0:T(4,128)S(1)} %get-tuple-element.22), channel_id=1, source_target_pairs={{0,32},{32,64},{64,96},{96,0},{1,33},{33,65},{65,97},{97,1},{2,34}... | collective-permute-start | bytes 12296 | tf_op jit(solution)/shard_map/ppermute | solution.py:29
  84.4 16.9 %copy-start.2 = (bf16[512,2048]{1,0:T(8,128)(2,1)S(1)}, bf16[512,2048]{1,0:T(8,128)(2,1)}, u32[]{:S(2)}) copy-start(bf16[512,2048]{1,0:T(8,128)(2,1)} %all-gather.3.cloned.1.call-done.straight.refs_4_.refs_6_) | copy-start | bytes 6291460
  93.8 7.5 %collective-permute-start.5 = (f32[3,256]{1,0:T(4,128)S(1)}, f32[3,256]{1,0:T(4,128)S(1)}, u32[]{:S(2)}, u32[]{:S(2)}) collective-permute-start(f32[3,256]{1,0:T(4,128)S(1)} %get-tuple-element.29), channel_id=1, source_target_pairs={{0,128},{128,0},{1,129},{129,1},{2,130},{130,2},{3,131},{131,3},{4... | collective-permute-start | bytes 9224 | tf_op jit(solution)/shard_map/ppermute | solution.py:47
  101.3 17.2 %collective-permute-start.8 = (bf16[512,2048]{1,0:T(8,128)(2,1)S(1)}, bf16[512,2048]{1,0:T(8,128)(2,1)}, u32[]{:S(2)}, u32[]{:S(2)}) collective-permute-start(bf16[512,2048]{1,0:T(8,128)(2,1)S(1)} %copy-done.2), channel_id=1, source_target_pairs={{0,16},{16,0},{1,17},{17,1},{2,18},{18,2},{3,19},{19,3},{4,20},{20... | collective-permute-start | bytes 6291464 | tf_op jit(solution)/shard_map/ppermute | solution.py:47
  101.3 17.2 %collective-permute-start.9 = (bf16[512,2048]{1,0:T(8,128)(2,1)}, bf16[512,2048]{1,0:T(8,128)(2,1)}, u32[]{:S(2)}, u32[]{:S(2)}) collective-permute-start(bf16[512,2048]{1,0:T(8,128)(2,1)} %all-gather.5.cloned.1.call-done.straight2.refs_5_.refs_7_), channel_id=1, source_target_pairs={{0,16},{16,0},{1,17},{17,1},{2,18},{18,2},{3,19},{19,3},{4,20},{20... | collective-permute-start | bytes 6291464 | tf_op jit(solution)/shard_map/ppermute | solution.py:47
  101.8 5.8 %copy-start.7 = (bf16[594,256]{1,0:T(8,128)(2,1)S(1)}, bf16[594,256]{1,0:T(8,128)(2,1)}, u32[]{:S(2)}) copy-start(bf16[594,256]{1,0:T(8,128)(2,1)} %get-tuple-element.34) | copy-start | bytes 912388
  101.8 34.7 %all-to-all-start.3 = ((bf16[16,16,4096]{2,1,0:T(8,128)(2,1)}), bf16[16,16,4096]{2,1,0:T(8,128)(2,1)}, u32[]{:S(2)}, u32[]{:S(2)}) async-start(bf16[16,16,4096]{2,1,0:T(8,128)(2,1)} %bitcast.13), calls=%async_computation.3 | async-start | bytes 4194304 | tf_op jit(solution)/shard_map/all_to_all | solution.py:343
  107.7 10.9 %copy-start = (bf16[594,256]{1,0:T(8,128)(2,1)S(1)}, bf16[594,256]{1,0:T(8,128)(2,1)}, u32[]{:S(2)}) copy-start(bf16[594,256]{1,0:T(8,128)(2,1)} %get-tuple-element.26.refs_0_) | copy-start | bytes 912388
  107.7 9.4 %collective-permute-start.6 = (bf16[594,256]{1,0:T(8,128)(2,1)S(1)}, bf16[594,256]{1,0:T(8,128)(2,1)S(1)}, u32[]{:S(2)}, u32[]{:S(2)}) collective-permute-start(bf16[594,256]{1,0:T(8,128)(2,1)S(1)} %copy-done.7), channel_id=1, source_target_pairs={{0,16},{16,0},{1,17},{17,1},{2,18},{18,2},{3,19},{19,3},{4,20},{20... | collective-permute-start | bytes 912392 | tf_op jit(solution)/shard_map/ppermute | solution.py:47
  116.6 1.9 %collective-permute-start.7 = (bf16[594,256]{1,0:T(8,128)(2,1)}, bf16[594,256]{1,0:T(8,128)(2,1)S(1)}, u32[]{:S(2)}, u32[]{:S(2)}) collective-permute-start(bf16[594,256]{1,0:T(8,128)(2,1)} %get-tuple-element.35), channel_id=1, source_target_pairs={{0,16},{16,0},{1,17},{17,1},{2,18},{18,2},{3,19},{19,3},{4,20},{20... | collective-permute-start | bytes 912392 | tf_op jit(solution)/shard_map/ppermute | solution.py:47
  118.5 1.0 copy-start.1
Sparse Core Ops, SparseCore 0:
  9.8 44.4 all-gather.2
  56.0 39.6 all-gather.4

commit v7 on v6

--- a/solution.py
+++ b/solution.py
@@ -263,32 +263,35 @@
     )(scalars, target, info, final, *straights, *weights)
 
 
-def head_kernel(s, *refs):
-    out, count = refs[-1], (len(refs) - 1) // 3
-    grads, firsts, seconds = refs[:count], refs[count:-1:2], refs[count + 1 : -1 : 2]
-
-    def use(hiddens):
-        total = 0.0
-        for grad, hidden in zip(grads, hiddens):
-            total = total + jnp.dot(grad[...], hidden[...], preferred_element_type=jnp.float32)
-        out[...] = total.astype(jnp.bfloat16)
-
-    halves(lambda: use(firsts), lambda: use(seconds))
-
-
-def head_gradient(scalars, grads, hiddens):
+def head_kernel(s, *refs, count):
+    out, total = refs[-1], 0.0
+    for grad, hidden in zip(refs[:count], refs[count : 2 * count]):
+        total = total + jnp.dot(grad[...], hidden[...], preferred_element_type=jnp.float32)
+    out[...] = total.astype(jnp.bfloat16)
+
+
+def head_half(scalars, grads, hiddens, before=None):
     width, tokens = grads[0].shape
-    depth = 2 * hiddens[0][0].shape[1]
-    return call(
-        head_kernel,
-        "grad_head",
-        depth,
-        [whole(width, tokens)] * 4
-        + (hidden_specs(tokens, depth, 0) + hidden_specs(tokens, depth, 1)) * 2,
-        tiles(width),
-        jax.ShapeDtypeStruct((width, depth), jnp.bfloat16),
-        flops=8 * tokens * width * depth,
-    )(scalars, *grads, *[h for pair in hiddens for h in (*pair, *pair)])
+    half = hiddens[0].shape[1]
+    steps = half // TILE
+    skip = 0 if before is None else steps
+    extra = [] if before is None else [before]
+    rows = [pl.BlockSpec((tokens, TILE), lambda i, s, g=g: (s[g], i)) for g in (0, 1)]
+    return pl.pallas_call(
+        functools.partial(head_kernel, count=4),
+        grid_spec=pltpu.PrefetchScalarGridSpec(
+            num_scalar_prefetch=1,
+            grid=(steps,),
+            in_specs=[whole(width, tokens)] * 4
+            + rows * 2
+            + [pl.BlockSpec(memory_space=pl.ANY)] * len(extra),
+            out_specs=pl.BlockSpec((width, TILE), lambda i, s: (0, i + skip)),
+        ),
+        out_shape=pltpu.HBM((width, 2 * half), jnp.bfloat16),
+        input_output_aliases={9: 0} if extra else {},
+        compiler_params=PARAMS,
+        name="grad_head",
+    )(scalars, *grads, *[h for hidden in hiddens for h in (hidden, hidden)], *extra)
 
 
 def in_hbm(value):
@@ -341,19 +344,16 @@
         scalars, own_target, own, parts, logits, weights, nz, nv
     )
     got = lax.all_to_all(partial.reshape(nv, nz * rows, depth), ("x", "y"), 0, 0, tiled=True)
-    straight, straight2, final = lax.optimization_barrier(
-        (straight, straight2, swap(final, "dp"))
-    )
     gathered = (in_hbm(straight), in_hbm(straight2))
     other0, other1 = other_gradient(
-        scalars, other_target, other, final, gathered, weights
-    )
-    grad_head = head_gradient(
-        scalars,
-        (own0, other0, swap(own1, "core"), swap(other1, "core")),
-        (gathered, (in_hbm(swap(straight, "core")), in_hbm(swap(straight2, "core")))),
-    )
-    got, grad_head = lax.optimization_barrier((got, grad_head))
+        scalars, other_target, other, swap(final, "dp"), gathered, weights
+    )
+    grads = (own0, other0, swap(own1, "core"), swap(other1, "core"))
+    grad_head = head_half(scalars, grads, (gathered[0], in_hbm(swap(straight, "core"))))
+    got, straight2, grad_head = lax.optimization_barrier((got, straight2, grad_head))
+    grad_head = head_half(
+        scalars, grads, (gathered[1], in_hbm(swap(straight2, "core"))), grad_head
+    )
     got = jnp.sum(got.astype(f32), axis=0).astype(bf16)
     grad_hidden = scatter_sum(got.reshape(nz, rows, depth), "z").astype(bf16)
     return grad_hidden, grad_head.T

time: 156 us -> 153 us (0.981)
  blocking collectives: 21.5 us -> 9.82 us
  starting transfers between devices: 31.3 us -> 37.9 us
  Pallas kernels: 36.9 us -> 38.8 us
    all_to_all x1 -> x0, blocking collectives: 13.2 us -> none  [spread(): return lax.all_to_all(copies, axis, 0, 0, tiled=True)]
    all_to_all x2 -> x3, starting transfers between devices: 13.4 us -> 20.6 us  [spread(): return lax.all_to_all(copies, axis, 0, 0, tiled=True)]
    all_to_all x2 -> x3, waiting for transfers between devices: 9.48 us -> 16.4 us  [spread(): return lax.all_to_all(copies, axis, 0, 0, tiled=True)]
    all_to_all x1, waiting for transfers between devices: 6.77 us -> 0.01 us  [per_device(): lax.all_to_all(partial.reshape(nv, nz * rows, depth), ('x', 'y'), 0, 0, t...]
    pallas_call x1 -> x2, Pallas kernels: 10.3 us -> 12.2 us  [head_half(): pl.pallas_call(functools.partial(head_kernel, count=4), grid_spec=pltpu.P...]
  transfers between devices with their start and end apart: 15 -> 16, of which waited for: 10 -> 10; matrix products, arithmetic and copies ran while one was open for 4% -> 7% of each run, Pallas kernels for 24% -> 22%
where the time goes in v7:
time: 153 us; the launch traced here: 152 us
  waiting for transfers between devices  39.1 us (26%)
  Pallas kernels  38.8 us (25%)
  starting transfers between devices  37.9 us (25%)
  between operations  14.2 us (9%)
  blocking collectives  9.82 us (6%)
  local copies, waits for them, and re-layouts  7.83 us (5%)
  other arithmetic  4.18 us (3%)
    all_to_all x3, starting transfers between devices, spread(): return lax.all_to_all(copies, axis, 0, 0, tiled=True)  20.6 us
    all_to_all x3, waiting for transfers between devices, spread(): return lax.all_to_all(copies, axis, 0, 0, tiled=True)  16.4 us
    pallas_call x2, Pallas kernels, head_half(): pl.pallas_call(functools.partial(head_kernel, count=4), grid_spec=pltpu.P...  12.2 us
    all_to_all x1, blocking collectives, scatter_sum(): got = lax.all_to_all(parts, axis, 0, 0, tiled=True)  9.82 us
    pallas_call x1, Pallas kernels, gradient_partial(): call(functools.partial(gradient_kernel, nz=nz, nv=nv), 'grad_hidden_parti...  9.37 us
    ppermute x7, waiting for transfers between devices, swap(): return lax.ppermute(value, axis, [(0, 1), (1, 0)])  9.32 us
    pallas_call x1, Pallas kernels, other_gradient(): call(other_kernel, 'other_group_grad_logits', depth, [whole(1, tokens), w...  8.62 us
    pallas_call x1, Pallas kernels, logits_and_stats(): call(logits_kernel, 'logits', depth, [whole(1, tokens), hidden_specs(toke...  8.6 us
  transfers between devices with their start and end apart: 16, of which 10 were waited for; matrix products, arithmetic and copies ran while one was open for 7% of the time, Pallas kernels for 22%

profile of v7, /device:TPU:2, one launch (start us, length us, event | category | flops | bytes accessed | tf_op | source)
XLA Modules:
  0.0 151.9 jit_solution(11062555375213627094)
XLA Ops:
  7.3 1.9 %fusion.8 = (bf16[64,2048]{1,0:T(8,128)(2,1)}, bf16[64,2048]{1,0:T(8,128)(2,1)}) fusion(bf16[64,4096]{1,0:T(8,128)(2,1)} %param.8), kind=kLoop, calls=%fused_computation.36 | loop fusion | bytes 1048576 | tf_op jit(solution)/shard_map/slice | solution.py:314
  10.6 5.9 %all-to-all-start = ((bf16[4,64,128]{2,1,0:T(8,128)(2,1)}), bf16[4,64,128]{2,1,0:T(8,128)(2,1)S(1)}, u32[]{:S(2)}, u32[]{:S(2)}) async-start(bf16[4,64,128]{2,1,0:T(8,128)(2,1)} %broadcast_in_dim.44), calls=%async_computation | async-start | bytes 131072 | tf_op jit(solution)/shard_map/all_to_all | solution.py:43
  17.2 5.1 %all-to-all-done = bf16[4,64,128]{2,1,0:T(8,128)(2,1)S(1)} async-done(((bf16[4,64,128]{2,1,0:T(8,128)(2,1)}), bf16[4,64,128]{2,1,0:T(8,128)(2,1)S(1)}, u32[]{:S(2)}, u32[]{:S(2)}) %all-to-all-start) | async-done | bytes 65568 | tf_op jit(solution)/shard_map/all_to_all | solution.py:43
  22.3 1.2 broadcast_in_dim.46
  23.4 7.5 %all-to-all-start.1 = ((bf16[16,256,128]{2,1,0:T(8,128)(2,1)}), bf16[16,256,128]{2,1,0:T(8,128)(2,1)S(1)}, u32[]{:S(2)}, u32[]{:S(2)}) async-start(bf16[16,256,128]{2,1,0:T(8,128)(2,1)} %broadcast_in_dim.46), calls=%async_computation.1 | async-start | bytes 2097152 | tf_op jit(solution)/shard_map/all_to_all | solution.py:43
  32.7 4.6 %collective-permute-start = (f32[4,256]{1,0:T(4,128)S(1)}, f32[4,256]{1,0:T(4,128)S(1)}, u32[]{:S(2)}, u32[]{:S(2)}) collective-permute-start(f32[4,256]{1,0:T(4,128)S(1)} %select_n.27.info), channel_id=1, source_target_pairs={{0,128},{128,0},{1,129},{129,1},{2,130},{130,2},{3,131},{131,3},{4... | collective-permute-start | bytes 12296 | tf_op jit(solution)/shard_map/ppermute | solution.py:47
  37.4 3.0 %collective-permute-done.info = f32[4,256]{1,0:T(4,128)S(1)} collective-permute-done((f32[4,256]{1,0:T(4,128)S(1)}, f32[4,256]{1,0:T(4,128)S(1)}, u32[]{:S(2)}, u32[]{:S(2)}) %collective-permute-start) | collective-permute-done | bytes 4128 | tf_op jit(solution)/shard_map/ppermute | solution.py:47
  40.4 5.2 %all-to-all-done.1.pieces = bf16[16,256,128]{2,1,0:T(8,128)(2,1)S(1)} async-done(((bf16[16,256,128]{2,1,0:T(8,128)(2,1)}), bf16[16,256,128]{2,1,0:T(8,128)(2,1)S(1)}, u32[]{:S(2)}, u32[]{:S(2)}) %all-to-all-start.1) | async-done | bytes 1048608 | tf_op jit(solution)/shard_map/all_to_all | solution.py:43
  45.6 8.3 %all-gather.3.cloned.1.call-done.straight.refs_4_.refs_5_ = bf16[512,2048]{1,0:T(8,128)(2,1)} async-done(((bf16[64,2048]{1,0:T(8,128)(2,1)}), bf16[512,2048]{1,0:T(8,128)(2,1)}) %all-gather.3.cloned.1.call-update) | async-done | bytes 2097168 | tf_op jit(solution)/shard_map/all_gather | solution.py:314
  54.1 8.6 %logits.1 = (f32[594,256]{1,0:T(8,128)}, f32[594,256]{1,0:T(8,128)}, f32[4,256]{1,0:T(4,128)S(1)}) custom-call(s32[4]{0:T(128)S(1)} %pad_add_fusion.s, s32[1,256]{1,0:T(1,128)S(1)} %convert_element_type.26.target, bf16[512,2048]{1,0:T(8,128)(2,1)} %all-gather.3.cloned.1.call-done.straight.refs_4_.refs_5_, bf16[16,256,128]{2,1,0:T(8,128)(2,1)S(1)} %all-to-all-done.1.pieces, ...), custom_call_target="tpu_custom_call" | custom-call | flops 2491416576 | bytes 4982833 | tf_op jit(solution)/shard_map/logits/pallas_call | solution.py:144
  62.7 2.8 %collective-permute-start.4 = (f32[4,256]{1,0:T(4,128)S(1)}, f32[4,256]{1,0:T(4,128)S(1)}, u32[]{:S(2)}, u32[]{:S(2)}) collective-permute-start(f32[4,256]{1,0:T(4,128)S(1)} %get-tuple-element.20), channel_id=1, source_target_pairs={{0,96},{32,0},{64,32},{96,64},{1,97},{33,1},{65,33},{97,65},{2,98}... | collective-permute-start | bytes 12296 | tf_op jit(solution)/shard_map/ppermute | solution.py:29
  66.8 3.3 %collective-permute-done.3 = f32[4,256]{1,0:T(4,128)S(1)} collective-permute-done((f32[4,256]{1,0:T(4,128)S(1)}, f32[4,256]{1,0:T(4,128)S(1)}, u32[]{:S(2)}, u32[]{:S(2)}) %collective-permute-start.3) | collective-permute-done | bytes 4128 | tf_op jit(solution)/shard_map/ppermute | solution.py:29
  71.8 7.2 %all-to-all-start.2 = ((f32[16,4,256]{2,1,0:T(4,128)}), f32[16,4,256]{2,1,0:T(4,128)S(1)}, u32[]{:S(2)}, u32[]{:S(2)}) async-start(f32[16,4,256]{2,1,0:T(4,128)} %broadcast_in_dim.47), calls=%async_computation.2 | async-start | bytes 131072 | tf_op jit(solution)/shard_map/all_to_all | solution.py:43
  79.1 6.2 %all-to-all-done.2.parts = f32[16,4,256]{2,1,0:T(4,128)S(1)} async-done(((f32[16,4,256]{2,1,0:T(4,128)}), f32[16,4,256]{2,1,0:T(4,128)S(1)}, u32[]{:S(2)}, u32[]{:S(2)}) %all-to-all-start.2) | async-done | bytes 65568 | tf_op jit(solution)/shard_map/all_to_all | solution.py:43
  85.3 9.4 %grad_hidden_partial.1 = (bf16[256,4096]{1,0:T(8,128)(2,1)}, bf16[594,256]{1,0:T(8,128)(2,1)}, bf16[594,256]{1,0:T(8,128)(2,1)}, f32[3,256]{1,0:T(4,128)S(1)}) custom-call(s32[4]{0:T(128)S(1)} %pad_add_fusion.s, s32[1,256]{1,0:T(1,128)S(1)} %convert_element_type.26.target, f32[4,256]{1,0:T(4,128)S(1)} %select_n.27.info, ...), custom_call_target="tpu_custom_call" | custom-call | flops 2491416576 | bytes 4982833 | tf_op jit(solution)/shard_map/grad_hidden_partial/pallas_call | solution.py:211
  94.7 5.8 %all-to-all-start.3 = ((bf16[16,16,4096]{2,1,0:T(8,128)(2,1)}), bf16[16,16,4096]{2,1,0:T(8,128)(2,1)}, u32[]{:S(2)}, u32[]{:S(2)}) async-start(bf16[16,16,4096]{2,1,0:T(8,128)(2,1)} %bitcast.13), calls=%async_computation.3 | async-start | bytes 4194304 | tf_op jit(solution)/shard_map/all_to_all | solution.py:346
  100.5 2.9 %collective-permute-start.5 = (f32[3,256]{1,0:T(4,128)S(1)}, f32[3,256]{1,0:T(4,128)S(1)}, u32[]{:S(2)}, u32[]{:S(2)}) collective-permute-start(f32[3,256]{1,0:T(4,128)S(1)} %get-tuple-element.27), channel_id=1, source_target_pairs={{0,128},{128,0},{1,129},{129,1},{2,130},{130,2},{3,131},{131,3},{4... | collective-permute-start | bytes 9224 | tf_op jit(solution)/shard_map/ppermute | solution.py:47
  103.5 4.5 %collective-permute-done.5.final = f32[3,256]{1,0:T(4,128)S(1)} collective-permute-done((f32[3,256]{1,0:T(4,128)S(1)}, f32[3,256]{1,0:T(4,128)S(1)}, u32[]{:S(2)}, u32[]{:S(2)}) %collective-permute-start.5) | collective-permute-done | bytes 3104 | tf_op jit(solution)/shard_map/ppermute | solution.py:47
  108.0 8.6 %other_group_grad_logits.1 = (bf16[594,256]{1,0:T(8,128)(2,1)}, bf16[594,256]{1,0:T(8,128)(2,1)}) custom-call(s32[4]{0:T(128)S(1)} %pad_add_fusion.s, s32[1,256]{1,0:T(1,128)S(1)} %slice_convert_fusion.1.target, f32[4,256]{1,0:T(4,128)S(1)} %collective-permute-done.info, f32[3,256]{1,0:T(4,128)S(1)} %collective-permute-done.5.final, ...), custom_call_target="tpu_custom_call" | custom-call | flops 2491416576 | bytes 4982833 | tf_op jit(solution)/shard_map/other_group_grad_logits/pallas_call | solution.py:252
  116.7 1.8 %collective-permute-done.7.refs_3_ = bf16[594,256]{1,0:T(8,128)(2,1)S(1)} collective-permute-done((bf16[594,256]{1,0:T(8,128)(2,1)}, bf16[594,256]{1,0:T(8,128)(2,1)S(1)}, u32[]{:S(2)}, u32[]{:S(2)}) %collective-permute-start.7) | collective-permute-done | bytes 304160 | tf_op jit(solution)/shard_map/ppermute | solution.py:47
  119.4 6.2 %grad_head.2.refs_8_ = bf16[594,4096]{1,0:T(8,128)(2,1)} custom-call(s32[4]{0:T(128)S(1)} %pad_add_fusion.s, bf16[594,256]{1,0:T(8,128)(2,1)S(1)} %copy-done, bf16[594,256]{1,0:T(8,128)(2,1)S(1)} %copy-done.1, bf16[594,256]{1,0:T(8,128)(2,1)S(1)} %collective-permute-done.6.refs_2_, bf16[594,256]{1,0:T(8,128)(2,1)S(1)} %collective-permute-done.7.refs_3_, ...), custom_call_target="tpu_custom_call" | custom-call | tf_op jit(solution)/shard_map/grad_head/pallas_call | solution.py:280
  125.8 1.9 %reduce_sum.44 = bf16[16,4096]{1,0:T(8,128)(2,1)S(1)} reduce(bf16[16,16,4096]{2,1,0:T(8,128)(2,1)} %all-to-all-done.3, bf16[]{:T(256)} %constant.46.clone.1), dimensions={0}, to_apply=%region_2.3 | reduce | flops 983040 | bytes 2228226 | tf_op jit(solution)/shard_map/reduce_sum | solution.py:357
  128.4 9.8 %all_to_all.25 = bf16[4,4,4096]{2,1,0:T(4,128)(2,1)S(1)} all-to-all(bf16[4,4,4096]{2,1,0:T(4,128)(2,1)} %reshape.51), channel_id=1, replica_groups=mesh['dp'=2,'z'=4,'core'=2,'x'=4,'y'=4] {'z'}, dimensions={0} | all-to-all | bytes 262144 | tf_op jit(solution)/shard_map/all_to_all | solution.py:36
  138.9 6.1 %grad_head.3 = bf16[594,4096]{1,0:T(8,128)(2,1)} custom-call(s32[4]{0:T(128)S(1)} %pad_add_fusion.s, bf16[594,256]{1,0:T(8,128)(2,1)S(1)} %copy-done, bf16[594,256]{1,0:T(8,128)(2,1)S(1)} %copy-done.2, bf16[594,256]{1,0:T(8,128)(2,1)S(1)} %collective-permute-done.6.refs_2_, ...), custom_call_target="tpu_custom_call", output_to_operand_aliasing={{}: (9, {})} | custom-call | tf_op jit(solution)/shard_map/grad_head/pallas_call | solution.py:280
  (68 shorter events, 10.0 us)
Async XLA Ops:
  7.2 46.7 %all-gather.3.cloned.1.call-start = ((), (), s32[]{:S(2)}) async-start(), calls=%async_computation.5 | async-start | bytes 2359296 | tf_op jit(solution)/shard_map/all_gather | solution.py:314
  7.2 46.9 %collective-permute-start.1 = (bf16[594,4096]{1,0:T(8,128)(2,1)}, bf16[594,4096]{1,0:T(8,128)(2,1)}, u32[]{:S(2)}, u32[]{:S(2)}) collective-permute-start(bf16[594,4096]{1,0:T(8,128)(2,1)} %bitcast.8), channel_id=1, source_target_pairs={{0,16},{16,0},{1,17},{17,1},{2,18},{18,2},{3,19},{19,3},{4,20},{20... | collective-permute-start | bytes 14598152 | tf_op jit(solution)/shard_map/ppermute | solution.py:47
  9.2 21.8 %copy-start.5 = (s32[512]{0:T(512)S(1)}, s32[512]{0:T(512)}, u32[]{:S(2)}) copy-start(s32[512]{0:T(512)} %param.11) | copy-start | bytes 6148
  9.2 21.8 %copy-start.9 = (f32[64]{0:T(128)S(1)}, f32[64]{0:T(128)}, u32[]{:S(2)}) copy-start(f32[64]{0:T(128)} %param.14) | copy-start | bytes 772
  9.2 22.0 %copy-start.6 = (s32[512]{0:T(512)S(1)}, s32[512]{0:T(512)}, u32[]{:S(2)}) copy-start(s32[512]{0:T(512)} %param.13) | copy-start | bytes 6148
  9.2 22.1 %copy-start.7 = (f32[512]{0:T(512)S(1)}, f32[512]{0:T(512)}, u32[]{:S(2)}) copy-start(f32[512]{0:T(512)} %param.15) | copy-start | bytes 6148
  9.2 22.1 %copy-start.8 = (s32[512]{0:T(512)S(1)}, s32[512]{0:T(512)}, u32[]{:S(2)}) copy-start(s32[512]{0:T(512)} %param.10) | copy-start | bytes 6148
  10.6 11.6 %all-to-all-start = ((bf16[4,64,128]{2,1,0:T(8,128)(2,1)}), bf16[4,64,128]{2,1,0:T(8,128)(2,1)S(1)}, u32[]{:S(2)}, u32[]{:S(2)}) async-start(bf16[4,64,128]{2,1,0:T(8,128)(2,1)} %broadcast_in_dim.44), calls=%async_computation | async-start | bytes 131072 | tf_op jit(solution)/shard_map/all_to_all | solution.py:43
  23.4 22.1 %all-to-all-start.1 = ((bf16[16,256,128]{2,1,0:T(8,128)(2,1)}), bf16[16,256,128]{2,1,0:T(8,128)(2,1)S(1)}, u32[]{:S(2)}, u32[]{:S(2)}) async-start(bf16[16,256,128]{2,1,0:T(8,128)(2,1)} %broadcast_in_dim.46), calls=%async_computation.1 | async-start | bytes 2097152 | tf_op jit(solution)/shard_map/all_to_all | solution.py:43
  30.9 77.1 %all-gather.5.cloned.1.call-start = ((), (), s32[]{:S(2)}) async-start(), calls=%async_computation.6 | async-start | bytes 2359296 | tf_op jit(solution)/shard_map/all_gather | solution.py:334
  32.7 7.6 %collective-permute-start = (f32[4,256]{1,0:T(4,128)S(1)}, f32[4,256]{1,0:T(4,128)S(1)}, u32[]{:S(2)}, u32[]{:S(2)}) collective-permute-start(f32[4,256]{1,0:T(4,128)S(1)} %select_n.27.info), channel_id=1, source_target_pairs={{0,128},{128,0},{1,129},{129,1},{2,130},{130,2},{3,131},{131,3},{4... | collective-permute-start | bytes 12296 | tf_op jit(solution)/shard_map/ppermute | solution.py:47
  54.1 24.9 %copy-start.3 = (bf16[512,2048]{1,0:T(8,128)(2,1)S(1)}, bf16[512,2048]{1,0:T(8,128)(2,1)}, u32[]{:S(2)}) copy-start(bf16[512,2048]{1,0:T(8,128)(2,1)} %all-gather.3.cloned.1.call-done.straight.refs_4_.refs_5_) | copy-start | bytes 6291460
  62.7 4.1 %collective-permute-start.4 = (f32[4,256]{1,0:T(4,128)S(1)}, f32[4,256]{1,0:T(4,128)S(1)}, u32[]{:S(2)}, u32[]{:S(2)}) collective-permute-start(f32[4,256]{1,0:T(4,128)S(1)} %get-tuple-element.20), channel_id=1, source_target_pairs={{0,96},{32,0},{64,32},{96,64},{1,97},{33,1},{65,33},{97,65},{2,98}... | collective-permute-start | bytes 12296 | tf_op jit(solution)/shard_map/ppermute | solution.py:29
  65.5 4.6 %collective-permute-start.3 = (f32[4,256]{1,0:T(4,128)S(1)}, f32[4,256]{1,0:T(4,128)S(1)}, u32[]{:S(2)}, u32[]{:S(2)}) collective-permute-start(f32[4,256]{1,0:T(4,128)S(1)} %get-tuple-element.20), channel_id=1, source_target_pairs={{0,64},{32,96},{64,0},{96,32},{1,65},{33,97},{65,1},{97,33},{2,66}... | collective-permute-start | bytes 12296 | tf_op jit(solution)/shard_map/ppermute | solution.py:29
  65.6 5.5 %collective-permute-start.2 = (f32[4,256]{1,0:T(4,128)S(1)}, f32[4,256]{1,0:T(4,128)S(1)}, u32[]{:S(2)}, u32[]{:S(2)}) collective-permute-start(f32[4,256]{1,0:T(4,128)S(1)} %get-tuple-element.20), channel_id=1, source_target_pairs={{0,32},{32,64},{64,96},{96,0},{1,33},{33,65},{65,97},{97,1},{2,34}... | collective-permute-start | bytes 12296 | tf_op jit(solution)/shard_map/ppermute | solution.py:29
  71.8 13.5 %all-to-all-start.2 = ((f32[16,4,256]{2,1,0:T(4,128)}), f32[16,4,256]{2,1,0:T(4,128)S(1)}, u32[]{:S(2)}, u32[]{:S(2)}) async-start(f32[16,4,256]{2,1,0:T(4,128)} %broadcast_in_dim.47), calls=%async_computation.2 | async-start | bytes 131072 | tf_op jit(solution)/shard_map/all_to_all | solution.py:43
  79.0 37.6 %collective-permute-start.8 = (bf16[512,2048]{1,0:T(8,128)(2,1)S(1)}, bf16[512,2048]{1,0:T(8,128)(2,1)}, u32[]{:S(2)}, u32[]{:S(2)}) collective-permute-start(bf16[512,2048]{1,0:T(8,128)(2,1)S(1)} %copy-done.3), channel_id=1, source_target_pairs={{0,16},{16,0},{1,17},{17,1},{2,18},{18,2},{3,19},{19,3},{4,20},{20... | collective-permute-start | bytes 6291464 | tf_op jit(solution)/shard_map/ppermute | solution.py:47
  94.7 30.9 %all-to-all-start.3 = ((bf16[16,16,4096]{2,1,0:T(8,128)(2,1)}), bf16[16,16,4096]{2,1,0:T(8,128)(2,1)}, u32[]{:S(2)}, u32[]{:S(2)}) async-start(bf16[16,16,4096]{2,1,0:T(8,128)(2,1)} %bitcast.13), calls=%async_computation.3 | async-start | bytes 4194304 | tf_op jit(solution)/shard_map/all_to_all | solution.py:346
  100.5 7.5 %collective-permute-start.5 = (f32[3,256]{1,0:T(4,128)S(1)}, f32[3,256]{1,0:T(4,128)S(1)}, u32[]{:S(2)}, u32[]{:S(2)}) collective-permute-start(f32[3,256]{1,0:T(4,128)S(1)} %get-tuple-element.27), channel_id=1, source_target_pairs={{0,128},{128,0},{1,129},{129,1},{2,130},{130,2},{3,131},{131,3},{4... | collective-permute-start | bytes 9224 | tf_op jit(solution)/shard_map/ppermute | solution.py:47
  103.4 15.0 %copy-start = (bf16[594,256]{1,0:T(8,128)(2,1)S(1)}, bf16[594,256]{1,0:T(8,128)(2,1)}, u32[]{:S(2)}) copy-start(bf16[594,256]{1,0:T(8,128)(2,1)} %get-tuple-element.25.refs_0_) | copy-start | bytes 912388
  103.4 13.2 %collective-permute-start.6 = (bf16[594,256]{1,0:T(8,128)(2,1)S(1)}, bf16[594,256]{1,0:T(8,128)(2,1)S(1)}, u32[]{:S(2)}, u32[]{:S(2)}) collective-permute-start(bf16[594,256]{1,0:T(8,128)(2,1)S(1)} %copy-done.10), channel_id=1, source_target_pairs={{0,16},{16,0},{1,17},{17,1},{2,18},{18,2},{3,19},{19,3},{4,20},{20... | collective-permute-start | bytes 912392 | tf_op jit(solution)/shard_map/ppermute | solution.py:47
  116.6 1.8 %collective-permute-start.7 = (bf16[594,256]{1,0:T(8,128)(2,1)}, bf16[594,256]{1,0:T(8,128)(2,1)S(1)}, u32[]{:S(2)}, u32[]{:S(2)}) collective-permute-start(bf16[594,256]{1,0:T(8,128)(2,1)} %get-tuple-element.30), channel_id=1, source_target_pairs={{0,16},{16,0},{1,17},{17,1},{2,18},{18,2},{3,19},{19,3},{4,20},{20... | collective-permute-start | bytes 912392 | tf_op jit(solution)/shard_map/ppermute | solution.py:47
  125.6 13.4 %copy-start.2 = (bf16[594,256]{1,0:T(8,128)(2,1)S(1)}, bf16[594,256]{1,0:T(8,128)(2,1)}, u32[]{:S(2)}) copy-start(bf16[594,256]{1,0:T(8,128)(2,1)} %get-tuple-element.28.refs_1_) | copy-start | bytes 912388
  125.6 13.3 %collective-permute-start.9 = (bf16[512,2048]{1,0:T(8,128)(2,1)S(1)}, bf16[512,2048]{1,0:T(8,128)(2,1)}, u32[]{:S(2)}, u32[]{:S(2)}) collective-permute-start(bf16[512,2048]{1,0:T(8,128)(2,1)S(1)} %copy-done.4), channel_id=1, source_target_pairs={{0,16},{16,0},{1,17},{17,1},{2,18},{18,2},{3,19},{19,3},{4,20},{20... | collective-permute-start | bytes 6291464 | tf_op jit(solution)/shard_map/ppermute | solution.py:47
  (3 other events, 15.9 us)
Sparse Core Ops, SparseCore 0:
  9.8 44.0 all-gather.2
  55.7 39.8 all-gather.4

commit v8 on v7

--- a/solution.py
+++ b/solution.py
@@ -32,11 +32,6 @@
     return [stats] + others
 
 
-def scatter_sum(parts, axis):
-    got = lax.all_to_all(parts, axis, 0, 0, tiled=True)
-    return jnp.sum(got.astype(jnp.float32), axis=0)
-
-
 def spread(value, axis):
     count = lax.axis_size(axis)
     copies = jnp.broadcast_to(value[None], (count,) + value.shape)
@@ -47,7 +42,8 @@
     return lax.ppermute(value, axis, [(0, 1), (1, 0)])
 
 
-TILE = 1024
+TILE = 2048
+HEAD_TILE = 1024
 PARAMS = pltpu.CompilerParams(vmem_limit_bytes=24 * 2**20)
 
 
@@ -273,10 +269,10 @@
 def head_half(scalars, grads, hiddens, before=None):
     width, tokens = grads[0].shape
     half = hiddens[0].shape[1]
-    steps = half // TILE
+    steps = half // HEAD_TILE
     skip = 0 if before is None else steps
     extra = [] if before is None else [before]
-    rows = [pl.BlockSpec((tokens, TILE), lambda i, s, g=g: (s[g], i)) for g in (0, 1)]
+    rows = [pl.BlockSpec((tokens, HEAD_TILE), lambda i, s, g=g: (s[g], i)) for g in (0, 1)]
     return pl.pallas_call(
         functools.partial(head_kernel, count=4),
         grid_spec=pltpu.PrefetchScalarGridSpec(
@@ -285,7 +281,7 @@
             in_specs=[whole(width, tokens)] * 4
             + rows * 2
             + [pl.BlockSpec(memory_space=pl.ANY)] * len(extra),
-            out_specs=pl.BlockSpec((width, TILE), lambda i, s: (0, i + skip)),
+            out_specs=pl.BlockSpec((width, HEAD_TILE), lambda i, s: (0, i + skip)),
         ),
         out_shape=pltpu.HBM((width, 2 * half), jnp.bfloat16),
         input_output_aliases={9: 0} if extra else {},
@@ -348,14 +344,30 @@
     other0, other1 = other_gradient(
         scalars, other_target, other, swap(final, "dp"), gathered, weights
     )
-    grads = (own0, other0, swap(own1, "core"), swap(other1, "core"))
+    grads = [
+        in_hbm(grad) for grad in (own0, other0, swap(own1, "core"), swap(other1, "core"))
+    ]
     grad_head = head_half(scalars, grads, (gathered[0], in_hbm(swap(straight, "core"))))
     got, straight2, grad_head = lax.optimization_barrier((got, straight2, grad_head))
     grad_head = head_half(
         scalars, grads, (gathered[1], in_hbm(swap(straight2, "core"))), grad_head
     )
     got = jnp.sum(got.astype(f32), axis=0).astype(bf16)
-    grad_hidden = scatter_sum(got.reshape(nz, rows, depth), "z").astype(bf16)
+
+    def block_for(index):
+        return lax.dynamic_slice_in_dim(got, index * rows, rows, 0)
+
+    received = [
+        lax.ppermute(
+            block_for((z + step) % nz), "z", [(i, (i + step) % nz) for i in range(nz)]
+        )
+        for step in range(1, nz)
+    ]
+    received, grad_head = lax.optimization_barrier((received, grad_head))
+    grad_hidden = block_for(z).astype(f32)
+    for part in received:
+        grad_hidden = grad_hidden + part.astype(f32)
+    grad_hidden = grad_hidden.astype(bf16)
     return grad_hidden, grad_head.T
 
 

time: 153 us -> 146 us (0.954)
  blocking collectives: 9.82 us -> 0 us
  starting transfers between devices: 37.9 us -> 42.1 us
    all_to_all x1 -> x0, blocking collectives: 9.82 us -> none  [scatter_sum(): got = lax.all_to_all(parts, axis, 0, 0, tiled=True)]
    ppermute x0 -> x3, starting transfers between devices: none -> 4.1 us  [per_device(): lax.ppermute(block_for((z + step) % nz), 'z', [(i, (i + step) % nz) for i...]
  transfers between devices with their start and end apart: 16 -> 19, of which waited for: 10 -> 10; matrix products, arithmetic and copies ran while one was open for 7% -> 7% of each run, Pallas kernels for 22% -> 27%
where the time goes in v8:
time: 146 us; the launch traced here: 145 us
  starting transfers between devices  42.1 us (29%)
  waiting for transfers between devices  39 us (27%)
  Pallas kernels  38.4 us (26%)
  between operations  14.2 us (10%)
  local copies, waits for them, and re-layouts  6.92 us (5%)
  other arithmetic  4.17 us (3%)
    all_to_all x3, starting transfers between devices, spread(): return lax.all_to_all(copies, axis, 0, 0, tiled=True)  20.7 us
    all_to_all x3, waiting for transfers between devices, spread(): return lax.all_to_all(copies, axis, 0, 0, tiled=True)  16.4 us
    pallas_call x2, Pallas kernels, head_half(): pl.pallas_call(functools.partial(head_kernel, count=4), grid_spec=pltpu.P...  13.3 us
    ppermute x7, waiting for transfers between devices, swap(): return lax.ppermute(value, axis, [(0, 1), (1, 0)])  9.36 us
    pallas_call x1, Pallas kernels, gradient_partial(): call(functools.partial(gradient_kernel, nz=nz, nv=nv), 'grad_hidden_parti...  8.85 us
    all_gather x1, waiting for transfers between devices, per_device(): straight = lax.all_gather(hidden[:, :half], ('dp', 'z'), axis=0, tiled=True)  8.3 us
    pallas_call x1, Pallas kernels, other_gradient(): call(other_kernel, 'other_group_grad_logits', depth, [whole(1, tokens), w...  8.14 us
    pallas_call x1, Pallas kernels, logits_and_stats(): call(logits_kernel, 'logits', depth, [whole(1, tokens), hidden_specs(toke...  8.11 us
  transfers between devices with their start and end apart: 19, of which 10 were waited for; matrix products, arithmetic and copies ran while one was open for 7% of the time, Pallas kernels for 27%

profile of v8, /device:TPU:2, one launch (start us, length us, event | category | flops | bytes accessed | tf_op | source)
XLA Modules:
  0.0 144.8 jit_solution(11525848430206956651)
XLA Ops:
  7.3 1.9 %fusion.8 = (bf16[64,2048]{1,0:T(8,128)(2,1)}, bf16[64,2048]{1,0:T(8,128)(2,1)}) fusion(bf16[64,4096]{1,0:T(8,128)(2,1)} %param.8), kind=kLoop, calls=%fused_computation.40 | loop fusion | bytes 1048576 | tf_op jit(solution)/shard_map/slice | solution.py:310
  10.6 5.9 %all-to-all-start = ((bf16[4,64,128]{2,1,0:T(8,128)(2,1)}), bf16[4,64,128]{2,1,0:T(8,128)(2,1)S(1)}, u32[]{:S(2)}, u32[]{:S(2)}) async-start(bf16[4,64,128]{2,1,0:T(8,128)(2,1)} %broadcast_in_dim.44), calls=%async_computation | async-start | bytes 131072 | tf_op jit(solution)/shard_map/all_to_all | solution.py:38
  17.2 5.1 %all-to-all-done = bf16[4,64,128]{2,1,0:T(8,128)(2,1)S(1)} async-done(((bf16[4,64,128]{2,1,0:T(8,128)(2,1)}), bf16[4,64,128]{2,1,0:T(8,128)(2,1)S(1)}, u32[]{:S(2)}, u32[]{:S(2)}) %all-to-all-start) | async-done | bytes 65568 | tf_op jit(solution)/shard_map/all_to_all | solution.py:38
  23.4 7.5 %all-to-all-start.1 = ((bf16[16,256,128]{2,1,0:T(8,128)(2,1)}), bf16[16,256,128]{2,1,0:T(8,128)(2,1)S(1)}, u32[]{:S(2)}, u32[]{:S(2)}) async-start(bf16[16,256,128]{2,1,0:T(8,128)(2,1)} %broadcast_in_dim.46), calls=%async_computation.1 | async-start | bytes 2097152 | tf_op jit(solution)/shard_map/all_to_all | solution.py:38
  32.7 4.6 %collective-permute-start = (f32[4,256]{1,0:T(4,128)S(1)}, f32[4,256]{1,0:T(4,128)S(1)}, u32[]{:S(2)}, u32[]{:S(2)}) collective-permute-start(f32[4,256]{1,0:T(4,128)S(1)} %select_n.54.info), channel_id=1, source_target_pairs={{0,128},{128,0},{1,129},{129,1},{2,130},{130,2},{3,131},{131,3},{4... | collective-permute-start | bytes 12296 | tf_op jit(solution)/shard_map/ppermute | solution.py:42
  37.4 3.0 %collective-permute-done.info = f32[4,256]{1,0:T(4,128)S(1)} collective-permute-done((f32[4,256]{1,0:T(4,128)S(1)}, f32[4,256]{1,0:T(4,128)S(1)}, u32[]{:S(2)}, u32[]{:S(2)}) %collective-permute-start) | collective-permute-done | bytes 4128 | tf_op jit(solution)/shard_map/ppermute | solution.py:42
  40.4 5.2 %all-to-all-done.1.pieces = bf16[16,256,128]{2,1,0:T(8,128)(2,1)S(1)} async-done(((bf16[16,256,128]{2,1,0:T(8,128)(2,1)}), bf16[16,256,128]{2,1,0:T(8,128)(2,1)S(1)}, u32[]{:S(2)}, u32[]{:S(2)}) %all-to-all-start.1) | async-done | bytes 1048608 | tf_op jit(solution)/shard_map/all_to_all | solution.py:38
  45.6 8.3 %all-gather.3.cloned.1.call-done.straight.refs_4_.refs_5_ = bf16[512,2048]{1,0:T(8,128)(2,1)} async-done(((bf16[64,2048]{1,0:T(8,128)(2,1)}), bf16[512,2048]{1,0:T(8,128)(2,1)}) %all-gather.3.cloned.1.call-update) | async-done | bytes 2097168 | tf_op jit(solution)/shard_map/all_gather | solution.py:310
  54.1 8.1 %logits.1 = (f32[594,256]{1,0:T(8,128)}, f32[594,256]{1,0:T(8,128)}, f32[4,256]{1,0:T(4,128)S(1)}) custom-call(s32[4]{0:T(128)S(1)} %pad_add_fusion.s, s32[1,256]{1,0:T(1,128)S(1)} %convert_element_type.39.target, bf16[512,2048]{1,0:T(8,128)(2,1)} %all-gather.3.cloned.1.call-done.straight.refs_4_.refs_5_, bf16[16,256,128]{2,1,0:T(8,128)(2,1)S(1)} %all-to-all-done.1.pieces, ...), custom_call_target="tpu_custom_call" | custom-call | flops 2491416576 | bytes 4982833 | tf_op jit(solution)/shard_map/logits/pallas_call | solution.py:140
  62.2 2.6 %collective-permute-start.4 = (f32[4,256]{1,0:T(4,128)S(1)}, f32[4,256]{1,0:T(4,128)S(1)}, u32[]{:S(2)}, u32[]{:S(2)}) collective-permute-start(f32[4,256]{1,0:T(4,128)S(1)} %get-tuple-element.24), channel_id=1, source_target_pairs={{0,96},{32,0},{64,32},{96,64},{1,97},{33,1},{65,33},{97,65},{2,98}... | collective-permute-start | bytes 12296 | tf_op jit(solution)/shard_map/ppermute | solution.py:29
  66.2 3.3 %collective-permute-done.3 = f32[4,256]{1,0:T(4,128)S(1)} collective-permute-done((f32[4,256]{1,0:T(4,128)S(1)}, f32[4,256]{1,0:T(4,128)S(1)}, u32[]{:S(2)}, u32[]{:S(2)}) %collective-permute-start.3) | collective-permute-done | bytes 4128 | tf_op jit(solution)/shard_map/ppermute | solution.py:29
  71.1 7.4 %all-to-all-start.2 = ((f32[16,4,256]{2,1,0:T(4,128)}), f32[16,4,256]{2,1,0:T(4,128)S(1)}, u32[]{:S(2)}, u32[]{:S(2)}) async-start(f32[16,4,256]{2,1,0:T(4,128)} %broadcast_in_dim.47), calls=%async_computation.2 | async-start | bytes 131072 | tf_op jit(solution)/shard_map/all_to_all | solution.py:38
  78.6 6.2 %all-to-all-done.2.parts = f32[16,4,256]{2,1,0:T(4,128)S(1)} async-done(((f32[16,4,256]{2,1,0:T(4,128)}), f32[16,4,256]{2,1,0:T(4,128)S(1)}, u32[]{:S(2)}, u32[]{:S(2)}) %all-to-all-start.2) | async-done | bytes 65568 | tf_op jit(solution)/shard_map/all_to_all | solution.py:38
  84.8 8.9 %grad_hidden_partial.1 = (bf16[256,4096]{1,0:T(8,128)(2,1)}, bf16[594,256]{1,0:T(8,128)(2,1)}, bf16[594,256]{1,0:T(8,128)(2,1)}, f32[3,256]{1,0:T(4,128)S(1)}) custom-call(s32[4]{0:T(128)S(1)} %pad_add_fusion.s, s32[1,256]{1,0:T(1,128)S(1)} %convert_element_type.39.target, f32[4,256]{1,0:T(4,128)S(1)} %select_n.54.info, ...), custom_call_target="tpu_custom_call" | custom-call | flops 2491416576 | bytes 4982833 | tf_op jit(solution)/shard_map/grad_hidden_partial/pallas_call | solution.py:207
  93.6 5.8 %all-to-all-start.3 = ((bf16[16,16,4096]{2,1,0:T(8,128)(2,1)}), bf16[16,16,4096]{2,1,0:T(8,128)(2,1)}, u32[]{:S(2)}, u32[]{:S(2)}) async-start(bf16[16,16,4096]{2,1,0:T(8,128)(2,1)} %bitcast.13), calls=%async_computation.3 | async-start | bytes 4194304 | tf_op jit(solution)/shard_map/all_to_all | solution.py:342
  99.4 2.9 %collective-permute-start.5 = (f32[3,256]{1,0:T(4,128)S(1)}, f32[3,256]{1,0:T(4,128)S(1)}, u32[]{:S(2)}, u32[]{:S(2)}) collective-permute-start(f32[3,256]{1,0:T(4,128)S(1)} %get-tuple-element.31), channel_id=1, source_target_pairs={{0,128},{128,0},{1,129},{129,1},{2,130},{130,2},{3,131},{131,3},{4... | collective-permute-start | bytes 9224 | tf_op jit(solution)/shard_map/ppermute | solution.py:42
  102.4 4.6 %collective-permute-done.5.final = f32[3,256]{1,0:T(4,128)S(1)} collective-permute-done((f32[3,256]{1,0:T(4,128)S(1)}, f32[3,256]{1,0:T(4,128)S(1)}, u32[]{:S(2)}, u32[]{:S(2)}) %collective-permute-start.5) | collective-permute-done | bytes 3104 | tf_op jit(solution)/shard_map/ppermute | solution.py:42
  107.0 8.1 %other_group_grad_logits.1 = (bf16[594,256]{1,0:T(8,128)(2,1)}, bf16[594,256]{1,0:T(8,128)(2,1)}) custom-call(s32[4]{0:T(128)S(1)} %pad_add_fusion.s, s32[1,256]{1,0:T(1,128)S(1)} %slice_convert_fusion.1.target, f32[4,256]{1,0:T(4,128)S(1)} %collective-permute-done.info, f32[3,256]{1,0:T(4,128)S(1)} %collective-permute-done.5.final, ...), custom_call_target="tpu_custom_call" | custom-call | flops 2491416576 | bytes 4982833 | tf_op jit(solution)/shard_map/other_group_grad_logits/pallas_call | solution.py:248
  115.1 1.8 %collective-permute-done.7.refs_3_ = bf16[594,256]{1,0:T(8,128)(2,1)S(1)} collective-permute-done((bf16[594,256]{1,0:T(8,128)(2,1)}, bf16[594,256]{1,0:T(8,128)(2,1)S(1)}, u32[]{:S(2)}, u32[]{:S(2)}) %collective-permute-start.7) | collective-permute-done | bytes 304160 | tf_op jit(solution)/shard_map/ppermute | solution.py:42
  117.7 6.7 %grad_head.2.refs_8_ = bf16[594,4096]{1,0:T(8,128)(2,1)} custom-call(s32[4]{0:T(128)S(1)} %pad_add_fusion.s, bf16[594,256]{1,0:T(8,128)(2,1)} %get-tuple-element.29.refs_0_, bf16[594,256]{1,0:T(8,128)(2,1)} %get-tuple-element.32.refs_1_, bf16[594,256]{1,0:T(8,128)(2,1)} %copy-done.2, bf16[594,256]{1,0:T(8,128)(2,1)} %copy-done.3, ...), custom_call_target="tpu_custom_call" | custom-call | tf_op jit(solution)/shard_map/grad_head/pallas_call | solution.py:276
  124.6 1.9 %reduce_sum.32 = bf16[16,4096]{1,0:T(8,128)(2,1)S(1)} reduce(bf16[16,16,4096]{2,1,0:T(8,128)(2,1)} %all-to-all-done.3, bf16[]{:T(256)} %constant.63.clone.1), dimensions={0}, to_apply=%region_2.3 | reduce | flops 983040 | bytes 2228226 | tf_op jit(solution)/shard_map/reduce_sum | solution.py:355
  126.6 1.2 collective-permute-start.10
  127.8 2.8 %collective-permute-start.11 = (bf16[4,4096]{1,0:T(4,128)(2,1)S(1)}, bf16[4,4096]{1,0:T(4,128)(2,1)S(1)}, u32[]{:S(2)}, u32[]{:S(2)}) collective-permute-start(bf16[4,4096]{1,0:T(4,128)(2,1)S(1)} %get-tuple-element.50), channel_id=1, source_target_pairs={{0,96},{32,0},{64,32},{96,64},{1,97},{33,1},{65,33},{97,65},{2,98}... | collective-permute-start | bytes 98312 | tf_op jit(solution)/shard_map/ppermute | solution.py:361
  130.7 6.6 %grad_head.3 = bf16[594,4096]{1,0:T(8,128)(2,1)} custom-call(s32[4]{0:T(128)S(1)} %pad_add_fusion.s, bf16[594,256]{1,0:T(8,128)(2,1)} %get-tuple-element.29.refs_0_, bf16[594,256]{1,0:T(8,128)(2,1)} %get-tuple-element.32.refs_1_, bf16[594,256]{1,0:T(8,128)(2,1)} %copy-done.2, bf16[594,256]{1,0:T(8,128)(2,1)} %copy-done.3, ...), custom_call_target="tpu_custom_call", output_to_operand_aliasing={{}: (9, {})} | custom-call | tf_op jit(solution)/shard_map/grad_head/pallas_call | solution.py:276
  (71 shorter events, 10.3 us)
Async XLA Ops:
  7.2 46.7 %all-gather.3.cloned.1.call-start = ((), (), s32[]{:S(2)}) async-start(), calls=%async_computation.4 | async-start | bytes 2359296 | tf_op jit(solution)/shard_map/all_gather | solution.py:310
  7.2 46.9 %collective-permute-start.1 = (bf16[594,4096]{1,0:T(8,128)(2,1)}, bf16[594,4096]{1,0:T(8,128)(2,1)}, u32[]{:S(2)}, u32[]{:S(2)}) collective-permute-start(bf16[594,4096]{1,0:T(8,128)(2,1)} %bitcast.8), channel_id=1, source_target_pairs={{0,16},{16,0},{1,17},{17,1},{2,18},{18,2},{3,19},{19,3},{4,20},{20... | collective-permute-start | bytes 14598152 | tf_op jit(solution)/shard_map/ppermute | solution.py:42
  9.2 21.8 %copy-start.8 = (f32[64]{0:T(128)S(1)}, f32[64]{0:T(128)}, u32[]{:S(2)}) copy-start(f32[64]{0:T(128)} %param.14) | copy-start | bytes 772
  9.2 22.0 %copy-start.5 = (s32[512]{0:T(512)S(1)}, s32[512]{0:T(512)}, u32[]{:S(2)}) copy-start(s32[512]{0:T(512)} %param.13) | copy-start | bytes 6148
  9.2 22.1 %copy-start.6 = (f32[512]{0:T(512)S(1)}, f32[512]{0:T(512)}, u32[]{:S(2)}) copy-start(f32[512]{0:T(512)} %param.15) | copy-start | bytes 6148
  9.2 22.1 %copy-start.7 = (s32[512]{0:T(512)S(1)}, s32[512]{0:T(512)}, u32[]{:S(2)}) copy-start(s32[512]{0:T(512)} %param.10) | copy-start | bytes 6148
  10.6 11.6 %all-to-all-start = ((bf16[4,64,128]{2,1,0:T(8,128)(2,1)}), bf16[4,64,128]{2,1,0:T(8,128)(2,1)S(1)}, u32[]{:S(2)}, u32[]{:S(2)}) async-start(bf16[4,64,128]{2,1,0:T(8,128)(2,1)} %broadcast_in_dim.44), calls=%async_computation | async-start | bytes 131072 | tf_op jit(solution)/shard_map/all_to_all | solution.py:38
  23.4 22.1 %all-to-all-start.1 = ((bf16[16,256,128]{2,1,0:T(8,128)(2,1)}), bf16[16,256,128]{2,1,0:T(8,128)(2,1)S(1)}, u32[]{:S(2)}, u32[]{:S(2)}) async-start(bf16[16,256,128]{2,1,0:T(8,128)(2,1)} %broadcast_in_dim.46), calls=%async_computation.1 | async-start | bytes 2097152 | tf_op jit(solution)/shard_map/all_to_all | solution.py:38
  30.9 76.1 %all-gather.5.cloned.1.call-start = ((), (), s32[]{:S(2)}) async-start(), calls=%async_computation.5 | async-start | bytes 2359296 | tf_op jit(solution)/shard_map/all_gather | solution.py:330
  32.7 7.6 %collective-permute-start = (f32[4,256]{1,0:T(4,128)S(1)}, f32[4,256]{1,0:T(4,128)S(1)}, u32[]{:S(2)}, u32[]{:S(2)}) collective-permute-start(f32[4,256]{1,0:T(4,128)S(1)} %select_n.54.info), channel_id=1, source_target_pairs={{0,128},{128,0},{1,129},{129,1},{2,130},{130,2},{3,131},{131,3},{4... | collective-permute-start | bytes 12296 | tf_op jit(solution)/shard_map/ppermute | solution.py:42
  54.1 24.4 %copy-start = (bf16[512,2048]{1,0:T(8,128)(2,1)S(1)}, bf16[512,2048]{1,0:T(8,128)(2,1)}, u32[]{:S(2)}) copy-start(bf16[512,2048]{1,0:T(8,128)(2,1)} %all-gather.3.cloned.1.call-done.straight.refs_4_.refs_5_) | copy-start | bytes 6291460
  62.2 3.9 %collective-permute-start.4 = (f32[4,256]{1,0:T(4,128)S(1)}, f32[4,256]{1,0:T(4,128)S(1)}, u32[]{:S(2)}, u32[]{:S(2)}) collective-permute-start(f32[4,256]{1,0:T(4,128)S(1)} %get-tuple-element.24), channel_id=1, source_target_pairs={{0,96},{32,0},{64,32},{96,64},{1,97},{33,1},{65,33},{97,65},{2,98}... | collective-permute-start | bytes 12296 | tf_op jit(solution)/shard_map/ppermute | solution.py:29
  64.8 4.6 %collective-permute-start.3 = (f32[4,256]{1,0:T(4,128)S(1)}, f32[4,256]{1,0:T(4,128)S(1)}, u32[]{:S(2)}, u32[]{:S(2)}) collective-permute-start(f32[4,256]{1,0:T(4,128)S(1)} %get-tuple-element.24), channel_id=1, source_target_pairs={{0,64},{32,96},{64,0},{96,32},{1,65},{33,97},{65,1},{97,33},{2,66}... | collective-permute-start | bytes 12296 | tf_op jit(solution)/shard_map/ppermute | solution.py:29
  64.9 5.5 %collective-permute-start.2 = (f32[4,256]{1,0:T(4,128)S(1)}, f32[4,256]{1,0:T(4,128)S(1)}, u32[]{:S(2)}, u32[]{:S(2)}) collective-permute-start(f32[4,256]{1,0:T(4,128)S(1)} %get-tuple-element.24), channel_id=1, source_target_pairs={{0,32},{32,64},{64,96},{96,0},{1,33},{33,65},{65,97},{97,1},{2,34}... | collective-permute-start | bytes 12296 | tf_op jit(solution)/shard_map/ppermute | solution.py:29
  71.1 13.6 %all-to-all-start.2 = ((f32[16,4,256]{2,1,0:T(4,128)}), f32[16,4,256]{2,1,0:T(4,128)S(1)}, u32[]{:S(2)}, u32[]{:S(2)}) async-start(f32[16,4,256]{2,1,0:T(4,128)} %broadcast_in_dim.47), calls=%async_computation.2 | async-start | bytes 131072 | tf_op jit(solution)/shard_map/all_to_all | solution.py:38
  78.5 36.6 %collective-permute-start.8 = (bf16[512,2048]{1,0:T(8,128)(2,1)S(1)}, bf16[512,2048]{1,0:T(8,128)(2,1)}, u32[]{:S(2)}, u32[]{:S(2)}) collective-permute-start(bf16[512,2048]{1,0:T(8,128)(2,1)S(1)} %copy-done), channel_id=1, source_target_pairs={{0,16},{16,0},{1,17},{17,1},{2,18},{18,2},{3,19},{19,3},{4,20},{20... | collective-permute-start | bytes 6291464 | tf_op jit(solution)/shard_map/ppermute | solution.py:42
  93.6 30.7 %all-to-all-start.3 = ((bf16[16,16,4096]{2,1,0:T(8,128)(2,1)}), bf16[16,16,4096]{2,1,0:T(8,128)(2,1)}, u32[]{:S(2)}, u32[]{:S(2)}) async-start(bf16[16,16,4096]{2,1,0:T(8,128)(2,1)} %bitcast.13), calls=%async_computation.3 | async-start | bytes 4194304 | tf_op jit(solution)/shard_map/all_to_all | solution.py:342
  99.4 7.5 %collective-permute-start.5 = (f32[3,256]{1,0:T(4,128)S(1)}, f32[3,256]{1,0:T(4,128)S(1)}, u32[]{:S(2)}, u32[]{:S(2)}) collective-permute-start(f32[3,256]{1,0:T(4,128)S(1)} %get-tuple-element.31), channel_id=1, source_target_pairs={{0,128},{128,0},{1,129},{129,1},{2,130},{130,2},{3,131},{131,3},{4... | collective-permute-start | bytes 9224 | tf_op jit(solution)/shard_map/ppermute | solution.py:42
  102.4 12.7 %collective-permute-start.6 = (bf16[594,256]{1,0:T(8,128)(2,1)S(1)}, bf16[594,256]{1,0:T(8,128)(2,1)S(1)}, u32[]{:S(2)}, u32[]{:S(2)}) collective-permute-start(bf16[594,256]{1,0:T(8,128)(2,1)S(1)} %copy-done.9), channel_id=1, source_target_pairs={{0,16},{16,0},{1,17},{17,1},{2,18},{18,2},{3,19},{19,3},{4,20},{20... | collective-permute-start | bytes 912392 | tf_op jit(solution)/shard_map/ppermute | solution.py:42
  115.1 1.8 %collective-permute-start.7 = (bf16[594,256]{1,0:T(8,128)(2,1)}, bf16[594,256]{1,0:T(8,128)(2,1)S(1)}, u32[]{:S(2)}, u32[]{:S(2)}) collective-permute-start(bf16[594,256]{1,0:T(8,128)(2,1)} %get-tuple-element.34), channel_id=1, source_target_pairs={{0,16},{16,0},{1,17},{17,1},{2,18},{18,2},{3,19},{19,3},{4,20},{20... | collective-permute-start | bytes 912392 | tf_op jit(solution)/shard_map/ppermute | solution.py:42
  124.3 6.3 %collective-permute-start.12 = (bf16[512,2048]{1,0:T(8,128)(2,1)S(1)}, bf16[512,2048]{1,0:T(8,128)(2,1)}, u32[]{:S(2)}, u32[]{:S(2)}) collective-permute-start(bf16[512,2048]{1,0:T(8,128)(2,1)S(1)} %copy-done.1), channel_id=1, source_target_pairs={{0,16},{16,0},{1,17},{17,1},{2,18},{18,2},{3,19},{19,3},{4,20},{20... | collective-permute-start | bytes 6291464 | tf_op jit(solution)/shard_map/ppermute | solution.py:42
  126.5 10.7 %collective-permute-start.9 = (bf16[4,4096]{1,0:T(4,128)(2,1)S(1)}, bf16[4,4096]{1,0:T(4,128)(2,1)S(1)}, u32[]{:S(2)}, u32[]{:S(2)}) collective-permute-start(bf16[4,4096]{1,0:T(4,128)(2,1)S(1)} %get-tuple-element.52), channel_id=1, source_target_pairs={{0,32},{32,64},{64,96},{96,0},{1,33},{33,65},{65,97},{97,1},{2,34}... | collective-permute-start | bytes 98312 | tf_op jit(solution)/shard_map/ppermute | solution.py:361
  126.6 10.7 %collective-permute-start.10 = (bf16[4,4096]{1,0:T(4,128)(2,1)S(1)}, bf16[4,4096]{1,0:T(4,128)(2,1)S(1)}, u32[]{:S(2)}, u32[]{:S(2)}) collective-permute-start(bf16[4,4096]{1,0:T(4,128)(2,1)S(1)} %get-tuple-element.51), channel_id=1, source_target_pairs={{0,64},{32,96},{64,0},{96,32},{1,65},{33,97},{65,1},{97,33},{2,66}... | collective-permute-start | bytes 98312 | tf_op jit(solution)/shard_map/ppermute | solution.py:361
  127.8 9.5 %collective-permute-start.11 = (bf16[4,4096]{1,0:T(4,128)(2,1)S(1)}, bf16[4,4096]{1,0:T(4,128)(2,1)S(1)}, u32[]{:S(2)}, u32[]{:S(2)}) collective-permute-start(bf16[4,4096]{1,0:T(4,128)(2,1)S(1)} %get-tuple-element.50), channel_id=1, source_target_pairs={{0,96},{32,0},{64,32},{96,64},{1,97},{33,1},{65,33},{97,65},{2,98}... | collective-permute-start | bytes 98312 | tf_op jit(solution)/shard_map/ppermute | solution.py:361
  (5 other events, 39.8 us)
Sparse Core Ops, SparseCore 0:
  9.8 44.0 all-gather.2
  55.7 40.1 all-gather.4

commit v9 on v8

--- a/solution.py
+++ b/solution.py
@@ -43,7 +43,7 @@
 
 
 TILE = 2048
-HEAD_TILE = 1024
+HALF_TILE = 1024
 PARAMS = pltpu.CompilerParams(vmem_limit_bytes=24 * 2**20)
 
 
@@ -97,21 +97,43 @@
     return first + lax.broadcasted_iota(jnp.int32, value.shape, 0) == target[...]
 
 
-def logits_kernel(s, target, straight, pieces, weight0, weight1, logits0, logits1, stats):
-    step = pl.program_id(0)
-
-    @pl.when(step == 0)
+def pieces_kernel(pieces, weight0, weight1, logits0, logits1):
+    @pl.when(pl.program_id(0) == 0)
     def _():
         logits0[...] = jnp.zeros_like(logits0)
         logits1[...] = jnp.zeros_like(logits1)
 
-    def use_second():
-        tile = jnp.concatenate([pieces[j] for j in range(pieces.shape[0])], axis=1)
-        add_logits(tile, (weight0, weight1), (logits0, logits1))
-
-    halves(
-        lambda: add_logits(straight[...], (weight0, weight1), (logits0, logits1)), use_second
-    )
+    tile = jnp.concatenate([pieces[j] for j in range(pieces.shape[0])], axis=1)
+    add_logits(tile, (weight0, weight1), (logits0, logits1))
+
+
+def second_half_logits(pieces, weights):
+    width, depth = weights[0].shape
+    tokens, piece = pieces.shape[1:]
+    steps = depth // 2 // HALF_TILE
+    return pl.pallas_call(
+        pieces_kernel,
+        grid=(steps,),
+        in_specs=[pl.BlockSpec((HALF_TILE // piece, tokens, piece), lambda i: (i, 0, 0))]
+        + [pl.BlockSpec((width, HALF_TILE), lambda i: (0, i + steps))] * 2,
+        out_specs=[pl.BlockSpec((width, tokens), lambda i: (0, 0))] * 2,
+        out_shape=[pltpu.HBM((width, tokens), jnp.float32)] * 2,
+        compiler_params=PARAMS,
+        name="logits_second_half",
+    )(pieces, *weights)
+
+
+def logits_kernel(
+    s, target, straight, before0, before1, weight0, weight1, logits0, logits1, stats
+):
+    step = pl.program_id(0)
+
+    @pl.when(step == 0)
+    def _():
+        logits0[...] = before0[...]
+        logits1[...] = before1[...]
+
+    add_logits(straight[...], (weight0, weight1), (logits0, logits1))
 
     @pl.when(step == pl.num_programs(0) - 1)
     def _():
@@ -133,28 +155,28 @@
         stats[3:4, :] = hit_sum
 
 
-def logits_and_stats(scalars, target, straight, pieces, weights):
+def logits_and_stats(scalars, target, straight, before, weights):
     width, depth = weights[0].shape
-    tokens, piece = pieces.shape[1:]
-    lead = depth // TILE // 2
-    return call(
+    tokens = before[0].shape[1]
+    tile = pl.BlockSpec((width, HALF_TILE), lambda i, s: (0, i))
+    return pl.pallas_call(
         logits_kernel,
-        "logits",
-        depth,
-        [
-            whole(1, tokens),
-            hidden_specs(tokens, depth, 0)[0],
-            pl.BlockSpec(
-                (TILE // piece, tokens, piece), lambda i, s: (jnp.maximum(i - lead, 0), 0, 0)
-            ),
-            tiles(width),
-            tiles(width),
-        ],
-        [whole(width, tokens)] * 2 + [whole(4, tokens)],
-        [pltpu.HBM((width, tokens), jnp.float32)] * 2
+        grid_spec=pltpu.PrefetchScalarGridSpec(
+            num_scalar_prefetch=1,
+            grid=(depth // 2 // HALF_TILE,),
+            in_specs=[
+                whole(1, tokens),
+                pl.BlockSpec((tokens, HALF_TILE), lambda i, s: (s[0], i)),
+            ]
+            + [whole(width, tokens)] * 2
+            + [tile] * 2,
+            out_specs=[whole(width, tokens)] * 2 + [whole(4, tokens)],
+        ),
+        out_shape=[pltpu.HBM((width, tokens), jnp.float32)] * 2
         + [jax.ShapeDtypeStruct((4, tokens), jnp.float32)],
-        flops=4 * tokens * width * depth,
-    )(scalars, target, straight, pieces, *weights)
+        compiler_params=PARAMS,
+        name="logits",
+    )(scalars, target, straight, *before, *weights)
 
 
 def logit_gradient(value, first, target, info, final):
@@ -269,10 +291,10 @@
 def head_half(scalars, grads, hiddens, before=None):
     width, tokens = grads[0].shape
     half = hiddens[0].shape[1]
-    steps = half // HEAD_TILE
+    steps = half // HALF_TILE
     skip = 0 if before is None else steps
     extra = [] if before is None else [before]
-    rows = [pl.BlockSpec((tokens, HEAD_TILE), lambda i, s, g=g: (s[g], i)) for g in (0, 1)]
+    rows = [pl.BlockSpec((tokens, HALF_TILE), lambda i, s, g=g: (s[g], i)) for g in (0, 1)]
     return pl.pallas_call(
         functools.partial(head_kernel, count=4),
         grid_spec=pltpu.PrefetchScalarGridSpec(
@@ -281,7 +303,7 @@
             in_specs=[whole(width, tokens)] * 4
             + rows * 2
             + [pl.BlockSpec(memory_space=pl.ANY)] * len(extra),
-            out_specs=pl.BlockSpec((width, HEAD_TILE), lambda i, s: (0, i + skip)),
+            out_specs=pl.BlockSpec((width, HALF_TILE), lambda i, s: (0, i + skip)),
         ),
         out_shape=pltpu.HBM((width, 2 * half), jnp.bfloat16),
         input_output_aliases={9: 0} if extra else {},
@@ -324,14 +346,15 @@
     own = own.reshape(4, nz, ncore, block)
     own = jnp.where(core == 0, own[:, :, 0], own[:, :, 1]).reshape(4, nz * block)
     other = swap(own, "dp")
-    later, straight, pieces, other = lax.optimization_barrier(
-        (hidden[:, half:], straight, pieces, other)
+    before = second_half_logits(pieces, weights)
+    later, straight, before, other = lax.optimization_barrier(
+        (hidden[:, half:], straight, before, other)
     )
     straight2 = lax.all_gather(later, ("dp", "z"), axis=0, tiled=True)
     own_target, other_target = own[3:4].astype(jnp.int32), other[3:4].astype(jnp.int32)
 
     *logits, stats = logits_and_stats(
-        scalars, own_target, in_hbm(straight), pieces, weights
+        scalars, own_target, in_hbm(straight), [in_hbm(part) for part in before], weights
     )
     stats = jnp.stack(combine(exchange(stats, "z")))
     parts = spread(stats, ("x", "y"))
@@ -344,6 +367,7 @@
     other0, other1 = other_gradient(
         scalars, other_target, other, swap(final, "dp"), gathered, weights
     )
+    own1, other1 = lax.optimization_barrier((own1, other1))
     grads = [
         in_hbm(grad) for grad in (own0, other0, swap(own1, "core"), swap(other1, "core"))
     ]

time: 146 us -> 144 us (0.986)
  waiting for transfers between devices: 39 us -> 34.2 us
  Pallas kernels: 38.4 us -> 41.5 us
    all_gather x1, waiting for transfers between devices: 8.3 us -> 4.13 us  [per_device(): straight = lax.all_gather(hidden[:, :half], ('dp', 'z'), axis=0, tiled=True)]
    pallas_call x1 -> x2, Pallas kernels: 8.11 us -> 11.1 us  [the longest x1 6.63 us: logits_and_stats(): pl.pallas_call(logits_kernel, grid_spec=pltpu.PrefetchScalarGridSpec(num_...]
    ppermute x7, waiting for transfers between devices: 9.36 us -> 6.41 us  [swap(): return lax.ppermute(value, axis, [(0, 1), (1, 0)])]
    all_to_all x3, waiting for transfers between devices: 16.4 us -> 18.8 us  [spread(): return lax.all_to_all(copies, axis, 0, 0, tiled=True)]
  transfers between devices with their start and end apart: 19 -> 19, of which waited for: 10 -> 10; matrix products, arithmetic and copies ran while one was open for 7% -> 7% of each run, Pallas kernels for 27% -> 29%
where the time goes in v9:
time: 144 us; the launch traced here: 143 us
  Pallas kernels  41.5 us (29%)
  starting transfers between devices  41 us (28%)
  waiting for transfers between devices  34.2 us (24%)
  between operations  14.2 us (10%)
  local copies, waits for them, and re-layouts  6.96 us (5%)
  other arithmetic  4.85 us (3%)
    all_to_all x3, starting transfers between devices, spread(): return lax.all_to_all(copies, axis, 0, 0, tiled=True)  20.6 us
    all_to_all x3, waiting for transfers between devices, spread(): return lax.all_to_all(copies, axis, 0, 0, tiled=True)  18.8 us
    pallas_call x2, Pallas kernels, head_half(): pl.pallas_call(functools.partial(head_kernel, count=4), grid_spec=pltpu.P...  13.3 us
    pallas_call x1, Pallas kernels, gradient_partial(): call(functools.partial(gradient_kernel, nz=nz, nv=nv), 'grad_hidden_parti...  8.87 us
    ppermute x7, starting transfers between devices, swap(): return lax.ppermute(value, axis, [(0, 1), (1, 0)])  8.38 us
    pallas_call x1, Pallas kernels, other_gradient(): call(other_kernel, 'other_group_grad_logits', depth, [whole(1, tokens), w...  8.16 us
    pallas_call x1, Pallas kernels, logits_and_stats(): pl.pallas_call(logits_kernel, grid_spec=pltpu.PrefetchScalarGridSpec(num_...  6.63 us
    ppermute x7, waiting for transfers between devices, swap(): return lax.ppermute(value, axis, [(0, 1), (1, 0)])  6.41 us
  transfers between devices with their start and end apart: 19, of which 10 were waited for; matrix products, arithmetic and copies ran while one was open for 7% of the time, Pallas kernels for 29%

profile of v9, /device:TPU:2, one launch (start us, length us, event | category | flops | bytes accessed | tf_op | source)
XLA Modules:
  0.0 142.7 jit_solution(11021537604490099404)
XLA Ops:
  7.3 1.9 %fusion.8 = (bf16[64,2048]{1,0:T(8,128)(2,1)}, bf16[64,2048]{1,0:T(8,128)(2,1)}) fusion(bf16[64,4096]{1,0:T(8,128)(2,1)} %param.8), kind=kLoop, calls=%fused_computation.40 | loop fusion | bytes 1048576 | tf_op jit(solution)/shard_map/slice | solution.py:332
  10.6 5.9 %all-to-all-start = ((bf16[4,64,128]{2,1,0:T(8,128)(2,1)}), bf16[4,64,128]{2,1,0:T(8,128)(2,1)S(1)}, u32[]{:S(2)}, u32[]{:S(2)}) async-start(bf16[4,64,128]{2,1,0:T(8,128)(2,1)} %broadcast_in_dim.44), calls=%async_computation | async-start | bytes 131072 | tf_op jit(solution)/shard_map/all_to_all | solution.py:38
  18.0 4.3 %all-to-all-done = bf16[4,64,128]{2,1,0:T(8,128)(2,1)S(1)} async-done(((bf16[4,64,128]{2,1,0:T(8,128)(2,1)}), bf16[4,64,128]{2,1,0:T(8,128)(2,1)S(1)}, u32[]{:S(2)}, u32[]{:S(2)}) %all-to-all-start) | async-done | bytes 65568 | tf_op jit(solution)/shard_map/all_to_all | solution.py:38
  22.3 1.2 broadcast_in_dim.46
  23.5 7.5 %all-to-all-start.1 = ((bf16[16,256,128]{2,1,0:T(8,128)(2,1)}), bf16[16,256,128]{2,1,0:T(8,128)(2,1)S(1)}, u32[]{:S(2)}, u32[]{:S(2)}) async-start(bf16[16,256,128]{2,1,0:T(8,128)(2,1)} %broadcast_in_dim.46), calls=%async_computation.1 | async-start | bytes 2097152 | tf_op jit(solution)/shard_map/all_to_all | solution.py:38
  32.7 4.6 %collective-permute-start.1 = (f32[4,256]{1,0:T(4,128)S(1)}, f32[4,256]{1,0:T(4,128)S(1)}, u32[]{:S(2)}, u32[]{:S(2)}) collective-permute-start(f32[4,256]{1,0:T(4,128)S(1)} %select_n.54.info), channel_id=1, source_target_pairs={{0,128},{128,0},{1,129},{129,1},{2,130},{130,2},{3,131},{131,3},{4... | collective-permute-start | bytes 12296 | tf_op jit(solution)/shard_map/ppermute | solution.py:42
  37.3 8.3 %all-to-all-done.1.pieces = bf16[16,256,128]{2,1,0:T(8,128)(2,1)S(1)} async-done(((bf16[16,256,128]{2,1,0:T(8,128)(2,1)}), bf16[16,256,128]{2,1,0:T(8,128)(2,1)S(1)}, u32[]{:S(2)}, u32[]{:S(2)}) %all-to-all-start.1) | async-done | bytes 1048608 | tf_op jit(solution)/shard_map/all_to_all | solution.py:38
  45.6 4.5 %logits_second_half.1 = (f32[594,256]{1,0:T(8,128)}, f32[594,256]{1,0:T(8,128)}) custom-call(bf16[16,256,128]{2,1,0:T(8,128)(2,1)S(1)} %all-to-all-done.1.pieces, bf16[594,4096]{1,0:T(8,128)(2,1)} %bitcast.9, bf16[594,4096]{1,0:T(8,128)(2,1)} %collective-permute-done.weight1), custom_call_target="tpu_custom_call" | custom-call | tf_op jit(solution)/shard_map/logits_second_half/pallas_call | solution.py:114
  50.1 4.1 %all-gather.3.cloned.1.call-done.straight.refs_4_.refs_5_ = bf16[512,2048]{1,0:T(8,128)(2,1)} async-done(((bf16[64,2048]{1,0:T(8,128)(2,1)}), bf16[512,2048]{1,0:T(8,128)(2,1)}) %all-gather.3.cloned.1.call-update) | async-done | bytes 2097168 | tf_op jit(solution)/shard_map/all_gather | solution.py:332
  54.5 6.6 %logits.1 = (f32[594,256]{1,0:T(8,128)}, f32[594,256]{1,0:T(8,128)}, f32[4,256]{1,0:T(4,128)S(1)}) custom-call(s32[4]{0:T(128)S(1)} %pad_add_fusion.s, s32[1,256]{1,0:T(1,128)S(1)} %convert_element_type.39.target, bf16[512,2048]{1,0:T(8,128)(2,1)} %all-gather.3.cloned.1.call-done.straight.refs_4_.refs_5_, f32[594,256]{1,0:T(8,128)} %get-tuple-element.30.before0, ...), custom_call_target="tpu_custom_call" | custom-call | tf_op jit(solution)/shard_map/logits/pallas_call | solution.py:162
  61.1 2.4 %collective-permute-start.4 = (f32[4,256]{1,0:T(4,128)S(1)}, f32[4,256]{1,0:T(4,128)S(1)}, u32[]{:S(2)}, u32[]{:S(2)}) collective-permute-start(f32[4,256]{1,0:T(4,128)S(1)} %get-tuple-element.32), channel_id=1, source_target_pairs={{0,96},{32,0},{64,32},{96,64},{1,97},{33,1},{65,33},{97,65},{2,98}... | collective-permute-start | bytes 12296 | tf_op jit(solution)/shard_map/ppermute | solution.py:29
  64.9 3.3 %collective-permute-done.3 = f32[4,256]{1,0:T(4,128)S(1)} collective-permute-done((f32[4,256]{1,0:T(4,128)S(1)}, f32[4,256]{1,0:T(4,128)S(1)}, u32[]{:S(2)}, u32[]{:S(2)}) %collective-permute-start.3) | collective-permute-done | bytes 4128 | tf_op jit(solution)/shard_map/ppermute | solution.py:29
  69.8 7.3 %all-to-all-start.2 = ((f32[16,4,256]{2,1,0:T(4,128)}), f32[16,4,256]{2,1,0:T(4,128)S(1)}, u32[]{:S(2)}, u32[]{:S(2)}) async-start(f32[16,4,256]{2,1,0:T(4,128)} %broadcast_in_dim.47), calls=%async_computation.2 | async-start | bytes 131072 | tf_op jit(solution)/shard_map/all_to_all | solution.py:38
  77.1 6.2 %all-to-all-done.2.parts = f32[16,4,256]{2,1,0:T(4,128)S(1)} async-done(((f32[16,4,256]{2,1,0:T(4,128)}), f32[16,4,256]{2,1,0:T(4,128)S(1)}, u32[]{:S(2)}, u32[]{:S(2)}) %all-to-all-start.2) | async-done | bytes 65568 | tf_op jit(solution)/shard_map/all_to_all | solution.py:38
  83.3 8.9 %grad_hidden_partial.1 = (bf16[256,4096]{1,0:T(8,128)(2,1)}, bf16[594,256]{1,0:T(8,128)(2,1)}, bf16[594,256]{1,0:T(8,128)(2,1)}, f32[3,256]{1,0:T(4,128)S(1)}) custom-call(s32[4]{0:T(128)S(1)} %pad_add_fusion.s, s32[1,256]{1,0:T(1,128)S(1)} %convert_element_type.39.target, f32[4,256]{1,0:T(4,128)S(1)} %select_n.54.info, ...), custom_call_target="tpu_custom_call" | custom-call | flops 2491416576 | bytes 4982833 | tf_op jit(solution)/shard_map/grad_hidden_partial/pallas_call | solution.py:229
  92.2 5.7 %all-to-all-start.3 = ((bf16[16,16,4096]{2,1,0:T(8,128)(2,1)}), bf16[16,16,4096]{2,1,0:T(8,128)(2,1)}, u32[]{:S(2)}, u32[]{:S(2)}) async-start(bf16[16,16,4096]{2,1,0:T(8,128)(2,1)} %bitcast.14), calls=%async_computation.3 | async-start | bytes 4194304 | tf_op jit(solution)/shard_map/all_to_all | solution.py:365
  97.8 2.8 %collective-permute-start.5 = (f32[3,256]{1,0:T(4,128)S(1)}, f32[3,256]{1,0:T(4,128)S(1)}, u32[]{:S(2)}, u32[]{:S(2)}) collective-permute-start(f32[3,256]{1,0:T(4,128)S(1)} %get-tuple-element.39), channel_id=1, source_target_pairs={{0,128},{128,0},{1,129},{129,1},{2,130},{130,2},{3,131},{131,3},{4... | collective-permute-start | bytes 9224 | tf_op jit(solution)/shard_map/ppermute | solution.py:42
  100.7 4.7 %collective-permute-done.5.final = f32[3,256]{1,0:T(4,128)S(1)} collective-permute-done((f32[3,256]{1,0:T(4,128)S(1)}, f32[3,256]{1,0:T(4,128)S(1)}, u32[]{:S(2)}, u32[]{:S(2)}) %collective-permute-start.5) | collective-permute-done | bytes 3104 | tf_op jit(solution)/shard_map/ppermute | solution.py:42
  105.3 8.2 %other_group_grad_logits.1 = (bf16[594,256]{1,0:T(8,128)(2,1)}, bf16[594,256]{1,0:T(8,128)(2,1)}) custom-call(s32[4]{0:T(128)S(1)} %pad_add_fusion.s, s32[1,256]{1,0:T(1,128)S(1)} %slice_convert_fusion.1.target, f32[4,256]{1,0:T(4,128)S(1)} %collective-permute-done.1.info, f32[3,256]{1,0:T(4,128)S(1)} %collective-permute-done.5.final, ...), custom_call_target="tpu_custom_call" | custom-call | flops 2491416576 | bytes 4982833 | tf_op jit(solution)/shard_map/other_group_grad_logits/pallas_call | solution.py:270
  114.0 1.1 collective-permute-done.6.refs_2_
  116.5 6.7 %grad_head.2.refs_8_ = bf16[594,4096]{1,0:T(8,128)(2,1)} custom-call(s32[4]{0:T(128)S(1)} %pad_add_fusion.s, bf16[594,256]{1,0:T(8,128)(2,1)} %get-tuple-element.37.refs_0_, bf16[594,256]{1,0:T(8,128)(2,1)} %get-tuple-element.40.refs_1_, bf16[594,256]{1,0:T(8,128)(2,1)} %copy-done.2, bf16[594,256]{1,0:T(8,128)(2,1)} %copy-done.3, ...), custom_call_target="tpu_custom_call" | custom-call | tf_op jit(solution)/shard_map/grad_head/pallas_call | solution.py:298
  123.4 1.9 %reduce_sum.32 = bf16[16,4096]{1,0:T(8,128)(2,1)S(1)} reduce(bf16[16,16,4096]{2,1,0:T(8,128)(2,1)} %all-to-all-done.3, bf16[]{:T(256)} %constant.63.clone.1), dimensions={0}, to_apply=%region_2.3 | reduce | flops 983040 | bytes 2228226 | tf_op jit(solution)/shard_map/reduce_sum | solution.py:379
  126.6 1.9 %collective-permute-start.9 = (bf16[4,4096]{1,0:T(4,128)(2,1)S(1)}, bf16[4,4096]{1,0:T(4,128)(2,1)S(1)}, u32[]{:S(2)}, u32[]{:S(2)}) collective-permute-start(bf16[4,4096]{1,0:T(4,128)(2,1)S(1)} %get-tuple-element.62), channel_id=1, source_target_pairs={{0,32},{32,64},{64,96},{96,0},{1,33},{33,65},{65,97},{97,1},{2,34}... | collective-permute-start | bytes 98312 | tf_op jit(solution)/shard_map/ppermute | solution.py:385
  128.6 6.6 %grad_head.3 = bf16[594,4096]{1,0:T(8,128)(2,1)} custom-call(s32[4]{0:T(128)S(1)} %pad_add_fusion.s, bf16[594,256]{1,0:T(8,128)(2,1)} %get-tuple-element.37.refs_0_, bf16[594,256]{1,0:T(8,128)(2,1)} %get-tuple-element.40.refs_1_, bf16[594,256]{1,0:T(8,128)(2,1)} %copy-done.2, bf16[594,256]{1,0:T(8,128)(2,1)} %copy-done.3, ...), custom_call_target="tpu_custom_call", output_to_operand_aliasing={{}: (9, {})} | custom-call | tf_op jit(solution)/shard_map/grad_head/pallas_call | solution.py:298
  (70 shorter events, 12.0 us)
Async XLA Ops:
  7.2 47.1 %all-gather.3.cloned.1.call-start = ((), (), s32[]{:S(2)}) async-start(), calls=%async_computation.4 | async-start | bytes 2359296 | tf_op jit(solution)/shard_map/all_gather | solution.py:332
  7.2 38.4 %collective-permute-start = (bf16[594,4096]{1,0:T(8,128)(2,1)}, bf16[594,4096]{1,0:T(8,128)(2,1)}, u32[]{:S(2)}, u32[]{:S(2)}) collective-permute-start(bf16[594,4096]{1,0:T(8,128)(2,1)} %bitcast.8), channel_id=1, source_target_pairs={{0,16},{16,0},{1,17},{17,1},{2,18},{18,2},{3,19},{19,3},{4,20},{20... | collective-permute-start | bytes 14598152 | tf_op jit(solution)/shard_map/ppermute | solution.py:42
  9.2 21.8 %copy-start.4 = (s32[512]{0:T(512)S(1)}, s32[512]{0:T(512)}, u32[]{:S(2)}) copy-start(s32[512]{0:T(512)} %param.11) | copy-start | bytes 6148
  9.2 21.8 %copy-start.7 = (f32[64]{0:T(128)S(1)}, f32[64]{0:T(128)}, u32[]{:S(2)}) copy-start(f32[64]{0:T(128)} %param.14) | copy-start | bytes 772
  9.2 21.9 %copy-start.5 = (s32[512]{0:T(512)S(1)}, s32[512]{0:T(512)}, u32[]{:S(2)}) copy-start(s32[512]{0:T(512)} %param.13) | copy-start | bytes 6148
  9.2 22.1 %copy-start.6 = (f32[512]{0:T(512)S(1)}, f32[512]{0:T(512)}, u32[]{:S(2)}) copy-start(f32[512]{0:T(512)} %param.15) | copy-start | bytes 6148
  10.6 11.6 %all-to-all-start = ((bf16[4,64,128]{2,1,0:T(8,128)(2,1)}), bf16[4,64,128]{2,1,0:T(8,128)(2,1)S(1)}, u32[]{:S(2)}, u32[]{:S(2)}) async-start(bf16[4,64,128]{2,1,0:T(8,128)(2,1)} %broadcast_in_dim.44), calls=%async_computation | async-start | bytes 131072 | tf_op jit(solution)/shard_map/all_to_all | solution.py:38
  23.5 22.1 %all-to-all-start.1 = ((bf16[16,256,128]{2,1,0:T(8,128)(2,1)}), bf16[16,256,128]{2,1,0:T(8,128)(2,1)S(1)}, u32[]{:S(2)}, u32[]{:S(2)}) async-start(bf16[16,256,128]{2,1,0:T(8,128)(2,1)} %broadcast_in_dim.46), calls=%async_computation.1 | async-start | bytes 2097152 | tf_op jit(solution)/shard_map/all_to_all | solution.py:38
  30.9 74.4 %all-gather.5.cloned.1.call-start = ((), (), s32[]{:S(2)}) async-start(), calls=%async_computation.5 | async-start | bytes 2359296 | tf_op jit(solution)/shard_map/all_gather | solution.py:353
  32.7 17.4 %collective-permute-start.1 = (f32[4,256]{1,0:T(4,128)S(1)}, f32[4,256]{1,0:T(4,128)S(1)}, u32[]{:S(2)}, u32[]{:S(2)}) collective-permute-start(f32[4,256]{1,0:T(4,128)S(1)} %select_n.54.info), channel_id=1, source_target_pairs={{0,128},{128,0},{1,129},{129,1},{2,130},{130,2},{3,131},{131,3},{4... | collective-permute-start | bytes 12296 | tf_op jit(solution)/shard_map/ppermute | solution.py:42
  54.5 22.5 %copy-start = (bf16[512,2048]{1,0:T(8,128)(2,1)S(1)}, bf16[512,2048]{1,0:T(8,128)(2,1)}, u32[]{:S(2)}) copy-start(bf16[512,2048]{1,0:T(8,128)(2,1)} %all-gather.3.cloned.1.call-done.straight.refs_4_.refs_5_) | copy-start | bytes 6291460
  61.1 3.7 %collective-permute-start.4 = (f32[4,256]{1,0:T(4,128)S(1)}, f32[4,256]{1,0:T(4,128)S(1)}, u32[]{:S(2)}, u32[]{:S(2)}) collective-permute-start(f32[4,256]{1,0:T(4,128)S(1)} %get-tuple-element.32), channel_id=1, source_target_pairs={{0,96},{32,0},{64,32},{96,64},{1,97},{33,1},{65,33},{97,65},{2,98}... | collective-permute-start | bytes 12296 | tf_op jit(solution)/shard_map/ppermute | solution.py:29
  63.5 4.6 %collective-permute-start.3 = (f32[4,256]{1,0:T(4,128)S(1)}, f32[4,256]{1,0:T(4,128)S(1)}, u32[]{:S(2)}, u32[]{:S(2)}) collective-permute-start(f32[4,256]{1,0:T(4,128)S(1)} %get-tuple-element.32), channel_id=1, source_target_pairs={{0,64},{32,96},{64,0},{96,32},{1,65},{33,97},{65,1},{97,33},{2,66}... | collective-permute-start | bytes 12296 | tf_op jit(solution)/shard_map/ppermute | solution.py:29
  63.5 5.5 %collective-permute-start.2 = (f32[4,256]{1,0:T(4,128)S(1)}, f32[4,256]{1,0:T(4,128)S(1)}, u32[]{:S(2)}, u32[]{:S(2)}) collective-permute-start(f32[4,256]{1,0:T(4,128)S(1)} %get-tuple-element.32), channel_id=1, source_target_pairs={{0,32},{32,64},{64,96},{96,0},{1,33},{33,65},{65,97},{97,1},{2,34}... | collective-permute-start | bytes 12296 | tf_op jit(solution)/shard_map/ppermute | solution.py:29
  69.8 13.5 %all-to-all-start.2 = ((f32[16,4,256]{2,1,0:T(4,128)}), f32[16,4,256]{2,1,0:T(4,128)S(1)}, u32[]{:S(2)}, u32[]{:S(2)}) async-start(f32[16,4,256]{2,1,0:T(4,128)} %broadcast_in_dim.47), calls=%async_computation.2 | async-start | bytes 131072 | tf_op jit(solution)/shard_map/all_to_all | solution.py:38
  77.0 37.0 %collective-permute-start.8 = (bf16[512,2048]{1,0:T(8,128)(2,1)S(1)}, bf16[512,2048]{1,0:T(8,128)(2,1)}, u32[]{:S(2)}, u32[]{:S(2)}) collective-permute-start(bf16[512,2048]{1,0:T(8,128)(2,1)S(1)} %copy-done), channel_id=1, source_target_pairs={{0,16},{16,0},{1,17},{17,1},{2,18},{18,2},{3,19},{19,3},{4,20},{20... | collective-permute-start | bytes 6291464 | tf_op jit(solution)/shard_map/ppermute | solution.py:42
  92.2 31.0 %all-to-all-start.3 = ((bf16[16,16,4096]{2,1,0:T(8,128)(2,1)}), bf16[16,16,4096]{2,1,0:T(8,128)(2,1)}, u32[]{:S(2)}, u32[]{:S(2)}) async-start(bf16[16,16,4096]{2,1,0:T(8,128)(2,1)} %bitcast.14), calls=%async_computation.3 | async-start | bytes 4194304 | tf_op jit(solution)/shard_map/all_to_all | solution.py:365
  97.8 7.5 %collective-permute-start.5 = (f32[3,256]{1,0:T(4,128)S(1)}, f32[3,256]{1,0:T(4,128)S(1)}, u32[]{:S(2)}, u32[]{:S(2)}) collective-permute-start(f32[3,256]{1,0:T(4,128)S(1)} %get-tuple-element.39), channel_id=1, source_target_pairs={{0,128},{128,0},{1,129},{129,1},{2,130},{130,2},{3,131},{131,3},{4... | collective-permute-start | bytes 9224 | tf_op jit(solution)/shard_map/ppermute | solution.py:42
  113.5 1.6 %collective-permute-start.6 = (bf16[594,256]{1,0:T(8,128)(2,1)S(1)}, bf16[594,256]{1,0:T(8,128)(2,1)S(1)}, u32[]{:S(2)}, u32[]{:S(2)}) collective-permute-start(bf16[594,256]{1,0:T(8,128)(2,1)S(1)} %copy-done.8), channel_id=1, source_target_pairs={{0,16},{16,0},{1,17},{17,1},{2,18},{18,2},{3,19},{19,3},{4,20},{20... | collective-permute-start | bytes 912392 | tf_op jit(solution)/shard_map/ppermute | solution.py:42
  113.5 2.2 %collective-permute-start.7 = (bf16[594,256]{1,0:T(8,128)(2,1)}, bf16[594,256]{1,0:T(8,128)(2,1)S(1)}, u32[]{:S(2)}, u32[]{:S(2)}) collective-permute-start(bf16[594,256]{1,0:T(8,128)(2,1)} %get-tuple-element.44), channel_id=1, source_target_pairs={{0,16},{16,0},{1,17},{17,1},{2,18},{18,2},{3,19},{19,3},{4,20},{20... | collective-permute-start | bytes 912392 | tf_op jit(solution)/shard_map/ppermute | solution.py:42
  123.2 5.4 %collective-permute-start.12 = (bf16[512,2048]{1,0:T(8,128)(2,1)S(1)}, bf16[512,2048]{1,0:T(8,128)(2,1)}, u32[]{:S(2)}, u32[]{:S(2)}) collective-permute-start(bf16[512,2048]{1,0:T(8,128)(2,1)S(1)} %copy-done.1), channel_id=1, source_target_pairs={{0,16},{16,0},{1,17},{17,1},{2,18},{18,2},{3,19},{19,3},{4,20},{20... | collective-permute-start | bytes 6291464 | tf_op jit(solution)/shard_map/ppermute | solution.py:42
  125.4 9.8 %collective-permute-start.11 = (bf16[4,4096]{1,0:T(4,128)(2,1)S(1)}, bf16[4,4096]{1,0:T(4,128)(2,1)S(1)}, u32[]{:S(2)}, u32[]{:S(2)}) collective-permute-start(bf16[4,4096]{1,0:T(4,128)(2,1)S(1)} %get-tuple-element.60), channel_id=1, source_target_pairs={{0,96},{32,0},{64,32},{96,64},{1,97},{33,1},{65,33},{97,65},{2,98}... | collective-permute-start | bytes 98312 | tf_op jit(solution)/shard_map/ppermute | solution.py:385
  126.0 9.2 %collective-permute-start.10 = (bf16[4,4096]{1,0:T(4,128)(2,1)S(1)}, bf16[4,4096]{1,0:T(4,128)(2,1)S(1)}, u32[]{:S(2)}, u32[]{:S(2)}) collective-permute-start(bf16[4,4096]{1,0:T(4,128)(2,1)S(1)} %get-tuple-element.61), channel_id=1, source_target_pairs={{0,64},{32,96},{64,0},{96,32},{1,65},{33,97},{65,1},{97,33},{2,66}... | collective-permute-start | bytes 98312 | tf_op jit(solution)/shard_map/ppermute | solution.py:385
  126.6 8.6 %collective-permute-start.9 = (bf16[4,4096]{1,0:T(4,128)(2,1)S(1)}, bf16[4,4096]{1,0:T(4,128)(2,1)S(1)}, u32[]{:S(2)}, u32[]{:S(2)}) collective-permute-start(bf16[4,4096]{1,0:T(4,128)(2,1)S(1)} %get-tuple-element.62), channel_id=1, source_target_pairs={{0,32},{32,64},{64,96},{96,0},{1,33},{33,65},{65,97},{97,1},{2,34}... | collective-permute-start | bytes 98312 | tf_op jit(solution)/shard_map/ppermute | solution.py:385
  (4 other events, 21.0 us)
Sparse Core Ops, SparseCore 0:
  9.8 44.4 all-gather.2
  56.0 39.4 all-gather.4

commit v10 on v9

--- a/solution.py
+++ b/solution.py
@@ -53,14 +53,6 @@
 
 def tiles(rows):
     return pl.BlockSpec((rows, TILE), lambda i, s: (0, i))
-
-
-def hidden_specs(tokens, depth, group):
-    lead = depth // TILE // 2
-    return [
-        pl.BlockSpec((tokens, TILE), lambda i, s: (s[group], jnp.minimum(i, lead - 1))),
-        pl.BlockSpec((tokens, TILE), lambda i, s: (s[group], jnp.maximum(i - lead, 0))),
-    ]
 
 
 def call(kernel, name, depth, in_specs, out_specs, out_shape, scratch=(), flops=0):
@@ -80,12 +72,6 @@
     )
 
 
-def halves(use_first, use_second):
-    step, lead = pl.program_id(0), pl.num_programs(0) // 2
-    pl.when(step < lead)(use_first)
-    pl.when(step >= lead)(use_second)
-
-
 def add_logits(tile, weights, logits):
     for weight, out in zip(weights, logits):
         out[...] += lax.dot_general(
@@ -124,7 +110,8 @@
 
 
 def logits_kernel(
-    s, target, straight, before0, before1, weight0, weight1, logits0, logits1, stats
+    s, target, straight, other_straight, before0, before1, weight0, weight1,
+    logits0, logits1, other0, other1, stats,
 ):
     step = pl.program_id(0)
 
@@ -132,8 +119,11 @@
     def _():
         logits0[...] = before0[...]
         logits1[...] = before1[...]
+        other0[...] = jnp.zeros_like(other0)
+        other1[...] = jnp.zeros_like(other1)
 
     add_logits(straight[...], (weight0, weight1), (logits0, logits1))
+    add_logits(other_straight[...], (weight0, weight1), (other0, other1))
 
     @pl.when(step == pl.num_programs(0) - 1)
     def _():
@@ -167,16 +157,17 @@
             in_specs=[
                 whole(1, tokens),
                 pl.BlockSpec((tokens, HALF_TILE), lambda i, s: (s[0], i)),
+                pl.BlockSpec((tokens, HALF_TILE), lambda i, s: (s[1], i)),
             ]
             + [whole(width, tokens)] * 2
             + [tile] * 2,
-            out_specs=[whole(width, tokens)] * 2 + [whole(4, tokens)],
+            out_specs=[whole(width, tokens)] * 4 + [whole(4, tokens)],
         ),
-        out_shape=[pltpu.HBM((width, tokens), jnp.float32)] * 2
+        out_shape=[pltpu.HBM((width, tokens), jnp.float32)] * 4
         + [jax.ShapeDtypeStruct((4, tokens), jnp.float32)],
         compiler_params=PARAMS,
         name="logits",
-    )(scalars, target, straight, *before, *weights)
+    )(scalars, target, straight, straight, *before, *weights)
 
 
 def logit_gradient(value, first, target, info, final):
@@ -243,19 +234,17 @@
 
 
 def other_kernel(
-    s, target, info, final, straight, straight2, weight0, weight1, grad0, grad1, logits0, logits1
+    s, target, info, final, before0, before1, straight2, weight0, weight1,
+    grad0, grad1, logits0, logits1,
 ):
     step = pl.program_id(0)
 
     @pl.when(step == 0)
     def _():
-        logits0[...] = jnp.zeros_like(logits0)
-        logits1[...] = jnp.zeros_like(logits1)
-
-    halves(
-        lambda: add_logits(straight[...], (weight0, weight1), (logits0, logits1)),
-        lambda: add_logits(straight2[...], (weight0, weight1), (logits0, logits1)),
-    )
+        logits0[...] = before0[...]
+        logits1[...] = before1[...]
+
+    add_logits(straight2[...], (weight0, weight1), (logits0, logits1))
 
     @pl.when(step == pl.num_programs(0) - 1)
     def _():
@@ -264,21 +253,26 @@
             grad[...] = logit_gradient(logits[...], s[2 + k], target, info, ends)
 
 
-def other_gradient(scalars, target, info, final, straights, weights):
+def other_gradient(scalars, target, info, final, before, straight2, weights):
     width, depth = weights[0].shape
     tokens = info.shape[1]
-    return call(
+    steps = depth // 2 // HALF_TILE
+    return pl.pallas_call(
         other_kernel,
-        "other_group_grad_logits",
-        depth,
-        [whole(1, tokens), whole(4, tokens), whole(3, tokens)]
-        + hidden_specs(tokens, depth, 1)
-        + [tiles(width)] * 2,
-        [whole(width, tokens)] * 2,
-        [pltpu.HBM((width, tokens), jnp.bfloat16)] * 2,
-        [pltpu.VMEM((width, tokens), jnp.float32)] * 2,
-        flops=4 * tokens * width * depth,
-    )(scalars, target, info, final, *straights, *weights)
+        grid_spec=pltpu.PrefetchScalarGridSpec(
+            num_scalar_prefetch=1,
+            grid=(steps,),
+            in_specs=[whole(1, tokens), whole(4, tokens), whole(3, tokens)]
+            + [whole(width, tokens)] * 2
+            + [pl.BlockSpec((tokens, HALF_TILE), lambda i, s: (s[1], i))]
+            + [pl.BlockSpec((width, HALF_TILE), lambda i, s: (0, i + steps))] * 2,
+            out_specs=[whole(width, tokens)] * 2,
+            scratch_shapes=[pltpu.VMEM((width, tokens), jnp.float32)] * 2,
+        ),
+        out_shape=[pltpu.HBM((width, tokens), jnp.bfloat16)] * 2,
+        compiler_params=PARAMS,
+        name="other_group_grad_logits",
+    )(scalars, target, info, final, *before, straight2, *weights)
 
 
 def head_kernel(s, *refs, count):
@@ -353,21 +347,26 @@
     straight2 = lax.all_gather(later, ("dp", "z"), axis=0, tiled=True)
     own_target, other_target = own[3:4].astype(jnp.int32), other[3:4].astype(jnp.int32)
 
-    *logits, stats = logits_and_stats(
+    logits0, logits1, *other_before, stats = logits_and_stats(
         scalars, own_target, in_hbm(straight), [in_hbm(part) for part in before], weights
     )
     stats = jnp.stack(combine(exchange(stats, "z")))
     parts = spread(stats, ("x", "y"))
-    logits = [in_hbm(value) for value in logits]
+    logits = [in_hbm(value) for value in (logits0, logits1)]
     partial, own0, own1, final = gradient_partial(
         scalars, own_target, own, parts, logits, weights, nz, nv
     )
     got = lax.all_to_all(partial.reshape(nv, nz * rows, depth), ("x", "y"), 0, 0, tiled=True)
     gathered = (in_hbm(straight), in_hbm(straight2))
     other0, other1 = other_gradient(
-        scalars, other_target, other, swap(final, "dp"), gathered, weights
-    )
-    own1, other1 = lax.optimization_barrier((own1, other1))
+        scalars,
+        other_target,
+        other,
+        swap(final, "dp"),
+        [in_hbm(part) for part in other_before],
+        gathered[1],
+        weights,
+    )
     grads = [
         in_hbm(grad) for grad in (own0, other0, swap(own1, "core"), swap(other1, "core"))
     ]

time: 144 us -> 145 us (level)
    pallas_call x1, Pallas kernels: 8.16 us -> 6.27 us  [other_gradient(): pl.pallas_call(other_kernel, grid_spec=pltpu.PrefetchScalarGridSpec(num_s...]
    pallas_call x1, Pallas kernels: 6.63 us -> 8.32 us  [logits_and_stats(): pl.pallas_call(logits_kernel, grid_spec=pltpu.PrefetchScalarGridSpec(num_...]
where the time goes in v10:
time: 145 us; the launch traced here: 143 us
  Pallas kernels  41.3 us (28%)
  starting transfers between devices  40.9 us (28%)
  waiting for transfers between devices  34.4 us (24%)
  between operations  14.2 us (10%)
  local copies, waits for them, and re-layouts  6.92 us (5%)
  other arithmetic  4.85 us (3%)
    all_to_all x3, starting transfers between devices, spread(): return lax.all_to_all(copies, axis, 0, 0, tiled=True)  20.6 us
    all_to_all x3, waiting for transfers between devices, spread(): return lax.all_to_all(copies, axis, 0, 0, tiled=True)  18.8 us
    pallas_call x2, Pallas kernels, head_half(): pl.pallas_call(functools.partial(head_kernel, count=4), grid_spec=pltpu.P...  13.3 us
    pallas_call x1, Pallas kernels, gradient_partial(): call(functools.partial(gradient_kernel, nz=nz, nv=nv), 'grad_hidden_parti...  8.85 us
    pallas_call x1, Pallas kernels, logits_and_stats(): pl.pallas_call(logits_kernel, grid_spec=pltpu.PrefetchScalarGridSpec(num_...  8.32 us
    ppermute x7, starting transfers between devices, swap(): return lax.ppermute(value, axis, [(0, 1), (1, 0)])  7.76 us
    ppermute x7, waiting for transfers between devices, swap(): return lax.ppermute(value, axis, [(0, 1), (1, 0)])  6.35 us
    pallas_call x1, Pallas kernels, other_gradient(): pl.pallas_call(other_kernel, grid_spec=pltpu.PrefetchScalarGridSpec(num_s...  6.27 us
  transfers between devices with their start and end apart: 19, of which 10 were waited for; matrix products, arithmetic and copies ran while one was open for 7% of the time, Pallas kernels for 29%

profile of v10, /device:TPU:2, one launch (start us, length us, event | category | flops | bytes accessed | tf_op | source)
XLA Modules:
  0.0 142.6 jit_solution(15725394273520891105)
XLA Ops:
  7.3 1.9 %fusion.8 = (bf16[64,2048]{1,0:T(8,128)(2,1)}, bf16[64,2048]{1,0:T(8,128)(2,1)}) fusion(bf16[64,4096]{1,0:T(8,128)(2,1)} %param.8), kind=kLoop, calls=%fused_computation.40 | loop fusion | bytes 1048576 | tf_op jit(solution)/shard_map/slice | solution.py:326
  10.6 5.9 %all-to-all-start = ((bf16[4,64,128]{2,1,0:T(8,128)(2,1)}), bf16[4,64,128]{2,1,0:T(8,128)(2,1)S(1)}, u32[]{:S(2)}, u32[]{:S(2)}) async-start(bf16[4,64,128]{2,1,0:T(8,128)(2,1)} %broadcast_in_dim.44), calls=%async_computation | async-start | bytes 131072 | tf_op jit(solution)/shard_map/all_to_all | solution.py:38
  17.9 4.3 %all-to-all-done = bf16[4,64,128]{2,1,0:T(8,128)(2,1)S(1)} async-done(((bf16[4,64,128]{2,1,0:T(8,128)(2,1)}), bf16[4,64,128]{2,1,0:T(8,128)(2,1)S(1)}, u32[]{:S(2)}, u32[]{:S(2)}) %all-to-all-start) | async-done | bytes 65568 | tf_op jit(solution)/shard_map/all_to_all | solution.py:38
  22.2 1.2 broadcast_in_dim.46
  23.4 7.5 %all-to-all-start.1 = ((bf16[16,256,128]{2,1,0:T(8,128)(2,1)}), bf16[16,256,128]{2,1,0:T(8,128)(2,1)S(1)}, u32[]{:S(2)}, u32[]{:S(2)}) async-start(bf16[16,256,128]{2,1,0:T(8,128)(2,1)} %broadcast_in_dim.46), calls=%async_computation.1 | async-start | bytes 2097152 | tf_op jit(solution)/shard_map/all_to_all | solution.py:38
  32.7 4.6 %collective-permute-start.1 = (f32[4,256]{1,0:T(4,128)S(1)}, f32[4,256]{1,0:T(4,128)S(1)}, u32[]{:S(2)}, u32[]{:S(2)}) collective-permute-start(f32[4,256]{1,0:T(4,128)S(1)} %select_n.54.info), channel_id=1, source_target_pairs={{0,128},{128,0},{1,129},{129,1},{2,130},{130,2},{3,131},{131,3},{4... | collective-permute-start | bytes 12296 | tf_op jit(solution)/shard_map/ppermute | solution.py:42
  37.3 8.3 %all-to-all-done.1.pieces = bf16[16,256,128]{2,1,0:T(8,128)(2,1)S(1)} async-done(((bf16[16,256,128]{2,1,0:T(8,128)(2,1)}), bf16[16,256,128]{2,1,0:T(8,128)(2,1)S(1)}, u32[]{:S(2)}, u32[]{:S(2)}) %all-to-all-start.1) | async-done | bytes 1048608 | tf_op jit(solution)/shard_map/all_to_all | solution.py:38
  45.6 4.5 %logits_second_half.1 = (f32[594,256]{1,0:T(8,128)}, f32[594,256]{1,0:T(8,128)}) custom-call(bf16[16,256,128]{2,1,0:T(8,128)(2,1)S(1)} %all-to-all-done.1.pieces, bf16[594,4096]{1,0:T(8,128)(2,1)} %bitcast.9, bf16[594,4096]{1,0:T(8,128)(2,1)} %collective-permute-done.weight1), custom_call_target="tpu_custom_call" | custom-call | tf_op jit(solution)/shard_map/logits_second_half/pallas_call | solution.py:100
  50.1 3.8 %all-gather.3.cloned.1.call-done.straight.other_straight.refs_4_.refs_5_ = bf16[512,2048]{1,0:T(8,128)(2,1)} async-done(((bf16[64,2048]{1,0:T(8,128)(2,1)}), bf16[512,2048]{1,0:T(8,128)(2,1)}) %all-gather.3.cloned.1.call-update) | async-done | bytes 2097168 | tf_op jit(solution)/shard_map/all_gather | solution.py:326
  54.1 8.3 %logits.1 = (f32[594,256]{1,0:T(8,128)}, f32[594,256]{1,0:T(8,128)}, f32[594,256]{1,0:T(8,128)}, f32[594,256]{1,0:T(8,128)}, f32[4,256]{1,0:T(4,128)S(1)}) custom-call(s32[4]{0:T(128)S(1)} %pad_add_fusion.s, s32[1,256]{1,0:T(1,128)S(1)} %convert_element_type.39.target, bf16[512,2048]{1,0:T(8,128)(2,1)} %all-gather.3.cloned.1.call-done.straight.other_straight.refs_4_.refs_5_, ...), custom_call_target="tpu_custom_call" | custom-call | tf_op jit(solution)/shard_map/logits/pallas_call | solution.py:152
  62.4 2.8 %collective-permute-start.4 = (f32[4,256]{1,0:T(4,128)S(1)}, f32[4,256]{1,0:T(4,128)S(1)}, u32[]{:S(2)}, u32[]{:S(2)}) collective-permute-start(f32[4,256]{1,0:T(4,128)S(1)} %get-tuple-element.32), channel_id=1, source_target_pairs={{0,96},{32,0},{64,32},{96,64},{1,97},{33,1},{65,33},{97,65},{2,98}... | collective-permute-start | bytes 12296 | tf_op jit(solution)/shard_map/ppermute | solution.py:29
  66.6 3.3 %collective-permute-done.3 = f32[4,256]{1,0:T(4,128)S(1)} collective-permute-done((f32[4,256]{1,0:T(4,128)S(1)}, f32[4,256]{1,0:T(4,128)S(1)}, u32[]{:S(2)}, u32[]{:S(2)}) %collective-permute-start.3) | collective-permute-done | bytes 4128 | tf_op jit(solution)/shard_map/ppermute | solution.py:29
  71.4 7.3 %all-to-all-start.2 = ((f32[16,4,256]{2,1,0:T(4,128)}), f32[16,4,256]{2,1,0:T(4,128)S(1)}, u32[]{:S(2)}, u32[]{:S(2)}) async-start(f32[16,4,256]{2,1,0:T(4,128)} %broadcast_in_dim.47), calls=%async_computation.2 | async-start | bytes 131072 | tf_op jit(solution)/shard_map/all_to_all | solution.py:38
  78.8 6.2 %all-to-all-done.2.parts = f32[16,4,256]{2,1,0:T(4,128)S(1)} async-done(((f32[16,4,256]{2,1,0:T(4,128)}), f32[16,4,256]{2,1,0:T(4,128)S(1)}, u32[]{:S(2)}, u32[]{:S(2)}) %all-to-all-start.2) | async-done | bytes 65568 | tf_op jit(solution)/shard_map/all_to_all | solution.py:38
  85.0 8.9 %grad_hidden_partial.1 = (bf16[256,4096]{1,0:T(8,128)(2,1)}, bf16[594,256]{1,0:T(8,128)(2,1)}, bf16[594,256]{1,0:T(8,128)(2,1)}, f32[3,256]{1,0:T(4,128)S(1)}) custom-call(s32[4]{0:T(128)S(1)} %pad_add_fusion.s, s32[1,256]{1,0:T(1,128)S(1)} %convert_element_type.39.target, f32[4,256]{1,0:T(4,128)S(1)} %select_n.54.info, ...), custom_call_target="tpu_custom_call" | custom-call | flops 2491416576 | bytes 4982833 | tf_op jit(solution)/shard_map/grad_hidden_partial/pallas_call | solution.py:220
  93.8 5.8 %all-to-all-start.3 = ((bf16[16,16,4096]{2,1,0:T(8,128)(2,1)}), bf16[16,16,4096]{2,1,0:T(8,128)(2,1)}, u32[]{:S(2)}, u32[]{:S(2)}) async-start(bf16[16,16,4096]{2,1,0:T(8,128)(2,1)} %bitcast.14), calls=%async_computation.3 | async-start | bytes 4194304 | tf_op jit(solution)/shard_map/all_to_all | solution.py:359
  99.7 2.9 %collective-permute-start.5 = (f32[3,256]{1,0:T(4,128)S(1)}, f32[3,256]{1,0:T(4,128)S(1)}, u32[]{:S(2)}, u32[]{:S(2)}) collective-permute-start(f32[3,256]{1,0:T(4,128)S(1)} %get-tuple-element.39), channel_id=1, source_target_pairs={{0,128},{128,0},{1,129},{129,1},{2,130},{130,2},{3,131},{131,3},{4... | collective-permute-start | bytes 9224 | tf_op jit(solution)/shard_map/ppermute | solution.py:42
  102.6 4.6 %collective-permute-done.5.final = f32[3,256]{1,0:T(4,128)S(1)} collective-permute-done((f32[3,256]{1,0:T(4,128)S(1)}, f32[3,256]{1,0:T(4,128)S(1)}, u32[]{:S(2)}, u32[]{:S(2)}) %collective-permute-start.5) | collective-permute-done | bytes 3104 | tf_op jit(solution)/shard_map/ppermute | solution.py:42
  107.2 6.3 %other_group_grad_logits.1 = (bf16[594,256]{1,0:T(8,128)(2,1)}, bf16[594,256]{1,0:T(8,128)(2,1)}) custom-call(s32[4]{0:T(128)S(1)} %pad_add_fusion.s, s32[1,256]{1,0:T(1,128)S(1)} %slice_convert_fusion.1.target, f32[4,256]{1,0:T(4,128)S(1)} %collective-permute-done.1.info, f32[3,256]{1,0:T(4,128)S(1)} %collective-permute-done.5.final, ...), custom_call_target="tpu_custom_call" | custom-call | tf_op jit(solution)/shard_map/other_group_grad_logits/pallas_call | solution.py:260
  113.5 1.8 %collective-permute-done.7.refs_3_ = bf16[594,256]{1,0:T(8,128)(2,1)S(1)} collective-permute-done((bf16[594,256]{1,0:T(8,128)(2,1)}, bf16[594,256]{1,0:T(8,128)(2,1)S(1)}, u32[]{:S(2)}, u32[]{:S(2)}) %collective-permute-start.7) | collective-permute-done | bytes 304160 | tf_op jit(solution)/shard_map/ppermute | solution.py:42
  116.0 6.7 %grad_head.2.refs_8_ = bf16[594,4096]{1,0:T(8,128)(2,1)} custom-call(s32[4]{0:T(128)S(1)} %pad_add_fusion.s, bf16[594,256]{1,0:T(8,128)(2,1)} %get-tuple-element.37.refs_0_, bf16[594,256]{1,0:T(8,128)(2,1)} %get-tuple-element.42.refs_1_, bf16[594,256]{1,0:T(8,128)(2,1)} %copy-done.2, bf16[594,256]{1,0:T(8,128)(2,1)} %copy-done.3, ...), custom_call_target="tpu_custom_call" | custom-call | tf_op jit(solution)/shard_map/grad_head/pallas_call | solution.py:292
  123.3 1.9 %reduce_sum.32 = bf16[16,4096]{1,0:T(8,128)(2,1)S(1)} reduce(bf16[16,16,4096]{2,1,0:T(8,128)(2,1)} %all-to-all-done.3, bf16[]{:T(256)} %constant.63.clone.1), dimensions={0}, to_apply=%region_2.3 | reduce | flops 983040 | bytes 2228226 | tf_op jit(solution)/shard_map/reduce_sum | solution.py:378
  126.5 1.9 %collective-permute-start.9 = (bf16[4,4096]{1,0:T(4,128)(2,1)S(1)}, bf16[4,4096]{1,0:T(4,128)(2,1)S(1)}, u32[]{:S(2)}, u32[]{:S(2)}) collective-permute-start(bf16[4,4096]{1,0:T(4,128)(2,1)S(1)} %get-tuple-element.62), channel_id=1, source_target_pairs={{0,32},{32,64},{64,96},{96,0},{1,33},{33,65},{65,97},{97,1},{2,34}... | collective-permute-start | bytes 98312 | tf_op jit(solution)/shard_map/ppermute | solution.py:384
  128.4 6.6 %grad_head.3 = bf16[594,4096]{1,0:T(8,128)(2,1)} custom-call(s32[4]{0:T(128)S(1)} %pad_add_fusion.s, bf16[594,256]{1,0:T(8,128)(2,1)} %get-tuple-element.37.refs_0_, bf16[594,256]{1,0:T(8,128)(2,1)} %get-tuple-element.42.refs_1_, bf16[594,256]{1,0:T(8,128)(2,1)} %copy-done.2, bf16[594,256]{1,0:T(8,128)(2,1)} %copy-done.3, ...), custom_call_target="tpu_custom_call", output_to_operand_aliasing={{}: (9, {})} | custom-call | tf_op jit(solution)/shard_map/grad_head/pallas_call | solution.py:292
  (70 shorter events, 11.2 us)
Async XLA Ops:
  7.2 46.7 %all-gather.3.cloned.1.call-start = ((), (), s32[]{:S(2)}) async-start(), calls=%async_computation.4 | async-start | bytes 2359296 | tf_op jit(solution)/shard_map/all_gather | solution.py:326
  7.2 38.4 %collective-permute-start = (bf16[594,4096]{1,0:T(8,128)(2,1)}, bf16[594,4096]{1,0:T(8,128)(2,1)}, u32[]{:S(2)}, u32[]{:S(2)}) collective-permute-start(bf16[594,4096]{1,0:T(8,128)(2,1)} %bitcast.8), channel_id=1, source_target_pairs={{0,16},{16,0},{1,17},{17,1},{2,18},{18,2},{3,19},{19,3},{4,20},{20... | collective-permute-start | bytes 14598152 | tf_op jit(solution)/shard_map/ppermute | solution.py:42
  9.2 21.8 %copy-start.4 = (s32[512]{0:T(512)S(1)}, s32[512]{0:T(512)}, u32[]{:S(2)}) copy-start(s32[512]{0:T(512)} %param.11) | copy-start | bytes 6148
  9.2 21.8 %copy-start.7 = (f32[64]{0:T(128)S(1)}, f32[64]{0:T(128)}, u32[]{:S(2)}) copy-start(f32[64]{0:T(128)} %param.14) | copy-start | bytes 772
  9.2 21.9 %copy-start.5 = (s32[512]{0:T(512)S(1)}, s32[512]{0:T(512)}, u32[]{:S(2)}) copy-start(s32[512]{0:T(512)} %param.13) | copy-start | bytes 6148
  9.2 22.1 %copy-start.6 = (f32[512]{0:T(512)S(1)}, f32[512]{0:T(512)}, u32[]{:S(2)}) copy-start(f32[512]{0:T(512)} %param.15) | copy-start | bytes 6148
  10.6 11.6 %all-to-all-start = ((bf16[4,64,128]{2,1,0:T(8,128)(2,1)}), bf16[4,64,128]{2,1,0:T(8,128)(2,1)S(1)}, u32[]{:S(2)}, u32[]{:S(2)}) async-start(bf16[4,64,128]{2,1,0:T(8,128)(2,1)} %broadcast_in_dim.44), calls=%async_computation | async-start | bytes 131072 | tf_op jit(solution)/shard_map/all_to_all | solution.py:38
  23.4 22.1 %all-to-all-start.1 = ((bf16[16,256,128]{2,1,0:T(8,128)(2,1)}), bf16[16,256,128]{2,1,0:T(8,128)(2,1)S(1)}, u32[]{:S(2)}, u32[]{:S(2)}) async-start(bf16[16,256,128]{2,1,0:T(8,128)(2,1)} %broadcast_in_dim.46), calls=%async_computation.1 | async-start | bytes 2097152 | tf_op jit(solution)/shard_map/all_to_all | solution.py:38
  30.9 76.3 %all-gather.5.cloned.1.call-start = ((), (), s32[]{:S(2)}) async-start(), calls=%async_computation.5 | async-start | bytes 2359296 | tf_op jit(solution)/shard_map/all_gather | solution.py:347
  32.7 17.4 %collective-permute-start.1 = (f32[4,256]{1,0:T(4,128)S(1)}, f32[4,256]{1,0:T(4,128)S(1)}, u32[]{:S(2)}, u32[]{:S(2)}) collective-permute-start(f32[4,256]{1,0:T(4,128)S(1)} %select_n.54.info), channel_id=1, source_target_pairs={{0,128},{128,0},{1,129},{129,1},{2,130},{130,2},{3,131},{131,3},{4... | collective-permute-start | bytes 12296 | tf_op jit(solution)/shard_map/ppermute | solution.py:42
  54.1 24.6 %copy-start = (bf16[512,2048]{1,0:T(8,128)(2,1)S(1)}, bf16[512,2048]{1,0:T(8,128)(2,1)}, u32[]{:S(2)}) copy-start(bf16[512,2048]{1,0:T(8,128)(2,1)} %all-gather.3.cloned.1.call-done.straight.other_straight.refs_4_.refs_5_) | copy-start | bytes 6291460
  62.4 4.1 %collective-permute-start.4 = (f32[4,256]{1,0:T(4,128)S(1)}, f32[4,256]{1,0:T(4,128)S(1)}, u32[]{:S(2)}, u32[]{:S(2)}) collective-permute-start(f32[4,256]{1,0:T(4,128)S(1)} %get-tuple-element.32), channel_id=1, source_target_pairs={{0,96},{32,0},{64,32},{96,64},{1,97},{33,1},{65,33},{97,65},{2,98}... | collective-permute-start | bytes 12296 | tf_op jit(solution)/shard_map/ppermute | solution.py:29
  65.2 4.6 %collective-permute-start.3 = (f32[4,256]{1,0:T(4,128)S(1)}, f32[4,256]{1,0:T(4,128)S(1)}, u32[]{:S(2)}, u32[]{:S(2)}) collective-permute-start(f32[4,256]{1,0:T(4,128)S(1)} %get-tuple-element.32), channel_id=1, source_target_pairs={{0,64},{32,96},{64,0},{96,32},{1,65},{33,97},{65,1},{97,33},{2,66}... | collective-permute-start | bytes 12296 | tf_op jit(solution)/shard_map/ppermute | solution.py:29
  65.2 5.5 %collective-permute-start.2 = (f32[4,256]{1,0:T(4,128)S(1)}, f32[4,256]{1,0:T(4,128)S(1)}, u32[]{:S(2)}, u32[]{:S(2)}) collective-permute-start(f32[4,256]{1,0:T(4,128)S(1)} %get-tuple-element.32), channel_id=1, source_target_pairs={{0,32},{32,64},{64,96},{96,0},{1,33},{33,65},{65,97},{97,1},{2,34}... | collective-permute-start | bytes 12296 | tf_op jit(solution)/shard_map/ppermute | solution.py:29
  71.4 13.5 %all-to-all-start.2 = ((f32[16,4,256]{2,1,0:T(4,128)}), f32[16,4,256]{2,1,0:T(4,128)S(1)}, u32[]{:S(2)}, u32[]{:S(2)}) async-start(f32[16,4,256]{2,1,0:T(4,128)} %broadcast_in_dim.47), calls=%async_computation.2 | async-start | bytes 131072 | tf_op jit(solution)/shard_map/all_to_all | solution.py:38
  78.7 34.8 %collective-permute-start.8 = (bf16[512,2048]{1,0:T(8,128)(2,1)S(1)}, bf16[512,2048]{1,0:T(8,128)(2,1)}, u32[]{:S(2)}, u32[]{:S(2)}) collective-permute-start(bf16[512,2048]{1,0:T(8,128)(2,1)S(1)} %copy-done), channel_id=1, source_target_pairs={{0,16},{16,0},{1,17},{17,1},{2,18},{18,2},{3,19},{19,3},{4,20},{20... | collective-permute-start | bytes 6291464 | tf_op jit(solution)/shard_map/ppermute | solution.py:42
  93.8 29.4 %all-to-all-start.3 = ((bf16[16,16,4096]{2,1,0:T(8,128)(2,1)}), bf16[16,16,4096]{2,1,0:T(8,128)(2,1)}, u32[]{:S(2)}, u32[]{:S(2)}) async-start(bf16[16,16,4096]{2,1,0:T(8,128)(2,1)} %bitcast.14), calls=%async_computation.3 | async-start | bytes 4194304 | tf_op jit(solution)/shard_map/all_to_all | solution.py:359
  99.7 7.5 %collective-permute-start.5 = (f32[3,256]{1,0:T(4,128)S(1)}, f32[3,256]{1,0:T(4,128)S(1)}, u32[]{:S(2)}, u32[]{:S(2)}) collective-permute-start(f32[3,256]{1,0:T(4,128)S(1)} %get-tuple-element.39), channel_id=1, source_target_pairs={{0,128},{128,0},{1,129},{129,1},{2,130},{130,2},{3,131},{131,3},{4... | collective-permute-start | bytes 9224 | tf_op jit(solution)/shard_map/ppermute | solution.py:42
  102.6 10.8 %collective-permute-start.6 = (bf16[594,256]{1,0:T(8,128)(2,1)S(1)}, bf16[594,256]{1,0:T(8,128)(2,1)S(1)}, u32[]{:S(2)}, u32[]{:S(2)}) collective-permute-start(bf16[594,256]{1,0:T(8,128)(2,1)S(1)} %copy-done.8), channel_id=1, source_target_pairs={{0,16},{16,0},{1,17},{17,1},{2,18},{18,2},{3,19},{19,3},{4,20},{20... | collective-permute-start | bytes 912392 | tf_op jit(solution)/shard_map/ppermute | solution.py:42
  113.5 1.8 %collective-permute-start.7 = (bf16[594,256]{1,0:T(8,128)(2,1)}, bf16[594,256]{1,0:T(8,128)(2,1)S(1)}, u32[]{:S(2)}, u32[]{:S(2)}) collective-permute-start(bf16[594,256]{1,0:T(8,128)(2,1)} %get-tuple-element.44), channel_id=1, source_target_pairs={{0,16},{16,0},{1,17},{17,1},{2,18},{18,2},{3,19},{19,3},{4,20},{20... | collective-permute-start | bytes 912392 | tf_op jit(solution)/shard_map/ppermute | solution.py:42
  123.3 5.2 %collective-permute-start.12 = (bf16[512,2048]{1,0:T(8,128)(2,1)S(1)}, bf16[512,2048]{1,0:T(8,128)(2,1)}, u32[]{:S(2)}, u32[]{:S(2)}) collective-permute-start(bf16[512,2048]{1,0:T(8,128)(2,1)S(1)} %copy-done.1), channel_id=1, source_target_pairs={{0,16},{16,0},{1,17},{17,1},{2,18},{18,2},{3,19},{19,3},{4,20},{20... | collective-permute-start | bytes 6291464 | tf_op jit(solution)/shard_map/ppermute | solution.py:42
  125.3 9.8 %collective-permute-start.11 = (bf16[4,4096]{1,0:T(4,128)(2,1)S(1)}, bf16[4,4096]{1,0:T(4,128)(2,1)S(1)}, u32[]{:S(2)}, u32[]{:S(2)}) collective-permute-start(bf16[4,4096]{1,0:T(4,128)(2,1)S(1)} %get-tuple-element.60), channel_id=1, source_target_pairs={{0,96},{32,0},{64,32},{96,64},{1,97},{33,1},{65,33},{97,65},{2,98}... | collective-permute-start | bytes 98312 | tf_op jit(solution)/shard_map/ppermute | solution.py:384
  125.8 9.3 %collective-permute-start.10 = (bf16[4,4096]{1,0:T(4,128)(2,1)S(1)}, bf16[4,4096]{1,0:T(4,128)(2,1)S(1)}, u32[]{:S(2)}, u32[]{:S(2)}) collective-permute-start(bf16[4,4096]{1,0:T(4,128)(2,1)S(1)} %get-tuple-element.61), channel_id=1, source_target_pairs={{0,64},{32,96},{64,0},{96,32},{1,65},{33,97},{65,1},{97,33},{2,66}... | collective-permute-start | bytes 98312 | tf_op jit(solution)/shard_map/ppermute | solution.py:384
  126.5 8.6 %collective-permute-start.9 = (bf16[4,4096]{1,0:T(4,128)(2,1)S(1)}, bf16[4,4096]{1,0:T(4,128)(2,1)S(1)}, u32[]{:S(2)}, u32[]{:S(2)}) collective-permute-start(bf16[4,4096]{1,0:T(4,128)(2,1)S(1)} %get-tuple-element.62), channel_id=1, source_target_pairs={{0,32},{32,64},{64,96},{96,0},{1,33},{33,65},{65,97},{97,1},{2,34}... | collective-permute-start | bytes 98312 | tf_op jit(solution)/shard_map/ppermute | solution.py:384
  (4 other events, 18.6 us)
Sparse Core Ops, SparseCore 0:
  9.8 44.0 all-gather.2
  55.7 39.8 all-gather.4

commit v11 on v9

--- a/solution.py
+++ b/solution.py
@@ -242,12 +242,8 @@
     )(scalars, target, info, parts, *logits, *weights)
 
 
-def other_kernel(
-    s, target, info, final, straight, straight2, weight0, weight1, grad0, grad1, logits0, logits1
-):
-    step = pl.program_id(0)
-
-    @pl.when(step == 0)
+def other_kernel(s, straight, straight2, weight0, weight1, logits0, logits1):
+    @pl.when(pl.program_id(0) == 0)
     def _():
         logits0[...] = jnp.zeros_like(logits0)
         logits1[...] = jnp.zeros_like(logits1)
@@ -257,28 +253,36 @@
         lambda: add_logits(straight2[...], (weight0, weight1), (logits0, logits1)),
     )
 
-    @pl.when(step == pl.num_programs(0) - 1)
-    def _():
-        ends = [final[i : i + 1, :] for i in range(3)]
-        for k, (logits, grad) in enumerate(((logits0, grad0), (logits1, grad1))):
-            grad[...] = logit_gradient(logits[...], s[2 + k], target, info, ends)
-
-
-def other_gradient(scalars, target, info, final, straights, weights):
+
+def other_gradient_kernel(first, target, info, final, logits0, logits1, grad0, grad1):
+    ends = [final[i : i + 1, :] for i in range(3)]
+    for k, (logits, grad) in enumerate(((logits0, grad0), (logits1, grad1))):
+        grad[...] = logit_gradient(logits[...], first[2 + k], target, info, ends)
+
+
+def other_logits(scalars, tokens, straights, weights):
     width, depth = weights[0].shape
-    tokens = info.shape[1]
     return call(
         other_kernel,
-        "other_group_grad_logits",
+        "other_group_logits",
         depth,
-        [whole(1, tokens), whole(4, tokens), whole(3, tokens)]
-        + hidden_specs(tokens, depth, 1)
-        + [tiles(width)] * 2,
+        hidden_specs(tokens, depth, 1) + [tiles(width)] * 2,
         [whole(width, tokens)] * 2,
-        [pltpu.HBM((width, tokens), jnp.bfloat16)] * 2,
-        [pltpu.VMEM((width, tokens), jnp.float32)] * 2,
-        flops=4 * tokens * width * depth,
-    )(scalars, target, info, final, *straights, *weights)
+        [pltpu.HBM((width, tokens), jnp.float32)] * 2,
+    )(scalars, *straights, *weights)
+
+
+def other_gradient(scalars, target, info, final, logits):
+    width, tokens = logits[0].shape
+    return pl.pallas_call(
+        other_gradient_kernel,
+        in_specs=[pl.BlockSpec(memory_space=pltpu.SMEM)]
+        + [pl.BlockSpec(memory_space=pltpu.VMEM)] * 5,
+        out_specs=[pl.BlockSpec(memory_space=pltpu.VMEM)] * 2,
+        out_shape=[pltpu.HBM((width, tokens), jnp.bfloat16)] * 2,
+        compiler_params=PARAMS,
+        name="other_group_grad_logits",
+    )(scalars, target, info, final, *logits)
 
 
 def head_kernel(s, *refs, count):
@@ -363,11 +367,12 @@
         scalars, own_target, own, parts, logits, weights, nz, nv
     )
     got = lax.all_to_all(partial.reshape(nv, nz * rows, depth), ("x", "y"), 0, 0, tiled=True)
+    moved = swap(final, "dp")
+    straight2, own1 = lax.optimization_barrier((straight2, own1))
     gathered = (in_hbm(straight), in_hbm(straight2))
-    other0, other1 = other_gradient(
-        scalars, other_target, other, swap(final, "dp"), gathered, weights
-    )
-    own1, other1 = lax.optimization_barrier((own1, other1))
+    logits = other_logits(scalars, nz * block, gathered, weights)
+    moved, logits = lax.optimization_barrier((moved, logits))
+    other0, other1 = other_gradient(scalars, other_target, other, moved, logits)
     grads = [
         in_hbm(grad) for grad in (own0, other0, swap(own1, "core"), swap(other1, "core"))
     ]

time: 144 us -> 143 us (level)
  waiting for transfers between devices: 34.2 us -> 29.4 us
  local copies, waits for them, and re-layouts: 6.96 us -> 9.19 us
  Pallas kernels: 41.5 us -> 43 us
    ppermute x7, waiting for transfers between devices: 6.41 us -> 1.69 us  [swap(): return lax.ppermute(value, axis, [(0, 1), (1, 0)])]
    unnamed x21 -> x25, local copies, waits for them, and re-layouts: 0.78 us -> 2.99 us
    pallas_call x1 -> x2, Pallas kernels: 8.16 us -> 9.63 us  [the longest x1 7.83 us: other_logits(): call(other_kernel, 'other_group_logits', depth, hidden_specs(tokens, dept...]
  transfers between devices with their start and end apart: 19 -> 19, of which waited for: 10 -> 8; matrix products, arithmetic and copies ran while one was open for 7% -> 7% of each run, Pallas kernels for 29% -> 30%
where the time goes in v11:
time: 143 us; the launch traced here: 141 us
  Pallas kernels  43 us (30%)
  starting transfers between devices  40.7 us (28%)
  waiting for transfers between devices  29.4 us (21%)
  between operations  14.2 us (10%)
  local copies, waits for them, and re-layouts  9.19 us (6%)
  other arithmetic  4.85 us (3%)
    all_to_all x3, starting transfers between devices, spread(): return lax.all_to_all(copies, axis, 0, 0, tiled=True)  20.7 us
    all_to_all x3, waiting for transfers between devices, spread(): return lax.all_to_all(copies, axis, 0, 0, tiled=True)  18.8 us
    pallas_call x2, Pallas kernels, head_half(): pl.pallas_call(functools.partial(head_kernel, count=4), grid_spec=pltpu.P...  13.3 us
    pallas_call x1, Pallas kernels, gradient_partial(): call(functools.partial(gradient_kernel, nz=nz, nv=nv), 'grad_hidden_parti...  8.92 us
    ppermute x7, starting transfers between devices, swap(): return lax.ppermute(value, axis, [(0, 1), (1, 0)])  8.36 us
    pallas_call x1, Pallas kernels, other_logits(): call(other_kernel, 'other_group_logits', depth, hidden_specs(tokens, dept...  7.83 us
    pallas_call x1, Pallas kernels, logits_and_stats(): pl.pallas_call(logits_kernel, grid_spec=pltpu.PrefetchScalarGridSpec(num_...  6.61 us
    all_to_all x1, starting transfers between devices, per_device(): lax.all_to_all(partial.reshape(nv, nz * rows, depth), ('x', 'y'), 0, 0, t...  5.67 us
  transfers between devices with their start and end apart: 19, of which 8 were waited for; matrix products, arithmetic and copies ran while one was open for 7% of the time, Pallas kernels for 30%

profile of v11, /device:TPU:2, one launch (start us, length us, event | category | flops | bytes accessed | tf_op | source)
XLA Modules:
  0.0 141.4 jit_solution(12930688616158332902)
XLA Ops:
  7.3 1.9 %fusion.8 = (bf16[64,2048]{1,0:T(8,128)(2,1)}, bf16[64,2048]{1,0:T(8,128)(2,1)}) fusion(bf16[64,4096]{1,0:T(8,128)(2,1)} %param.8), kind=kLoop, calls=%fused_computation.40 | loop fusion | bytes 1048576 | tf_op jit(solution)/shard_map/slice | solution.py:336
  10.7 5.9 %all-to-all-start = ((bf16[4,64,128]{2,1,0:T(8,128)(2,1)}), bf16[4,64,128]{2,1,0:T(8,128)(2,1)S(1)}, u32[]{:S(2)}, u32[]{:S(2)}) async-start(bf16[4,64,128]{2,1,0:T(8,128)(2,1)} %broadcast_in_dim.44), calls=%async_computation | async-start | bytes 131072 | tf_op jit(solution)/shard_map/all_to_all | solution.py:38
  18.0 4.3 %all-to-all-done = bf16[4,64,128]{2,1,0:T(8,128)(2,1)S(1)} async-done(((bf16[4,64,128]{2,1,0:T(8,128)(2,1)}), bf16[4,64,128]{2,1,0:T(8,128)(2,1)S(1)}, u32[]{:S(2)}, u32[]{:S(2)}) %all-to-all-start) | async-done | bytes 65568 | tf_op jit(solution)/shard_map/all_to_all | solution.py:38
  22.3 1.2 broadcast_in_dim.46
  23.5 7.5 %all-to-all-start.1 = ((bf16[16,256,128]{2,1,0:T(8,128)(2,1)}), bf16[16,256,128]{2,1,0:T(8,128)(2,1)S(1)}, u32[]{:S(2)}, u32[]{:S(2)}) async-start(bf16[16,256,128]{2,1,0:T(8,128)(2,1)} %broadcast_in_dim.46), calls=%async_computation.1 | async-start | bytes 2097152 | tf_op jit(solution)/shard_map/all_to_all | solution.py:38
  32.7 4.6 %collective-permute-start.1 = (f32[4,256]{1,0:T(4,128)S(1)}, f32[4,256]{1,0:T(4,128)S(1)}, u32[]{:S(2)}, u32[]{:S(2)}) collective-permute-start(f32[4,256]{1,0:T(4,128)S(1)} %select_n.54.info), channel_id=1, source_target_pairs={{0,128},{128,0},{1,129},{129,1},{2,130},{130,2},{3,131},{131,3},{4... | collective-permute-start | bytes 12296 | tf_op jit(solution)/shard_map/ppermute | solution.py:42
  37.3 8.3 %all-to-all-done.1.pieces = bf16[16,256,128]{2,1,0:T(8,128)(2,1)S(1)} async-done(((bf16[16,256,128]{2,1,0:T(8,128)(2,1)}), bf16[16,256,128]{2,1,0:T(8,128)(2,1)S(1)}, u32[]{:S(2)}, u32[]{:S(2)}) %all-to-all-start.1) | async-done | bytes 1048608 | tf_op jit(solution)/shard_map/all_to_all | solution.py:38
  45.6 4.5 %logits_second_half.1 = (f32[594,256]{1,0:T(8,128)}, f32[594,256]{1,0:T(8,128)}) custom-call(bf16[16,256,128]{2,1,0:T(8,128)(2,1)S(1)} %all-to-all-done.1.pieces, bf16[594,4096]{1,0:T(8,128)(2,1)} %bitcast.9, bf16[594,4096]{1,0:T(8,128)(2,1)} %collective-permute-done.weight1), custom_call_target="tpu_custom_call" | custom-call | tf_op jit(solution)/shard_map/logits_second_half/pallas_call | solution.py:114
  50.2 4.1 %all-gather.3.cloned.1.call-done.straight.refs_4_.refs_5_ = bf16[512,2048]{1,0:T(8,128)(2,1)} async-done(((bf16[64,2048]{1,0:T(8,128)(2,1)}), bf16[512,2048]{1,0:T(8,128)(2,1)}) %all-gather.3.cloned.1.call-update) | async-done | bytes 2097168 | tf_op jit(solution)/shard_map/all_gather | solution.py:336
  54.5 6.6 %logits.1 = (f32[594,256]{1,0:T(8,128)}, f32[594,256]{1,0:T(8,128)}, f32[4,256]{1,0:T(4,128)S(1)}) custom-call(s32[4]{0:T(128)S(1)} %pad_add_fusion.s.first, s32[1,256]{1,0:T(1,128)S(1)} %convert_element_type.39.target, bf16[512,2048]{1,0:T(8,128)(2,1)} %all-gather.3.cloned.1.call-done.straight.refs_4_.refs_5_, f32[594,256]{1,0:T(8,128)} %get-tuple-element.35.before0, ...), custom_call_target="tpu_custom_call" | custom-call | tf_op jit(solution)/shard_map/logits/pallas_call | solution.py:162
  61.1 2.5 %collective-permute-start.4 = (f32[4,256]{1,0:T(4,128)S(1)}, f32[4,256]{1,0:T(4,128)S(1)}, u32[]{:S(2)}, u32[]{:S(2)}) collective-permute-start(f32[4,256]{1,0:T(4,128)S(1)} %get-tuple-element.37), channel_id=1, source_target_pairs={{0,96},{32,0},{64,32},{96,64},{1,97},{33,1},{65,33},{97,65},{2,98}... | collective-permute-start | bytes 12296 | tf_op jit(solution)/shard_map/ppermute | solution.py:29
  64.8 3.3 %collective-permute-done.3 = f32[4,256]{1,0:T(4,128)S(1)} collective-permute-done((f32[4,256]{1,0:T(4,128)S(1)}, f32[4,256]{1,0:T(4,128)S(1)}, u32[]{:S(2)}, u32[]{:S(2)}) %collective-permute-start.3) | collective-permute-done | bytes 4128 | tf_op jit(solution)/shard_map/ppermute | solution.py:29
  69.7 7.3 %all-to-all-start.2 = ((f32[16,4,256]{2,1,0:T(4,128)}), f32[16,4,256]{2,1,0:T(4,128)S(1)}, u32[]{:S(2)}, u32[]{:S(2)}) async-start(f32[16,4,256]{2,1,0:T(4,128)} %broadcast_in_dim.47), calls=%async_computation.2 | async-start | bytes 131072 | tf_op jit(solution)/shard_map/all_to_all | solution.py:38
  77.1 6.2 %all-to-all-done.2.parts = f32[16,4,256]{2,1,0:T(4,128)S(1)} async-done(((f32[16,4,256]{2,1,0:T(4,128)}), f32[16,4,256]{2,1,0:T(4,128)S(1)}, u32[]{:S(2)}, u32[]{:S(2)}) %all-to-all-start.2) | async-done | bytes 65568 | tf_op jit(solution)/shard_map/all_to_all | solution.py:38
  83.3 8.9 %grad_hidden_partial.1 = (bf16[256,4096]{1,0:T(8,128)(2,1)}, bf16[594,256]{1,0:T(8,128)(2,1)}, bf16[594,256]{1,0:T(8,128)(2,1)}, f32[3,256]{1,0:T(4,128)S(1)}) custom-call(s32[4]{0:T(128)S(1)} %pad_add_fusion.s.first, s32[1,256]{1,0:T(1,128)S(1)} %convert_element_type.39.target, f32[4,256]{1,0:T(4,128)S(1)} %select_n.54.info, ...), custom_call_target="tpu_custom_call" | custom-call | flops 2491416576 | bytes 4982833 | tf_op jit(solution)/shard_map/grad_hidden_partial/pallas_call | solution.py:229
  92.2 5.7 %all-to-all-start.3 = ((bf16[16,16,4096]{2,1,0:T(8,128)(2,1)}), bf16[16,16,4096]{2,1,0:T(8,128)(2,1)}, u32[]{:S(2)}, u32[]{:S(2)}) async-start(bf16[16,16,4096]{2,1,0:T(8,128)(2,1)} %bitcast.14), calls=%async_computation.3 | async-start | bytes 4194304 | tf_op jit(solution)/shard_map/all_to_all | solution.py:369
  97.9 2.8 %collective-permute-start.5 = (f32[3,256]{1,0:T(4,128)S(1)}, f32[3,256]{1,0:T(4,128)S(1)}, u32[]{:S(2)}, u32[]{:S(2)}) collective-permute-start(f32[3,256]{1,0:T(4,128)S(1)} %get-tuple-element.46), channel_id=1, source_target_pairs={{0,128},{128,0},{1,129},{129,1},{2,130},{130,2},{3,131},{131,3},{4... | collective-permute-start | bytes 9224 | tf_op jit(solution)/shard_map/ppermute | solution.py:42
  100.7 7.8 %other_group_logits.1 = (f32[594,256]{1,0:T(8,128)}, f32[594,256]{1,0:T(8,128)}) custom-call(s32[4]{0:T(128)S(1)} %pad_add_fusion.s.first, bf16[512,2048]{1,0:T(8,128)(2,1)} %all-gather.3.cloned.1.call-done.straight.refs_4_.refs_5_, bf16[512,2048]{1,0:T(8,128)(2,1)} %all-gather.5.cloned.1.call-done.straight2.refs_4_.refs_5_, bf16[594,4096]{1,0:T(8,128)(2,1)} %bitcast.12, ...), custom_call_target="tpu_custom_call" | custom-call | tf_op jit(solution)/shard_map/other_group_logits/pallas_call | solution.py:265
  110.7 1.8 %other_group_grad_logits.1 = (bf16[594,256]{1,0:T(8,128)(2,1)}, bf16[594,256]{1,0:T(8,128)(2,1)}) custom-call(s32[4]{0:T(128)S(1)} %pad_add_fusion.s.first, s32[1,256]{1,0:T(1,128)S(1)} %slice_convert_fusion.1.target, f32[4,256]{1,0:T(4,128)S(1)} %collective-permute-done.1.info, f32[3,256]{1,0:T(4,128)S(1)} %collective-permute-done.5.final, ...), custom_call_target="tpu_custom_call" | custom-call | tf_op jit(solution)/shard_map/other_group_grad_logits/pallas_call | solution.py:277
  113.0 1.7 %collective-permute-done.7.refs_3_ = bf16[594,256]{1,0:T(8,128)(2,1)S(1)} collective-permute-done((bf16[594,256]{1,0:T(8,128)(2,1)}, bf16[594,256]{1,0:T(8,128)(2,1)S(1)}, u32[]{:S(2)}, u32[]{:S(2)}) %collective-permute-start.7) | collective-permute-done | bytes 304160 | tf_op jit(solution)/shard_map/ppermute | solution.py:42
  115.5 6.7 %grad_head.2.refs_8_ = bf16[594,4096]{1,0:T(8,128)(2,1)} custom-call(s32[4]{0:T(128)S(1)} %pad_add_fusion.s.first, bf16[594,256]{1,0:T(8,128)(2,1)} %get-tuple-element.44.refs_0_, bf16[594,256]{1,0:T(8,128)(2,1)} %get-tuple-element.52.refs_1_, bf16[594,256]{1,0:T(8,128)(2,1)} %copy-done.5, bf16[594,256]{1,0:T(8,128)(2,1)} %copy-done.4, ...), custom_call_target="tpu_custom_call" | custom-call | tf_op jit(solution)/shard_map/grad_head/pallas_call | solution.py:302
  122.4 1.9 %reduce_sum.32 = bf16[16,4096]{1,0:T(8,128)(2,1)S(1)} reduce(bf16[16,16,4096]{2,1,0:T(8,128)(2,1)} %all-to-all-done.3, bf16[]{:T(256)} %constant.63.clone.1), dimensions={0}, to_apply=%region_2.3 | reduce | flops 983040 | bytes 2228226 | tf_op jit(solution)/shard_map/reduce_sum | solution.py:384
  125.3 1.9 %collective-permute-start.9 = (bf16[4,4096]{1,0:T(4,128)(2,1)S(1)}, bf16[4,4096]{1,0:T(4,128)(2,1)S(1)}, u32[]{:S(2)}, u32[]{:S(2)}) collective-permute-start(bf16[4,4096]{1,0:T(4,128)(2,1)S(1)} %get-tuple-element.72), channel_id=1, source_target_pairs={{0,32},{32,64},{64,96},{96,0},{1,33},{33,65},{65,97},{97,1},{2,34}... | collective-permute-start | bytes 98312 | tf_op jit(solution)/shard_map/ppermute | solution.py:390
  127.2 6.6 %grad_head.3 = bf16[594,4096]{1,0:T(8,128)(2,1)} custom-call(s32[4]{0:T(128)S(1)} %pad_add_fusion.s.first, bf16[594,256]{1,0:T(8,128)(2,1)} %get-tuple-element.44.refs_0_, bf16[594,256]{1,0:T(8,128)(2,1)} %get-tuple-element.52.refs_1_, bf16[594,256]{1,0:T(8,128)(2,1)} %copy-done.5, bf16[594,256]{1,0:T(8,128)(2,1)} %copy-done.4, ...), custom_call_target="tpu_custom_call", output_to_operand_aliasing={{}: (9, {})} | custom-call | tf_op jit(solution)/shard_map/grad_head/pallas_call | solution.py:302
  (75 shorter events, 13.2 us)
Async XLA Ops:
  7.2 47.1 %all-gather.3.cloned.1.call-start = ((), (), s32[]{:S(2)}) async-start(), calls=%async_computation.4 | async-start | bytes 2359296 | tf_op jit(solution)/shard_map/all_gather | solution.py:336
  7.2 38.4 %collective-permute-start = (bf16[594,4096]{1,0:T(8,128)(2,1)}, bf16[594,4096]{1,0:T(8,128)(2,1)}, u32[]{:S(2)}, u32[]{:S(2)}) collective-permute-start(bf16[594,4096]{1,0:T(8,128)(2,1)} %bitcast.8), channel_id=1, source_target_pairs={{0,16},{16,0},{1,17},{17,1},{2,18},{18,2},{3,19},{19,3},{4,20},{20... | collective-permute-start | bytes 14598152 | tf_op jit(solution)/shard_map/ppermute | solution.py:42
  9.2 21.8 %copy-start.6 = (s32[512]{0:T(512)S(1)}, s32[512]{0:T(512)}, u32[]{:S(2)}) copy-start(s32[512]{0:T(512)} %param.11) | copy-start | bytes 6148
  9.2 21.8 %copy-start.9 = (f32[64]{0:T(128)S(1)}, f32[64]{0:T(128)}, u32[]{:S(2)}) copy-start(f32[64]{0:T(128)} %param.14) | copy-start | bytes 772
  9.2 21.9 %copy-start.7 = (s32[512]{0:T(512)S(1)}, s32[512]{0:T(512)}, u32[]{:S(2)}) copy-start(s32[512]{0:T(512)} %param.13) | copy-start | bytes 6148
  9.2 22.1 %copy-start.8 = (f32[512]{0:T(512)S(1)}, f32[512]{0:T(512)}, u32[]{:S(2)}) copy-start(f32[512]{0:T(512)} %param.15) | copy-start | bytes 6148
  10.7 11.6 %all-to-all-start = ((bf16[4,64,128]{2,1,0:T(8,128)(2,1)}), bf16[4,64,128]{2,1,0:T(8,128)(2,1)S(1)}, u32[]{:S(2)}, u32[]{:S(2)}) async-start(bf16[4,64,128]{2,1,0:T(8,128)(2,1)} %broadcast_in_dim.44), calls=%async_computation | async-start | bytes 131072 | tf_op jit(solution)/shard_map/all_to_all | solution.py:38
  23.5 22.1 %all-to-all-start.1 = ((bf16[16,256,128]{2,1,0:T(8,128)(2,1)}), bf16[16,256,128]{2,1,0:T(8,128)(2,1)S(1)}, u32[]{:S(2)}, u32[]{:S(2)}) async-start(bf16[16,256,128]{2,1,0:T(8,128)(2,1)} %broadcast_in_dim.46), calls=%async_computation.1 | async-start | bytes 2097152 | tf_op jit(solution)/shard_map/all_to_all | solution.py:38
  31.0 69.7 %all-gather.5.cloned.1.call-start = ((), (), s32[]{:S(2)}) async-start(), calls=%async_computation.5 | async-start | bytes 2359296 | tf_op jit(solution)/shard_map/all_gather | solution.py:357
  32.7 17.4 %collective-permute-start.1 = (f32[4,256]{1,0:T(4,128)S(1)}, f32[4,256]{1,0:T(4,128)S(1)}, u32[]{:S(2)}, u32[]{:S(2)}) collective-permute-start(f32[4,256]{1,0:T(4,128)S(1)} %select_n.54.info), channel_id=1, source_target_pairs={{0,128},{128,0},{1,129},{129,1},{2,130},{130,2},{3,131},{131,3},{4... | collective-permute-start | bytes 12296 | tf_op jit(solution)/shard_map/ppermute | solution.py:42
  54.4 22.6 %copy-start.2 = (bf16[512,2048]{1,0:T(8,128)(2,1)S(1)}, bf16[512,2048]{1,0:T(8,128)(2,1)}, u32[]{:S(2)}) copy-start(bf16[512,2048]{1,0:T(8,128)(2,1)} %all-gather.3.cloned.1.call-done.straight.refs_4_.refs_5_) | copy-start | bytes 6291460
  61.1 3.8 %collective-permute-start.4 = (f32[4,256]{1,0:T(4,128)S(1)}, f32[4,256]{1,0:T(4,128)S(1)}, u32[]{:S(2)}, u32[]{:S(2)}) collective-permute-start(f32[4,256]{1,0:T(4,128)S(1)} %get-tuple-element.37), channel_id=1, source_target_pairs={{0,96},{32,0},{64,32},{96,64},{1,97},{33,1},{65,33},{97,65},{2,98}... | collective-permute-start | bytes 12296 | tf_op jit(solution)/shard_map/ppermute | solution.py:29
  63.5 4.6 %collective-permute-start.3 = (f32[4,256]{1,0:T(4,128)S(1)}, f32[4,256]{1,0:T(4,128)S(1)}, u32[]{:S(2)}, u32[]{:S(2)}) collective-permute-start(f32[4,256]{1,0:T(4,128)S(1)} %get-tuple-element.37), channel_id=1, source_target_pairs={{0,64},{32,96},{64,0},{96,32},{1,65},{33,97},{65,1},{97,33},{2,66}... | collective-permute-start | bytes 12296 | tf_op jit(solution)/shard_map/ppermute | solution.py:29
  63.5 5.5 %collective-permute-start.2 = (f32[4,256]{1,0:T(4,128)S(1)}, f32[4,256]{1,0:T(4,128)S(1)}, u32[]{:S(2)}, u32[]{:S(2)}) collective-permute-start(f32[4,256]{1,0:T(4,128)S(1)} %get-tuple-element.37), channel_id=1, source_target_pairs={{0,32},{32,64},{64,96},{96,0},{1,33},{33,65},{65,97},{97,1},{2,34}... | collective-permute-start | bytes 12296 | tf_op jit(solution)/shard_map/ppermute | solution.py:29
  69.7 13.5 %all-to-all-start.2 = ((f32[16,4,256]{2,1,0:T(4,128)}), f32[16,4,256]{2,1,0:T(4,128)S(1)}, u32[]{:S(2)}, u32[]{:S(2)}) async-start(f32[16,4,256]{2,1,0:T(4,128)} %broadcast_in_dim.47), calls=%async_computation.2 | async-start | bytes 131072 | tf_op jit(solution)/shard_map/all_to_all | solution.py:38
  77.0 36.0 %collective-permute-start.8 = (bf16[512,2048]{1,0:T(8,128)(2,1)S(1)}, bf16[512,2048]{1,0:T(8,128)(2,1)}, u32[]{:S(2)}, u32[]{:S(2)}) collective-permute-start(bf16[512,2048]{1,0:T(8,128)(2,1)S(1)} %copy-done.2), channel_id=1, source_target_pairs={{0,16},{16,0},{1,17},{17,1},{2,18},{18,2},{3,19},{19,3},{4,20},{20... | collective-permute-start | bytes 6291464 | tf_op jit(solution)/shard_map/ppermute | solution.py:42
  92.2 30.0 %all-to-all-start.3 = ((bf16[16,16,4096]{2,1,0:T(8,128)(2,1)}), bf16[16,16,4096]{2,1,0:T(8,128)(2,1)}, u32[]{:S(2)}, u32[]{:S(2)}) async-start(bf16[16,16,4096]{2,1,0:T(8,128)(2,1)} %bitcast.14), calls=%async_computation.3 | async-start | bytes 4194304 | tf_op jit(solution)/shard_map/all_to_all | solution.py:369
  97.9 10.7 %collective-permute-start.5 = (f32[3,256]{1,0:T(4,128)S(1)}, f32[3,256]{1,0:T(4,128)S(1)}, u32[]{:S(2)}, u32[]{:S(2)}) collective-permute-start(f32[3,256]{1,0:T(4,128)S(1)} %get-tuple-element.46), channel_id=1, source_target_pairs={{0,128},{128,0},{1,129},{129,1},{2,130},{130,2},{3,131},{131,3},{4... | collective-permute-start | bytes 9224 | tf_op jit(solution)/shard_map/ppermute | solution.py:42
  112.5 2.2 %collective-permute-start.7 = (bf16[594,256]{1,0:T(8,128)(2,1)}, bf16[594,256]{1,0:T(8,128)(2,1)S(1)}, u32[]{:S(2)}, u32[]{:S(2)}) collective-permute-start(bf16[594,256]{1,0:T(8,128)(2,1)} %get-tuple-element.54), channel_id=1, source_target_pairs={{0,16},{16,0},{1,17},{17,1},{2,18},{18,2},{3,19},{19,3},{4,20},{20... | collective-permute-start | bytes 912392 | tf_op jit(solution)/shard_map/ppermute | solution.py:42
  112.5 2.2 %collective-permute-start.6 = (bf16[594,256]{1,0:T(8,128)(2,1)S(1)}, bf16[594,256]{1,0:T(8,128)(2,1)S(1)}, u32[]{:S(2)}, u32[]{:S(2)}) collective-permute-start(bf16[594,256]{1,0:T(8,128)(2,1)S(1)} %copy-done.10), channel_id=1, source_target_pairs={{0,16},{16,0},{1,17},{17,1},{2,18},{18,2},{3,19},{19,3},{4,20},{20... | collective-permute-start | bytes 912392 | tf_op jit(solution)/shard_map/ppermute | solution.py:42
  122.2 5.0 %collective-permute-start.12 = (bf16[512,2048]{1,0:T(8,128)(2,1)S(1)}, bf16[512,2048]{1,0:T(8,128)(2,1)}, u32[]{:S(2)}, u32[]{:S(2)}) collective-permute-start(bf16[512,2048]{1,0:T(8,128)(2,1)S(1)} %copy-done.3), channel_id=1, source_target_pairs={{0,16},{16,0},{1,17},{17,1},{2,18},{18,2},{3,19},{19,3},{4,20},{20... | collective-permute-start | bytes 6291464 | tf_op jit(solution)/shard_map/ppermute | solution.py:42
  124.4 9.5 %collective-permute-start.11 = (bf16[4,4096]{1,0:T(4,128)(2,1)S(1)}, bf16[4,4096]{1,0:T(4,128)(2,1)S(1)}, u32[]{:S(2)}, u32[]{:S(2)}) collective-permute-start(bf16[4,4096]{1,0:T(4,128)(2,1)S(1)} %get-tuple-element.70), channel_id=1, source_target_pairs={{0,96},{32,0},{64,32},{96,64},{1,97},{33,1},{65,33},{97,65},{2,98}... | collective-permute-start | bytes 98312 | tf_op jit(solution)/shard_map/ppermute | solution.py:390
  124.6 9.2 %collective-permute-start.10 = (bf16[4,4096]{1,0:T(4,128)(2,1)S(1)}, bf16[4,4096]{1,0:T(4,128)(2,1)S(1)}, u32[]{:S(2)}, u32[]{:S(2)}) collective-permute-start(bf16[4,4096]{1,0:T(4,128)(2,1)S(1)} %get-tuple-element.71), channel_id=1, source_target_pairs={{0,64},{32,96},{64,0},{96,32},{1,65},{33,97},{65,1},{97,33},{2,66}... | collective-permute-start | bytes 98312 | tf_op jit(solution)/shard_map/ppermute | solution.py:390
  125.3 8.6 %collective-permute-start.9 = (bf16[4,4096]{1,0:T(4,128)(2,1)S(1)}, bf16[4,4096]{1,0:T(4,128)(2,1)S(1)}, u32[]{:S(2)}, u32[]{:S(2)}) collective-permute-start(bf16[4,4096]{1,0:T(4,128)(2,1)S(1)} %get-tuple-element.72), channel_id=1, source_target_pairs={{0,32},{32,64},{64,96},{96,0},{1,33},{33,65},{65,97},{97,1},{2,34}... | collective-permute-start | bytes 98312 | tf_op jit(solution)/shard_map/ppermute | solution.py:390
  (6 other events, 22.2 us)
Sparse Core Ops, SparseCore 0:
  9.8 44.3 all-gather.2
  56.0 39.4 all-gather.4

commit v12 on v11

--- a/solution.py
+++ b/solution.py
@@ -268,7 +268,7 @@
         depth,
         hidden_specs(tokens, depth, 1) + [tiles(width)] * 2,
         [whole(width, tokens)] * 2,
-        [pltpu.HBM((width, tokens), jnp.float32)] * 2,
+        [jax.ShapeDtypeStruct((width, tokens), jnp.float32)] * 2,
     )(scalars, *straights, *weights)
 
 

time: 143 us -> 143 us (level)
  waiting for transfers between devices: 29.4 us -> 31.9 us
  local copies, waits for them, and re-layouts: 9.19 us -> 7.08 us
    all_to_all x1, waiting for transfers between devices: 0.01 us -> 2.41 us  [per_device(): lax.all_to_all(partial.reshape(nv, nz * rows, depth), ('x', 'y'), 0, 0, t...]
    unnamed x25 -> x21, local copies, waits for them, and re-layouts: 2.99 us -> 0.9 us
  transfers between devices with their start and end apart: 19 -> 19, of which waited for: 8 -> 9; matrix products, arithmetic and copies ran while one was open for 7% -> 7% of each run, Pallas kernels for 30% -> 30%
where the time goes in v12:
time: 143 us; the launch traced here: 141 us
  Pallas kernels  42 us (29%)
  starting transfers between devices  40.8 us (29%)
  waiting for transfers between devices  31.9 us (22%)
  between operations  14.2 us (10%)
  local copies, waits for them, and re-layouts  7.08 us (5%)
  other arithmetic  4.85 us (3%)
    all_to_all x3, starting transfers between devices, spread(): return lax.all_to_all(copies, axis, 0, 0, tiled=True)  20.7 us
    all_to_all x3, waiting for transfers between devices, spread(): return lax.all_to_all(copies, axis, 0, 0, tiled=True)  18.8 us
    pallas_call x2, Pallas kernels, head_half(): pl.pallas_call(functools.partial(head_kernel, count=4), grid_spec=pltpu.P...  13.3 us
    pallas_call x1, Pallas kernels, gradient_partial(): call(functools.partial(gradient_kernel, nz=nz, nv=nv), 'grad_hidden_parti...  8.91 us
    ppermute x7, starting transfers between devices, swap(): return lax.ppermute(value, axis, [(0, 1), (1, 0)])  8.16 us
    pallas_call x1, Pallas kernels, other_logits(): call(other_kernel, 'other_group_logits', depth, hidden_specs(tokens, dept...  6.81 us
    pallas_call x1, Pallas kernels, logits_and_stats(): pl.pallas_call(logits_kernel, grid_spec=pltpu.PrefetchScalarGridSpec(num_...  6.62 us
    all_to_all x1, starting transfers between devices, per_device(): lax.all_to_all(partial.reshape(nv, nz * rows, depth), ('x', 'y'), 0, 0, t...  5.66 us
  transfers between devices with their start and end apart: 19, of which 9 were waited for; matrix products, arithmetic and copies ran while one was open for 7% of the time, Pallas kernels for 30%

profile of v12, /device:TPU:2, one launch (start us, length us, event | category | flops | bytes accessed | tf_op | source)
XLA Modules:
  0.0 140.8 jit_solution(15250163007384971245)
XLA Ops:
  7.3 1.9 %fusion.8 = (bf16[64,2048]{1,0:T(8,128)(2,1)}, bf16[64,2048]{1,0:T(8,128)(2,1)}) fusion(bf16[64,4096]{1,0:T(8,128)(2,1)} %param.8), kind=kLoop, calls=%fused_computation.40 | loop fusion | bytes 1048576 | tf_op jit(solution)/shard_map/slice | solution.py:336
  10.6 5.9 %all-to-all-start = ((bf16[4,64,128]{2,1,0:T(8,128)(2,1)}), bf16[4,64,128]{2,1,0:T(8,128)(2,1)S(1)}, u32[]{:S(2)}, u32[]{:S(2)}) async-start(bf16[4,64,128]{2,1,0:T(8,128)(2,1)} %broadcast_in_dim.44), calls=%async_computation | async-start | bytes 131072 | tf_op jit(solution)/shard_map/all_to_all | solution.py:38
  18.0 4.3 %all-to-all-done = bf16[4,64,128]{2,1,0:T(8,128)(2,1)S(1)} async-done(((bf16[4,64,128]{2,1,0:T(8,128)(2,1)}), bf16[4,64,128]{2,1,0:T(8,128)(2,1)S(1)}, u32[]{:S(2)}, u32[]{:S(2)}) %all-to-all-start) | async-done | bytes 65568 | tf_op jit(solution)/shard_map/all_to_all | solution.py:38
  23.5 7.5 %all-to-all-start.1 = ((bf16[16,256,128]{2,1,0:T(8,128)(2,1)}), bf16[16,256,128]{2,1,0:T(8,128)(2,1)S(1)}, u32[]{:S(2)}, u32[]{:S(2)}) async-start(bf16[16,256,128]{2,1,0:T(8,128)(2,1)} %broadcast_in_dim.46), calls=%async_computation.1 | async-start | bytes 2097152 | tf_op jit(solution)/shard_map/all_to_all | solution.py:38
  32.7 4.6 %collective-permute-start.1 = (f32[4,256]{1,0:T(4,128)S(1)}, f32[4,256]{1,0:T(4,128)S(1)}, u32[]{:S(2)}, u32[]{:S(2)}) collective-permute-start(f32[4,256]{1,0:T(4,128)S(1)} %select_n.54.info), channel_id=1, source_target_pairs={{0,128},{128,0},{1,129},{129,1},{2,130},{130,2},{3,131},{131,3},{4... | collective-permute-start | bytes 12296 | tf_op jit(solution)/shard_map/ppermute | solution.py:42
  37.3 8.3 %all-to-all-done.1.pieces = bf16[16,256,128]{2,1,0:T(8,128)(2,1)S(1)} async-done(((bf16[16,256,128]{2,1,0:T(8,128)(2,1)}), bf16[16,256,128]{2,1,0:T(8,128)(2,1)S(1)}, u32[]{:S(2)}, u32[]{:S(2)}) %all-to-all-start.1) | async-done | bytes 1048608 | tf_op jit(solution)/shard_map/all_to_all | solution.py:38
  45.6 4.5 %logits_second_half.1 = (f32[594,256]{1,0:T(8,128)}, f32[594,256]{1,0:T(8,128)}) custom-call(bf16[16,256,128]{2,1,0:T(8,128)(2,1)S(1)} %all-to-all-done.1.pieces, bf16[594,4096]{1,0:T(8,128)(2,1)} %bitcast.9, bf16[594,4096]{1,0:T(8,128)(2,1)} %collective-permute-done.weight1), custom_call_target="tpu_custom_call" | custom-call | tf_op jit(solution)/shard_map/logits_second_half/pallas_call | solution.py:114
  50.1 4.1 %all-gather.3.cloned.1.call-done.straight.refs_4_.refs_5_ = bf16[512,2048]{1,0:T(8,128)(2,1)} async-done(((bf16[64,2048]{1,0:T(8,128)(2,1)}), bf16[512,2048]{1,0:T(8,128)(2,1)}) %all-gather.3.cloned.1.call-update) | async-done | bytes 2097168 | tf_op jit(solution)/shard_map/all_gather | solution.py:336
  54.5 6.6 %logits.1 = (f32[594,256]{1,0:T(8,128)}, f32[594,256]{1,0:T(8,128)}, f32[4,256]{1,0:T(4,128)S(1)}) custom-call(s32[4]{0:T(128)S(1)} %pad_add_fusion.s.first, s32[1,256]{1,0:T(1,128)S(1)} %convert_element_type.39.target, bf16[512,2048]{1,0:T(8,128)(2,1)} %all-gather.3.cloned.1.call-done.straight.refs_4_.refs_5_, f32[594,256]{1,0:T(8,128)} %get-tuple-element.35.before0, ...), custom_call_target="tpu_custom_call" | custom-call | tf_op jit(solution)/shard_map/logits/pallas_call | solution.py:162
  61.1 2.4 %collective-permute-start.4 = (f32[4,256]{1,0:T(4,128)S(1)}, f32[4,256]{1,0:T(4,128)S(1)}, u32[]{:S(2)}, u32[]{:S(2)}) collective-permute-start(f32[4,256]{1,0:T(4,128)S(1)} %get-tuple-element.37), channel_id=1, source_target_pairs={{0,96},{32,0},{64,32},{96,64},{1,97},{33,1},{65,33},{97,65},{2,98}... | collective-permute-start | bytes 12296 | tf_op jit(solution)/shard_map/ppermute | solution.py:29
  64.9 3.3 %collective-permute-done.3 = f32[4,256]{1,0:T(4,128)S(1)} collective-permute-done((f32[4,256]{1,0:T(4,128)S(1)}, f32[4,256]{1,0:T(4,128)S(1)}, u32[]{:S(2)}, u32[]{:S(2)}) %collective-permute-start.3) | collective-permute-done | bytes 4128 | tf_op jit(solution)/shard_map/ppermute | solution.py:29
  69.7 7.3 %all-to-all-start.2 = ((f32[16,4,256]{2,1,0:T(4,128)}), f32[16,4,256]{2,1,0:T(4,128)S(1)}, u32[]{:S(2)}, u32[]{:S(2)}) async-start(f32[16,4,256]{2,1,0:T(4,128)} %broadcast_in_dim.47), calls=%async_computation.2 | async-start | bytes 131072 | tf_op jit(solution)/shard_map/all_to_all | solution.py:38
  77.1 6.2 %all-to-all-done.2.parts = f32[16,4,256]{2,1,0:T(4,128)S(1)} async-done(((f32[16,4,256]{2,1,0:T(4,128)}), f32[16,4,256]{2,1,0:T(4,128)S(1)}, u32[]{:S(2)}, u32[]{:S(2)}) %all-to-all-start.2) | async-done | bytes 65568 | tf_op jit(solution)/shard_map/all_to_all | solution.py:38
  83.3 8.9 %grad_hidden_partial.1 = (bf16[256,4096]{1,0:T(8,128)(2,1)}, bf16[594,256]{1,0:T(8,128)(2,1)}, bf16[594,256]{1,0:T(8,128)(2,1)}, f32[3,256]{1,0:T(4,128)S(1)}) custom-call(s32[4]{0:T(128)S(1)} %pad_add_fusion.s.first, s32[1,256]{1,0:T(1,128)S(1)} %convert_element_type.39.target, f32[4,256]{1,0:T(4,128)S(1)} %select_n.54.info, ...), custom_call_target="tpu_custom_call" | custom-call | flops 2491416576 | bytes 4982833 | tf_op jit(solution)/shard_map/grad_hidden_partial/pallas_call | solution.py:229
  92.2 5.7 %all-to-all-start.3 = ((bf16[16,16,4096]{2,1,0:T(8,128)(2,1)}), bf16[16,16,4096]{2,1,0:T(8,128)(2,1)}, u32[]{:S(2)}, u32[]{:S(2)}) async-start(bf16[16,16,4096]{2,1,0:T(8,128)(2,1)} %bitcast.14), calls=%async_computation.3 | async-start | bytes 4194304 | tf_op jit(solution)/shard_map/all_to_all | solution.py:369
  97.9 2.8 %collective-permute-start.5 = (f32[3,256]{1,0:T(4,128)S(1)}, f32[3,256]{1,0:T(4,128)S(1)}, u32[]{:S(2)}, u32[]{:S(2)}) collective-permute-start(f32[3,256]{1,0:T(4,128)S(1)} %get-tuple-element.46), channel_id=1, source_target_pairs={{0,128},{128,0},{1,129},{129,1},{2,130},{130,2},{3,131},{131,3},{4... | collective-permute-start | bytes 9224 | tf_op jit(solution)/shard_map/ppermute | solution.py:42
  100.7 6.8 %other_group_logits.1 = (f32[594,256]{1,0:T(8,128)S(1)}, f32[594,256]{1,0:T(8,128)S(1)}) custom-call(s32[4]{0:T(128)S(1)} %pad_add_fusion.s.first, bf16[512,2048]{1,0:T(8,128)(2,1)} %all-gather.3.cloned.1.call-done.straight.refs_4_.refs_5_, bf16[512,2048]{1,0:T(8,128)(2,1)} %all-gather.5.cloned.1.call-done.straight2.refs_4_.refs_5_, ...), custom_call_target="tpu_custom_call" | custom-call | tf_op jit(solution)/shard_map/other_group_logits/pallas_call | solution.py:265
  107.5 1.8 %other_group_grad_logits.1 = (bf16[594,256]{1,0:T(8,128)(2,1)}, bf16[594,256]{1,0:T(8,128)(2,1)}) custom-call(s32[4]{0:T(128)S(1)} %pad_add_fusion.s.first, s32[1,256]{1,0:T(1,128)S(1)} %slice_convert_fusion.1.target, f32[4,256]{1,0:T(4,128)S(1)} %collective-permute-done.1.info, f32[3,256]{1,0:T(4,128)S(1)} %collective-permute-done.5.final, ...), custom_call_target="tpu_custom_call" | custom-call | tf_op jit(solution)/shard_map/other_group_grad_logits/pallas_call | solution.py:277
  109.8 1.7 %collective-permute-done.7.refs_3_ = bf16[594,256]{1,0:T(8,128)(2,1)S(1)} collective-permute-done((bf16[594,256]{1,0:T(8,128)(2,1)}, bf16[594,256]{1,0:T(8,128)(2,1)S(1)}, u32[]{:S(2)}, u32[]{:S(2)}) %collective-permute-start.7) | collective-permute-done | bytes 304160 | tf_op jit(solution)/shard_map/ppermute | solution.py:42
  112.4 6.7 %grad_head.2.refs_8_ = bf16[594,4096]{1,0:T(8,128)(2,1)} custom-call(s32[4]{0:T(128)S(1)} %pad_add_fusion.s.first, bf16[594,256]{1,0:T(8,128)(2,1)} %get-tuple-element.44.refs_0_, bf16[594,256]{1,0:T(8,128)(2,1)} %get-tuple-element.52.refs_1_, bf16[594,256]{1,0:T(8,128)(2,1)} %copy-done.3, bf16[594,256]{1,0:T(8,128)(2,1)} %copy-done.2, ...), custom_call_target="tpu_custom_call" | custom-call | tf_op jit(solution)/shard_map/grad_head/pallas_call | solution.py:302
  119.1 2.4 %all-to-all-done.3 = bf16[16,16,4096]{2,1,0:T(8,128)(2,1)} async-done(((bf16[16,16,4096]{2,1,0:T(8,128)(2,1)}), bf16[16,16,4096]{2,1,0:T(8,128)(2,1)}, u32[]{:S(2)}, u32[]{:S(2)}) %all-to-all-start.3) | async-done | bytes 2097184 | tf_op jit(solution)/shard_map/all_to_all | solution.py:369
  121.5 1.9 %reduce_sum.32 = bf16[16,4096]{1,0:T(8,128)(2,1)S(1)} reduce(bf16[16,16,4096]{2,1,0:T(8,128)(2,1)} %all-to-all-done.3, bf16[]{:T(256)} %constant.63.clone.1), dimensions={0}, to_apply=%region_2.3 | reduce | flops 983040 | bytes 2228226 | tf_op jit(solution)/shard_map/reduce_sum | solution.py:384
  124.7 1.9 %collective-permute-start.9 = (bf16[4,4096]{1,0:T(4,128)(2,1)S(1)}, bf16[4,4096]{1,0:T(4,128)(2,1)S(1)}, u32[]{:S(2)}, u32[]{:S(2)}) collective-permute-start(bf16[4,4096]{1,0:T(4,128)(2,1)S(1)} %get-tuple-element.72), channel_id=1, source_target_pairs={{0,32},{32,64},{64,96},{96,0},{1,33},{33,65},{65,97},{97,1},{2,34}... | collective-permute-start | bytes 98312 | tf_op jit(solution)/shard_map/ppermute | solution.py:390
  126.6 6.6 %grad_head.3 = bf16[594,4096]{1,0:T(8,128)(2,1)} custom-call(s32[4]{0:T(128)S(1)} %pad_add_fusion.s.first, bf16[594,256]{1,0:T(8,128)(2,1)} %get-tuple-element.44.refs_0_, bf16[594,256]{1,0:T(8,128)(2,1)} %get-tuple-element.52.refs_1_, bf16[594,256]{1,0:T(8,128)(2,1)} %copy-done.3, bf16[594,256]{1,0:T(8,128)(2,1)} %copy-done.2, ...), custom_call_target="tpu_custom_call", output_to_operand_aliasing={{}: (9, {})} | custom-call | tf_op jit(solution)/shard_map/grad_head/pallas_call | solution.py:302
  (71 shorter events, 12.4 us)
Async XLA Ops:
  7.2 47.1 %all-gather.3.cloned.1.call-start = ((), (), s32[]{:S(2)}) async-start(), calls=%async_computation.4 | async-start | bytes 2359296 | tf_op jit(solution)/shard_map/all_gather | solution.py:336
  7.2 38.4 %collective-permute-start = (bf16[594,4096]{1,0:T(8,128)(2,1)}, bf16[594,4096]{1,0:T(8,128)(2,1)}, u32[]{:S(2)}, u32[]{:S(2)}) collective-permute-start(bf16[594,4096]{1,0:T(8,128)(2,1)} %bitcast.8), channel_id=1, source_target_pairs={{0,16},{16,0},{1,17},{17,1},{2,18},{18,2},{3,19},{19,3},{4,20},{20... | collective-permute-start | bytes 14598152 | tf_op jit(solution)/shard_map/ppermute | solution.py:42
  9.2 21.8 %copy-start.4 = (s32[512]{0:T(512)S(1)}, s32[512]{0:T(512)}, u32[]{:S(2)}) copy-start(s32[512]{0:T(512)} %param.11) | copy-start | bytes 6148
  9.2 21.8 %copy-start.7 = (f32[64]{0:T(128)S(1)}, f32[64]{0:T(128)}, u32[]{:S(2)}) copy-start(f32[64]{0:T(128)} %param.14) | copy-start | bytes 772
  9.2 21.9 %copy-start.5 = (s32[512]{0:T(512)S(1)}, s32[512]{0:T(512)}, u32[]{:S(2)}) copy-start(s32[512]{0:T(512)} %param.13) | copy-start | bytes 6148
  9.2 22.1 %copy-start.6 = (f32[512]{0:T(512)S(1)}, f32[512]{0:T(512)}, u32[]{:S(2)}) copy-start(f32[512]{0:T(512)} %param.15) | copy-start | bytes 6148
  10.6 11.6 %all-to-all-start = ((bf16[4,64,128]{2,1,0:T(8,128)(2,1)}), bf16[4,64,128]{2,1,0:T(8,128)(2,1)S(1)}, u32[]{:S(2)}, u32[]{:S(2)}) async-start(bf16[4,64,128]{2,1,0:T(8,128)(2,1)} %broadcast_in_dim.44), calls=%async_computation | async-start | bytes 131072 | tf_op jit(solution)/shard_map/all_to_all | solution.py:38
  23.5 22.1 %all-to-all-start.1 = ((bf16[16,256,128]{2,1,0:T(8,128)(2,1)}), bf16[16,256,128]{2,1,0:T(8,128)(2,1)S(1)}, u32[]{:S(2)}, u32[]{:S(2)}) async-start(bf16[16,256,128]{2,1,0:T(8,128)(2,1)} %broadcast_in_dim.46), calls=%async_computation.1 | async-start | bytes 2097152 | tf_op jit(solution)/shard_map/all_to_all | solution.py:38
  30.9 69.8 %all-gather.5.cloned.1.call-start = ((), (), s32[]{:S(2)}) async-start(), calls=%async_computation.5 | async-start | bytes 2359296 | tf_op jit(solution)/shard_map/all_gather | solution.py:357
  32.7 17.4 %collective-permute-start.1 = (f32[4,256]{1,0:T(4,128)S(1)}, f32[4,256]{1,0:T(4,128)S(1)}, u32[]{:S(2)}, u32[]{:S(2)}) collective-permute-start(f32[4,256]{1,0:T(4,128)S(1)} %select_n.54.info), channel_id=1, source_target_pairs={{0,128},{128,0},{1,129},{129,1},{2,130},{130,2},{3,131},{131,3},{4... | collective-permute-start | bytes 12296 | tf_op jit(solution)/shard_map/ppermute | solution.py:42
  54.5 22.6 %copy-start = (bf16[512,2048]{1,0:T(8,128)(2,1)S(1)}, bf16[512,2048]{1,0:T(8,128)(2,1)}, u32[]{:S(2)}) copy-start(bf16[512,2048]{1,0:T(8,128)(2,1)} %all-gather.3.cloned.1.call-done.straight.refs_4_.refs_5_) | copy-start | bytes 6291460
  61.1 3.8 %collective-permute-start.4 = (f32[4,256]{1,0:T(4,128)S(1)}, f32[4,256]{1,0:T(4,128)S(1)}, u32[]{:S(2)}, u32[]{:S(2)}) collective-permute-start(f32[4,256]{1,0:T(4,128)S(1)} %get-tuple-element.37), channel_id=1, source_target_pairs={{0,96},{32,0},{64,32},{96,64},{1,97},{33,1},{65,33},{97,65},{2,98}... | collective-permute-start | bytes 12296 | tf_op jit(solution)/shard_map/ppermute | solution.py:29
  63.5 4.6 %collective-permute-start.3 = (f32[4,256]{1,0:T(4,128)S(1)}, f32[4,256]{1,0:T(4,128)S(1)}, u32[]{:S(2)}, u32[]{:S(2)}) collective-permute-start(f32[4,256]{1,0:T(4,128)S(1)} %get-tuple-element.37), channel_id=1, source_target_pairs={{0,64},{32,96},{64,0},{96,32},{1,65},{33,97},{65,1},{97,33},{2,66}... | collective-permute-start | bytes 12296 | tf_op jit(solution)/shard_map/ppermute | solution.py:29
  63.5 5.5 %collective-permute-start.2 = (f32[4,256]{1,0:T(4,128)S(1)}, f32[4,256]{1,0:T(4,128)S(1)}, u32[]{:S(2)}, u32[]{:S(2)}) collective-permute-start(f32[4,256]{1,0:T(4,128)S(1)} %get-tuple-element.37), channel_id=1, source_target_pairs={{0,32},{32,64},{64,96},{96,0},{1,33},{33,65},{65,97},{97,1},{2,34}... | collective-permute-start | bytes 12296 | tf_op jit(solution)/shard_map/ppermute | solution.py:29
  69.7 13.5 %all-to-all-start.2 = ((f32[16,4,256]{2,1,0:T(4,128)}), f32[16,4,256]{2,1,0:T(4,128)S(1)}, u32[]{:S(2)}, u32[]{:S(2)}) async-start(f32[16,4,256]{2,1,0:T(4,128)} %broadcast_in_dim.47), calls=%async_computation.2 | async-start | bytes 131072 | tf_op jit(solution)/shard_map/all_to_all | solution.py:38
  77.0 32.8 %collective-permute-start.8 = (bf16[512,2048]{1,0:T(8,128)(2,1)S(1)}, bf16[512,2048]{1,0:T(8,128)(2,1)}, u32[]{:S(2)}, u32[]{:S(2)}) collective-permute-start(bf16[512,2048]{1,0:T(8,128)(2,1)S(1)} %copy-done), channel_id=1, source_target_pairs={{0,16},{16,0},{1,17},{17,1},{2,18},{18,2},{3,19},{19,3},{4,20},{20... | collective-permute-start | bytes 6291464 | tf_op jit(solution)/shard_map/ppermute | solution.py:42
  92.2 29.3 %all-to-all-start.3 = ((bf16[16,16,4096]{2,1,0:T(8,128)(2,1)}), bf16[16,16,4096]{2,1,0:T(8,128)(2,1)}, u32[]{:S(2)}, u32[]{:S(2)}) async-start(bf16[16,16,4096]{2,1,0:T(8,128)(2,1)} %bitcast.14), calls=%async_computation.3 | async-start | bytes 4194304 | tf_op jit(solution)/shard_map/all_to_all | solution.py:369
  97.9 9.7 %collective-permute-start.5 = (f32[3,256]{1,0:T(4,128)S(1)}, f32[3,256]{1,0:T(4,128)S(1)}, u32[]{:S(2)}, u32[]{:S(2)}) collective-permute-start(f32[3,256]{1,0:T(4,128)S(1)} %get-tuple-element.46), channel_id=1, source_target_pairs={{0,128},{128,0},{1,129},{129,1},{2,130},{130,2},{3,131},{131,3},{4... | collective-permute-start | bytes 9224 | tf_op jit(solution)/shard_map/ppermute | solution.py:42
  109.3 2.2 %collective-permute-start.7 = (bf16[594,256]{1,0:T(8,128)(2,1)}, bf16[594,256]{1,0:T(8,128)(2,1)S(1)}, u32[]{:S(2)}, u32[]{:S(2)}) collective-permute-start(bf16[594,256]{1,0:T(8,128)(2,1)} %get-tuple-element.54), channel_id=1, source_target_pairs={{0,16},{16,0},{1,17},{17,1},{2,18},{18,2},{3,19},{19,3},{4,20},{20... | collective-permute-start | bytes 912392 | tf_op jit(solution)/shard_map/ppermute | solution.py:42
  109.3 2.2 %collective-permute-start.6 = (bf16[594,256]{1,0:T(8,128)(2,1)S(1)}, bf16[594,256]{1,0:T(8,128)(2,1)S(1)}, u32[]{:S(2)}, u32[]{:S(2)}) collective-permute-start(bf16[594,256]{1,0:T(8,128)(2,1)S(1)} %copy-done.8), channel_id=1, source_target_pairs={{0,16},{16,0},{1,17},{17,1},{2,18},{18,2},{3,19},{19,3},{4,20},{20... | collective-permute-start | bytes 912392 | tf_op jit(solution)/shard_map/ppermute | solution.py:42
  121.5 5.1 %collective-permute-start.12 = (bf16[512,2048]{1,0:T(8,128)(2,1)S(1)}, bf16[512,2048]{1,0:T(8,128)(2,1)}, u32[]{:S(2)}, u32[]{:S(2)}) collective-permute-start(bf16[512,2048]{1,0:T(8,128)(2,1)S(1)} %copy-done.1), channel_id=1, source_target_pairs={{0,16},{16,0},{1,17},{17,1},{2,18},{18,2},{3,19},{19,3},{4,20},{20... | collective-permute-start | bytes 6291464 | tf_op jit(solution)/shard_map/ppermute | solution.py:42
  123.5 9.8 %collective-permute-start.11 = (bf16[4,4096]{1,0:T(4,128)(2,1)S(1)}, bf16[4,4096]{1,0:T(4,128)(2,1)S(1)}, u32[]{:S(2)}, u32[]{:S(2)}) collective-permute-start(bf16[4,4096]{1,0:T(4,128)(2,1)S(1)} %get-tuple-element.70), channel_id=1, source_target_pairs={{0,96},{32,0},{64,32},{96,64},{1,97},{33,1},{65,33},{97,65},{2,98}... | collective-permute-start | bytes 98312 | tf_op jit(solution)/shard_map/ppermute | solution.py:390
  124.0 9.2 %collective-permute-start.10 = (bf16[4,4096]{1,0:T(4,128)(2,1)S(1)}, bf16[4,4096]{1,0:T(4,128)(2,1)S(1)}, u32[]{:S(2)}, u32[]{:S(2)}) collective-permute-start(bf16[4,4096]{1,0:T(4,128)(2,1)S(1)} %get-tuple-element.71), channel_id=1, source_target_pairs={{0,64},{32,96},{64,0},{96,32},{1,65},{33,97},{65,1},{97,33},{2,66}... | collective-permute-start | bytes 98312 | tf_op jit(solution)/shard_map/ppermute | solution.py:390
  124.7 8.6 %collective-permute-start.9 = (bf16[4,4096]{1,0:T(4,128)(2,1)S(1)}, bf16[4,4096]{1,0:T(4,128)(2,1)S(1)}, u32[]{:S(2)}, u32[]{:S(2)}) collective-permute-start(bf16[4,4096]{1,0:T(4,128)(2,1)S(1)} %get-tuple-element.72), channel_id=1, source_target_pairs={{0,32},{32,64},{64,96},{96,0},{1,33},{33,65},{65,97},{97,1},{2,34}... | collective-permute-start | bytes 98312 | tf_op jit(solution)/shard_map/ppermute | solution.py:390
  (4 other events, 19.3 us)
Sparse Core Ops, SparseCore 0:
  9.8 44.4 all-gather.2
  56.0 39.4 all-gather.4
